TPU v7x, 256 devices: a whole 4x4x8 slice. The times are simulated.
256 devices in a mesh: seq: 64 (over y_hi, z, x), chan: 4 (over y_lo, core).
Axes of the slice: x: 4, y: 4 (y_hi: 2, y_lo: 2; y = y_hi * 2 + y_lo), z: 8, core: 2. Of those that a mesh axis runs over, the one named last changes fastest.
Arguments:
- pre_gate: bfloat16 [16384, 4096], P('seq', 'chan'), may hold values from -6 to 6
- post_gate: bfloat16 [16384, 4096], P('seq', 'chan'), may hold values from -6 to 6
- values: bfloat16 [16384, 4096], P('seq', 'chan'), may hold values from -6 to 6
- decay_rates: float32 [4096, 16], P('chan'), may hold values from 1.2207031e-06 to 0.03
- residues: float32 [4096, 16], P('chan'), may hold values from -1.5 to 1.5
- skip_gain: float32 [4096], P('chan'), may hold values from -1 to 1
- out_weight: bfloat16 [4096, 4096], P('chan'), may hold values from -0.125 to 0.125
Outputs:
- mixed: bfloat16 [16384, 4096], P('seq', 'chan')
All inputs are finite; a program needn't handle non-finite values.
Results may differ from a plain program's by a relative error of at most 0.02.
Values may be sent and summed in bfloat16 or wider, within the bound.
No kernel may reach another device: no remote copies, remote signals or barrier semaphores. Data moves between devices by JAX's collectives and lax.ppermute only.
A program may use at most 128 MiB of HBM per device.

v0:
```python
import functools

import jax
import jax.numpy as jnp
from jax import lax
from jax.experimental import pallas as pl
from jax.experimental.pallas import tpu as pltpu
from jax.sharding import Mesh
from jax.sharding import PartitionSpec as P

Y_HI, Z, X, Y_LO, CORE = 2, 8, 4, 2, 2
MODES = 16
ROWS = 256
SUBS = 8
STEPS = ROWS // SUBS
LANES = 128


def rows8(row):
    return jnp.broadcast_to(row, (SUBS, row.shape[-1]))


def inner_of(pre_ref, val_ref):
    product = pre_ref[...].astype(jnp.float32) * val_ref[...].astype(jnp.float32)
    return product.astype(jnp.bfloat16).astype(jnp.float32)


def states_kernel(pre_ref, val_ref, rate_ref, sub_ref, total_ref, inner_buf):
    inner_buf[...] = inner_of(pre_ref, val_ref)
    decay = jnp.exp(-rate_ref[...])
    factors = [rows8(decay[m : m + 1]) for m in range(MODES)]
    states = None
    for step in range(STEPS):
        value = inner_buf[pl.ds(step, SUBS, stride=STEPS), :]
        if states is None:
            states = [value] * MODES
        else:
            states = [f * s + value for f, s in zip(factors, states)]
    left = (SUBS - 1 - lax.broadcasted_iota(jnp.int32, (SUBS, LANES), 0)) * STEPS
    left = left.astype(jnp.float32)
    for m in range(MODES):
        sub_ref[m] = states[m]
        weight = jnp.exp(-rows8(rate_ref[m : m + 1]) * left)
        total_ref[m : m + 1, :] = jnp.sum(states[m] * weight, axis=0, keepdims=True)


def local_kernel(pre_ref, val_ref, rate_ref, weight_ref, skip_ref, sub_ref, out_ref, inner_buf, taps_buf):
    inner_buf[...] = inner_of(pre_ref, val_ref)
    lag = lax.broadcasted_iota(jnp.int32, (STEPS, LANES), 0).astype(jnp.float32)
    taps = jnp.zeros((STEPS, LANES), jnp.float32)
    for m in range(MODES):
        taps = taps + weight_ref[m : m + 1] * jnp.exp(-rate_ref[m : m + 1] * lag)
    first = lax.broadcasted_iota(jnp.int32, (STEPS, LANES), 0) == 0
    taps_buf[...] = taps + jnp.where(first, skip_ref[...], 0.0)
    where = lax.broadcasted_iota(jnp.int32, (SUBS, LANES), 0)
    entering = []
    factors = []
    for m in range(MODES):
        rate = rows8(rate_ref[m : m + 1])
        state = sub_ref[m]
        span = 1
        while span < SUBS:
            moved = jnp.where(where >= span, pltpu.roll(state, span, 0), 0.0)
            state = state + jnp.exp(-rate * float(span * STEPS)) * moved
            span *= 2
        state = jnp.where(where >= 1, pltpu.roll(state, 1, 0), 0.0)
        factor = jnp.exp(-rate)
        factors.append(factor)
        entering.append(state * factor * rows8(weight_ref[m : m + 1]))
    for step in range(STEPS):
        total = functools.reduce(lambda a, b: a + b, entering)
        for back in range(step + 1):
            total = total + rows8(taps_buf[back : back + 1]) * inner_buf[pl.ds(step - back, SUBS, stride=STEPS), :]
        out_ref[pl.ds(step, SUBS, stride=STEPS), :] = total
        entering = [f * e for f, e in zip(factors, entering)]


def carry_kernel(local_ref, post_ref, rate_ref, weight_ref, carry_ref, out_ref):
    ahead = (lax.broadcasted_iota(jnp.int32, (SUBS, LANES), 0) + 1).astype(jnp.float32)
    terms = []
    factors = []
    for m in range(MODES):
        rate = rows8(rate_ref[m : m + 1])
        terms.append(jnp.exp(-rate * ahead) * rows8(weight_ref[m : m + 1] * carry_ref[m : m + 1]))
        factors.append(jnp.exp(-rate * float(SUBS)))
    for pair in range(ROWS // (2 * SUBS)):
        sums = []
        for _ in range(2):
            sums.append(functools.reduce(lambda a, b: a + b, terms))
            terms = [f * t for f, t in zip(factors, terms)]
        rows = pl.ds(pair * 2 * SUBS, 2 * SUBS)
        conv = local_ref[rows, :] + jnp.concatenate(sums, axis=0)
        out_ref[rows, :] = (post_ref[rows, :].astype(jnp.float32) * conv).astype(jnp.bfloat16)


def column(rows):
    return pl.BlockSpec((rows, LANES), lambda i: (0, i))


SUB_SPEC = pl.BlockSpec((MODES, SUBS, LANES), lambda i: (0, 0, i))


def carries(total, rates, y_hi, z, x):
    width = total.shape[1]
    decay = jnp.exp(-float(ROWS) * rates)
    decay_group = jnp.exp(-float(ROWS * X) * rates)
    slots = jnp.broadcast_to(total.astype(jnp.bfloat16)[None], (Y_HI * X, MODES, width))
    slots = lax.all_to_all(slots, ("y_hi", "x"), 0, 0, tiled=True).astype(jnp.float32)

    def through(y):
        state = slots[X * y]
        for i in range(1, X):
            state = state * decay + slots[X * y + i]
        return state

    ends = [through(y) for y in range(Y_HI)]
    here = jnp.where(y_hi == 0, ends[0], ends[1])
    near = jnp.zeros_like(total)
    for i in range(X - 1):
        slot = jnp.where(y_hi == 0, slots[i], slots[X + i])
        near = jnp.where(i < x, near * decay + slot, near)
    shift = jnp.exp(-rates * (x * ROWS).astype(jnp.float32))
    wrap = jnp.exp(-rates * ((Z - 1 - z) * (ROWS * X)).astype(jnp.float32))
    state = jnp.where(y_hi == 1, wrap * ends[0], 0.0)
    sends = []
    for i in range(Z):
        sends.append((state * shift).astype(jnp.bfloat16))
        state = state * decay_group + jnp.where(z == i, here, 0.0)
    far = lax.all_to_all(jnp.stack(sends), "z", 0, 0, tiled=True).astype(jnp.float32)
    return near + far.sum(axis=0)


def body(pre_gate, post_gate, values, decay_rates, residues, skip_gain, out_weight):
    rows, width = pre_gate.shape
    y_hi, z, x = lax.axis_index("y_hi"), lax.axis_index("z"), lax.axis_index("x")
    y_lo, core = lax.axis_index("y_lo"), lax.axis_index("core")
    tiles = width // LANES
    rates = decay_rates.T
    f32 = functools.partial(jax.ShapeDtypeStruct, dtype=jnp.float32)
    subs, total = pl.pallas_call(
        states_kernel,
        grid=(tiles,),
        in_specs=[column(rows), column(rows), column(MODES)],
        out_specs=[SUB_SPEC, column(MODES)],
        out_shape=[f32((MODES, SUBS, width)), f32((MODES, width))],
        scratch_shapes=[pltpu.VMEM((rows, LANES), jnp.float32)],
        name="states",
    )(pre_gate, values, rates)
    weights = (residues * jnp.sqrt(-jnp.expm1(-2.0 * decay_rates))).T
    local = pl.pallas_call(
        local_kernel,
        grid=(tiles,),
        in_specs=[column(rows), column(rows), column(MODES), column(MODES), column(1), SUB_SPEC],
        out_specs=column(rows),
        out_shape=f32((rows, width)),
        scratch_shapes=[pltpu.VMEM((rows, LANES), jnp.float32), pltpu.VMEM((STEPS, LANES), jnp.float32)],
        cost_estimate=pl.CostEstimate(flops=3 * 10**9, bytes_accessed=3 * 2**20, transcendentals=0),
        name="local",
    )(pre_gate, values, rates, weights, skip_gain[None, :], subs)
    carry = carries(total, rates, y_hi, z, x)
    gated = pl.pallas_call(
        carry_kernel,
        grid=(tiles,),
        in_specs=[column(rows), column(rows), column(MODES), column(MODES), column(MODES)],
        out_specs=column(rows),
        out_shape=jax.ShapeDtypeStruct((rows, width), jnp.bfloat16),
        name="carry",
    )(local, post_gate, rates, weights, carry)

    def block(yl, k):
        return lax.dynamic_slice(out_weight, (0, (yl * CORE + k) * width), (width, width))

    def product(yl, k):
        return jnp.dot(gated, block(yl, k), preferred_element_type=jnp.float32)

    def swap(array, axis):
        return lax.ppermute(array.astype(jnp.bfloat16), axis, [(0, 1), (1, 0)]).astype(jnp.float32)

    far_sum = swap(product(1 - y_lo, 1 - core), "core") + product(1 - y_lo, core)
    far_sum = swap(far_sum, "y_lo")
    near_sum = swap(product(y_lo, 1 - core), "core") + product(y_lo, core)
    return (near_sum + far_sum).astype(jnp.bfloat16)


def solution(mesh):
    axes = ("y_hi", "z", "x", "y_lo", "core")
    split = Mesh(mesh.devices.reshape(Y_HI, Z, X, Y_LO, CORE), axes)
    seq, chan = axes[:3], axes[3:]
    placed = (P(seq, chan), P(seq, chan), P(seq, chan), P(chan, None), P(chan, None), P(chan), P(chan, None))
    return jax.shard_map(body, mesh=split, in_specs=placed, out_specs=P(seq, chan), check_vma=False)
```

profile of v0, /device:TPU:1, one launch (start us, length us, event | category | flops | bytes accessed | tf_op | source)
XLA Modules:
  0.0 86.3 jit_solution(2605003442000313210)
XLA Ops:
  0.0 5.7 %states.1 = (f32[16,8,1024]{2,1,0:T(8,128)}, f32[16,1024]{1,0:T(8,128)}) custom-call(bf16[256,1024]{1,0:T(8,128)(2,1)} %pre_ref.3, bf16[256,1024]{1,0:T(8,128)(2,1)} %val_ref.3, f32[16,1024]{1,0:T(8,128)} %bitcast.136), custom_call_target="tpu_custom_call" | custom-call | tf_op jit(solution)/shard_map/states/pallas_call | solution.py:140
  5.7 0.0 copy-start
  5.7 0.9 %convert_element_type.60 = bf16[16,1024]{1,0:T(8,128)(2,1)S(1)} convert(f32[16,1024]{1,0:T(8,128)} %get-tuple-element.8) | non-fusion elementwise | flops 16384 | bytes 98304 | tf_op jit(solution)/shard_map/convert_element_type | solution.py:107
  6.6 0.7 broadcast_in_dim.23
  7.3 7.5 %all-to-all-start = ((bf16[8,16,1024]{2,1,0:T(8,128)(2,1)}), bf16[8,16,1024]{2,1,0:T(8,128)(2,1)S(1)}, u32[]{:S(2)}, u32[]{:S(2)}) async-start(bf16[8,16,1024]{2,1,0:T(8,128)(2,1)} %broadcast_in_dim.23), calls=%async_computation | async-start | bytes 524288 | tf_op jit(solution)/shard_map/all_to_all | solution.py:108
  14.8 7.8 %all-to-all-done = bf16[8,16,1024]{2,1,0:T(8,128)(2,1)S(1)} async-done(((bf16[8,16,1024]{2,1,0:T(8,128)(2,1)}), bf16[8,16,1024]{2,1,0:T(8,128)(2,1)S(1)}, u32[]{:S(2)}, u32[]{:S(2)}) %all-to-all-start) | async-done | bytes 262176 | tf_op jit(solution)/shard_map/all_to_all | solution.py:108
  22.6 1.5 %fusion.18 = (bf16[8,16,1024]{2,1,0:T(8,128)(2,1)}, f32[16,1024]{1,0:T(8,128)S(1)}) fusion(f32[]{:T(128)S(6)} %convert_element_type.63, f32[1024,16]{0,1:T(8,128)} %param.10, f32[]{:T(128)S(6)} %convert_element_type.62, pred[]{:T(512)S(6)} %eq.31, f32[8,16,1024]{2,1,0:T(8,128)S(1)} %convert_element_type.61), kind=kLoop, calls=%fused_computation.45 | loop fusion | flops 229375 | bytes 425993
  24.1 1.5 %fusion.20 = (bf16[8,16,1024]{2,1,0:T(8,128)(2,1)}, f32[16,1024]{1,0:T(8,128)S(1)}) fusion(bf16[8,16,1024]{2,1,0:T(8,128)(2,1)} %get-tuple-element.11, pred[]{:T(512)S(6)} %eq.32, f32[1024,16]{0,1:T(8,128)} %param.10, f32[]{:T(128)S(6)} %convert_element_type.63, f32[16,1024]{1,0:T(8,128)S(1)} %get-tuple-element.12, f32[]{:T(128)S(6)} %convert_element_type.62, ...), kind=kLoop, calls=%fused_computation.47 | loop fusion | flops 311296 | bytes 491531
  25.6 1.5 %fusion.22 = bf16[8,16,1024]{2,1,0:T(8,128)(2,1)} fusion(bf16[8,16,1024]{2,1,0:T(8,128)(2,1)} %get-tuple-element.9, f32[]{:T(128)S(6)} %convert_element_type.63, f32[1024,16]{0,1:T(8,128)} %param.10, f32[16,1024]{1,0:T(8,128)S(1)} %get-tuple-element.10, pred[]{:T(512)S(6)} %eq.33, pred[]{:T(512)S(6)} %eq.32, f32[16,1024]{1,0:T(8,128)S(1)} %get-tuple-element.12, ...), kind=kLoop, calls=%fused_computation.49 | loop fusion | flops 229376 | bytes 229387
  27.1 1.5 %fusion.24 = bf16[8,16,1024]{2,1,0:T(8,128)(2,1)} fusion(bf16[8,16,1024]{2,1,0:T(8,128)(2,1)} %fusion.22, f32[16,1024]{1,0:T(8,128)S(1)} %get-tuple-element.10, pred[]{:T(512)S(6)} %eq.34, f32[1024,16]{0,1:T(8,128)} %param.10, f32[]{:T(128)S(6)} %convert_element_type.63, pred[]{:T(512)S(6)} %eq.33, pred[]{:T(512)S(6)} %eq.32, ...), kind=kLoop, calls=%fused_computation.51 | loop fusion | flops 278528 | bytes 229388
  28.6 1.5 %fusion.26 = bf16[8,16,1024]{2,1,0:T(8,128)(2,1)} fusion(bf16[8,16,1024]{2,1,0:T(8,128)(2,1)} %fusion.24, f32[16,1024]{1,0:T(8,128)S(1)} %get-tuple-element.10, pred[]{:T(512)S(6)} %eq.35, pred[]{:T(512)S(6)} %eq.34, f32[1024,16]{0,1:T(8,128)} %param.10, f32[]{:T(128)S(6)} %convert_element_type.63, pred[]{:T(512)S(6)} %eq.33, pred[]{:T(512)S(6)} %eq.32, ...), kind=kLoop, calls=%fused_computation.53 | loop fusion | flops 327680 | bytes 229389
  30.1 1.5 %bitcast_dynamic-update-slice_fusion.2 = bf16[8,16,1024]{2,1,0:T(8,128)(2,1)} fusion(bf16[8,16,1024]{2,1,0:T(8,128)(2,1)} %fusion.26, f32[16,1024]{1,0:T(8,128)S(1)} %get-tuple-element.10, pred[]{:T(512)S(6)} %eq.36, pred[]{:T(512)S(6)} %eq.35, pred[]{:T(512)S(6)} %eq.34, f32[1024,16]{0,1:T(8,128)} %param.10, f32[]{:T(128)S(6)} %convert_element_type.63, ...), kind=kLoop, calls=%fused_computation.56 | loop fusion | flops 376832 | bytes 229390
  31.6 1.5 %bitcast_dynamic-update-slice_fusion.1 = bf16[8,16,1024]{2,1,0:T(8,128)(2,1)} fusion(bf16[8,16,1024]{2,1,0:T(8,128)(2,1)} %bitcast_dynamic-update-slice_fusion.2, f32[16,1024]{1,0:T(8,128)S(1)} %get-tuple-element.10, pred[]{:T(512)S(6)} %eq.37, pred[]{:T(512)S(6)} %eq.36, pred[]{:T(512)S(6)} %eq.35, pred[]{:T(512)S(6)} %eq.34, f32[1024,16]{0,1:T(8,128)} %param.10, ...), kind=kLoop, calls=%fused_computation.55 | loop fusion | flops 425984 | bytes 229391
  33.2 1.5 %bitcast_dynamic-update-slice_fusion = bf16[8,16,1024]{2,1,0:T(8,128)(2,1)} fusion(bf16[8,16,1024]{2,1,0:T(8,128)(2,1)} %bitcast_dynamic-update-slice_fusion.1, f32[16,1024]{1,0:T(8,128)S(1)} %get-tuple-element.10, pred[]{:T(512)S(6)} %eq.38, pred[]{:T(512)S(6)} %eq.37, pred[]{:T(512)S(6)} %eq.36, pred[]{:T(512)S(6)} %eq.35, pred[]{:T(512)S(6)} %eq.34, ...), kind=kLoop, calls=%fused_computation.54 | loop fusion | flops 475136 | bytes 229392 | tf_op jit(solution)/shard_map/stack | solution.py:129
  34.7 8.2 %all-to-all-start.1 = ((bf16[8,16,1024]{2,1,0:T(8,128)(2,1)}), bf16[8,16,1024]{2,1,0:T(8,128)(2,1)S(1)}, u32[]{:S(2)}, u32[]{:S(2)}) async-start(bf16[8,16,1024]{2,1,0:T(8,128)(2,1)} %bitcast_dynamic-update-slice_fusion), calls=%async_computation.1 | async-start | bytes 524288 | tf_op jit(solution)/shard_map/all_to_all | solution.py:129
  42.9 1.5 %multiply_bitcast_fusion.weight_ref = f32[16,1024]{1,0:T(8,128)} fusion(f32[1024,16]{0,1:T(8,128)} %param.11, f32[1024,16]{0,1:T(8,128)} %param.10), kind=kLoop, calls=%fused_computation.43 | loop fusion | flops 49152 | bytes 196608 | tf_op jit(solution)/shard_map/transpose | solution.py:149
  44.4 11.2 %local.1.local_ref = f32[256,1024]{1,0:T(8,128)} custom-call(bf16[256,1024]{1,0:T(8,128)(2,1)} %pre_ref.3, bf16[256,1024]{1,0:T(8,128)(2,1)} %val_ref.3, f32[16,1024]{1,0:T(8,128)} %bitcast.137, f32[16,1024]{1,0:T(8,128)} %multiply_bitcast_fusion.weight_ref, f32[1,1024]{1,0:T(1,128)} %bitcast.139, f32[16,8,1024]{2,1,0:T(8,128)} %get-tuple-element.7.sub_ref), custom_call_target="tpu_custom_call" | custom-call | flops 3000000000 | bytes 3145728 | tf_op jit(solution)/shard_map/local/pallas_call | solution.py:150
  55.6 0.0 all-to-all-done.1
  55.6 0.0 copy-done
  55.7 0.7 select_add_fusion.6.carry_ref
  56.3 6.0 %carry.1 = bf16[256,1024]{1,0:T(8,128)(2,1)} custom-call(f32[256,1024]{1,0:T(8,128)} %local.1.local_ref, bf16[256,1024]{1,0:T(8,128)(2,1)} %post_ref.1, f32[16,1024]{1,0:T(8,128)} %bitcast.138, f32[16,1024]{1,0:T(8,128)} %multiply_bitcast_fusion.weight_ref, f32[16,1024]{1,0:T(8,128)} %select_add_fusion.6.carry_ref), custom_call_target="tpu_custom_call" | custom-call | tf_op jit(solution)/shard_map/carry/pallas_call | solution.py:161
  62.3 0.0 copy-start.1
  62.3 2.5 %fusion.11 = bf16[256,1024]{1,0:T(8,128)(2,1)S(1)} fusion(bf16[256,1024]{1,0:T(8,128)(2,1)} %carry.1, bf16[1024,4096]{1,0:T(8,128)(2,1)} %param.13, s32[]{:T(128)S(6)} %select_n.129), kind=kOutput, calls=%fused_computation.9 | convolution fusion | flops 537133056 | bytes 3145732 | tf_op jit(solution)/shard_map/dot_general | solution.py:174
  64.8 2.3 %collective-permute-start.1 = (bf16[256,1024]{1,0:T(8,128)(2,1)S(1)}, bf16[256,1024]{1,0:T(8,128)(2,1)S(1)}, u32[]{:S(2)}, u32[]{:S(2)}) collective-permute-start(bf16[256,1024]{1,0:T(8,128)(2,1)S(1)} %fusion.11), channel_id=1, source_target_pairs={{0,1},{1,0},{2,3},{3,2},{4,5},{5,4},{6,7},{7,6},{8,9},{9,8},{10,11... | collective-permute-start | bytes 1572872 | tf_op jit(solution)/shard_map/ppermute | solution.py:177
  67.1 2.5 %fusion.8 = bf16[256,1024]{1,0:T(8,128)(2,1)S(1)} fusion(bf16[256,1024]{1,0:T(8,128)(2,1)} %carry.1, bf16[1024,4096]{1,0:T(8,128)(2,1)} %param.13, s32[]{:T(128)S(6)} %select_n.127), kind=kOutput, calls=%fused_computation.8 | convolution fusion | flops 537133056 | bytes 3145732 | tf_op jit(solution)/shard_map/dot_general | solution.py:174
  69.6 0.1 collective-permute-start
  69.7 0.0 collective-permute-done.1
  69.7 2.5 %add_convert_fusion.1 = bf16[256,1024]{1,0:T(8,128)(2,1)S(1)} fusion(bf16[256,1024]{1,0:T(8,128)(2,1)S(1)} %collective-permute-done.1, bf16[256,1024]{1,0:T(8,128)(2,1)} %carry.1, bf16[1024,4096]{1,0:T(8,128)(2,1)} %param.13, s32[]{:T(128)S(6)} %select_n.130), kind=kOutput, calls=%fused_computation.11 | convolution fusion | flops 537657344 | bytes 3670020 | tf_op jit(solution)/shard_map/dot_general | solution.py:174
  72.2 0.5 collective-permute-start.2
  72.7 0.0 copy-done.1
  72.7 2.3 %fusion.4 = f32[256,1024]{1,0:T(8,128)S(1)} fusion(bf16[256,1024]{1,0:T(8,128)(2,1)S(1)} %copy-done.1, bf16[1024,4096]{1,0:T(8,128)(2,1)} %param.13, s32[]{:T(128)S(6)} %select_n.128), kind=kOutput, calls=%fused_computation.4 | convolution fusion | flops 536870912 | bytes 3670020 | tf_op jit(solution)/shard_map/dot_general | solution.py:174
  75.0 0.0 collective-permute-done
  75.0 10.3 %collective-permute-done.2 = bf16[256,1024]{1,0:T(8,128)(2,1)S(1)} collective-permute-done((bf16[256,1024]{1,0:T(8,128)(2,1)S(1)}, bf16[256,1024]{1,0:T(8,128)(2,1)S(1)}, u32[]{:S(2)}, u32[]{:S(2)}) %collective-permute-start.2) | collective-permute-done | bytes 524320 | tf_op jit(solution)/shard_map/ppermute | solution.py:177
  85.3 1.0 %add_convert_fusion = bf16[256,1024]{1,0:T(8,128)(2,1)} fusion(bf16[256,1024]{1,0:T(8,128)(2,1)S(1)} %collective-permute-done.2, f32[256,1024]{1,0:T(8,128)S(1)} %fusion.4, bf16[256,1024]{1,0:T(8,128)(2,1)S(1)} %collective-permute-done), kind=kLoop, calls=%fused_computation.10 | loop fusion | flops 1310720 | bytes 2621440 | tf_op jit(solution)/shard_map/convert_element_type | solution.py:182
  (2 shorter events, 0.1 us)
Async XLA Ops:
  5.7 50.0 %copy-start = (f32[1024,16]{0,1:T(8,128)S(1)}, f32[1024,16]{0,1:T(8,128)}, u32[]{:S(2)}) copy-start(f32[1024,16]{0,1:T(8,128)} %param.10) | copy-start | bytes 196612
  7.3 15.3 %all-to-all-start = ((bf16[8,16,1024]{2,1,0:T(8,128)(2,1)}), bf16[8,16,1024]{2,1,0:T(8,128)(2,1)S(1)}, u32[]{:S(2)}, u32[]{:S(2)}) async-start(bf16[8,16,1024]{2,1,0:T(8,128)(2,1)} %broadcast_in_dim.23), calls=%async_computation | async-start | bytes 524288 | tf_op jit(solution)/shard_map/all_to_all | solution.py:108
  34.7 20.9 %all-to-all-start.1 = ((bf16[8,16,1024]{2,1,0:T(8,128)(2,1)}), bf16[8,16,1024]{2,1,0:T(8,128)(2,1)S(1)}, u32[]{:S(2)}, u32[]{:S(2)}) async-start(bf16[8,16,1024]{2,1,0:T(8,128)(2,1)} %bitcast_dynamic-update-slice_fusion), calls=%async_computation.1 | async-start | bytes 524288 | tf_op jit(solution)/shard_map/all_to_all | solution.py:129
  62.3 10.4 %copy-start.1 = (bf16[256,1024]{1,0:T(8,128)(2,1)S(1)}, bf16[256,1024]{1,0:T(8,128)(2,1)}, u32[]{:S(2)}) copy-start(bf16[256,1024]{1,0:T(8,128)(2,1)} %carry.1) | copy-start | bytes 1572868
  64.8 4.9 %collective-permute-start.1 = (bf16[256,1024]{1,0:T(8,128)(2,1)S(1)}, bf16[256,1024]{1,0:T(8,128)(2,1)S(1)}, u32[]{:S(2)}, u32[]{:S(2)}) collective-permute-start(bf16[256,1024]{1,0:T(8,128)(2,1)S(1)} %fusion.11), channel_id=1, source_target_pairs={{0,1},{1,0},{2,3},{3,2},{4,5},{5,4},{6,7},{7,6},{8,9},{9,8},{10,11... | collective-permute-start | bytes 1572872 | tf_op jit(solution)/shard_map/ppermute | solution.py:177
  69.6 5.4 %collective-permute-start = (bf16[256,1024]{1,0:T(8,128)(2,1)S(1)}, bf16[256,1024]{1,0:T(8,128)(2,1)S(1)}, u32[]{:S(2)}, u32[]{:S(2)}) collective-permute-start(bf16[256,1024]{1,0:T(8,128)(2,1)S(1)} %fusion.8), channel_id=1, source_target_pairs={{0,1},{1,0},{2,3},{3,2},{4,5},{5,4},{6,7},{7,6},{8,9},{9,8},{10,11... | collective-permute-start | bytes 1572872 | tf_op jit(solution)/shard_map/ppermute | solution.py:177
  72.2 13.1 %collective-permute-start.2 = (bf16[256,1024]{1,0:T(8,128)(2,1)S(1)}, bf16[256,1024]{1,0:T(8,128)(2,1)S(1)}, u32[]{:S(2)}, u32[]{:S(2)}) collective-permute-start(bf16[256,1024]{1,0:T(8,128)(2,1)S(1)} %add_convert_fusion.1), channel_id=1, source_target_pairs={{0,2},{2,0},{1,3},{3,1},{4,6},{6,4},{5,7},{7,5},{8,10},{10,8},{9,1... | collective-permute-start | bytes 1572872 | tf_op jit(solution)/shard_map/ppermute | solution.py:177
where the time goes:
time: 87.7 us; the launch traced here: 86.3 us
  Pallas kernels  22.8 us (26%)
  starting transfers between devices  18.6 us (21%)
  waiting for transfers between devices  18.1 us (21%)
  other arithmetic  16.3 us (19%)
  matrix products  9.76 us (11%)
    pallas_call x1, Pallas kernels, body(): pl.pallas_call(local_kernel, grid=(tiles,), in_specs=[column(rows), colum...  11.2 us
    unnamed x7, other arithmetic  10.5 us
    ppermute x3, waiting for transfers between devices, swap(): lax.ppermute(array.astype(jnp.bfloat16), axis, [(0, 1), (1, 0)])  10.3 us
    dot_general x4, matrix products, product(): return jnp.dot(gated, block(yl, k), preferred_element_type=jnp.float32)  9.76 us
    all_to_all x1, starting transfers between devices, carries(): lax.all_to_all(jnp.stack(sends), 'z', 0, 0, tiled=True).astype(jnp.float32)  8.19 us
    all_to_all x1, waiting for transfers between devices, carries(): lax.all_to_all(slots, ('y_hi', 'x'), 0, 0, tiled=True).astype(jnp.float32)  7.8 us
    all_to_all x1, starting transfers between devices, carries(): lax.all_to_all(slots, ('y_hi', 'x'), 0, 0, tiled=True).astype(jnp.float32)  7.48 us
    pallas_call x1, Pallas kernels, body(): pl.pallas_call(carry_kernel, grid=(tiles,), in_specs=[column(rows), colum...  5.95 us
  transfers between devices with their start and end apart: 5, of which 2 were waited for; matrix products, arithmetic and copies ran while one was open for 10% of the time, Pallas kernels for 13%

commit v1 on v0

v1 whole, which is shorter than its diff:
```python
import functools

import jax
import jax.numpy as jnp
from jax import lax
from jax.experimental import pallas as pl
from jax.experimental.pallas import tpu as pltpu
from jax.sharding import Mesh
from jax.sharding import PartitionSpec as P

Y_HI, Z, X, Y_LO, CORE = 2, 8, 4, 2, 2
MODES = 16
ROWS = 256
SUBS = 8
STEPS = ROWS // SUBS
LANES = 128
CHUNK = 256
ANY = pl.BlockSpec(memory_space=pl.ANY)
VMEM = pl.BlockSpec(memory_space=pltpu.VMEM)
SMEM = pl.BlockSpec(memory_space=pltpu.SMEM)
PARAMS = pltpu.CompilerParams(vmem_limit_bytes=16 * 2**20)


def in_hbm(array):
    return pltpu.with_memory_space_constraint(array, pltpu.HBM)


def in_vmem(array):
    return pltpu.with_memory_space_constraint(array, pltpu.VMEM)


def shape_of(shape, dtype=jnp.float32):
    return jax.ShapeDtypeStruct(shape, dtype)


def rows8(row):
    return jnp.broadcast_to(row, (SUBS, row.shape[-1]))


def add_all(terms):
    terms = list(terms)
    while len(terms) > 1:
        terms = [a + b for a, b in zip(terms[::2], terms[1::2])] + terms[len(terms) & ~1 :]
    return terms[0]


def inner_of(pre, val):
    product = pre.astype(jnp.float32) * val.astype(jnp.float32)
    return product.astype(jnp.bfloat16).astype(jnp.float32)


def tile_of(index):
    return pl.ds(pl.multiple_of(index * LANES, LANES), LANES)


def states_kernel(pre_hbm, val_hbm, rate_hbm, slots_ref, pre_buf, val_buf, rate_buf, sems):
    width = pre_hbm.shape[1]
    copies = []
    for start in range(0, width, CHUNK):
        part = pl.ds(start, CHUNK)
        n = len(copies)
        copies.append(
            [
                pltpu.make_async_copy(hbm.at[:, part], buf.at[:, part], sems.at[n, j])
                for j, (hbm, buf) in enumerate(((rate_hbm, rate_buf), (pre_hbm, pre_buf), (val_hbm, val_buf)))
            ]
        )
        for copy in copies[-1]:
            copy.start()
    left = (SUBS - 1 - lax.broadcasted_iota(jnp.int32, (SUBS, LANES), 0)).astype(jnp.float32)

    def tile(index):
        cols = tile_of(index)
        factors = [jnp.exp(-float(SUBS) * rows8(rate_buf[m : m + 1, cols])) for m in range(MODES)]
        states = None
        for start in range(0, ROWS, 2 * SUBS):
            rows = pl.ds(start, 2 * SUBS)
            value = inner_of(pre_buf[rows, cols], val_buf[rows, cols])
            for half in (value[:SUBS], value[SUBS:]):
                if states is None:
                    states = [half] * MODES
                else:
                    states = [f * s + half for f, s in zip(factors, states)]
        totals = []
        for m in range(MODES):
            weight = jnp.exp(-rows8(rate_buf[m : m + 1, cols]) * left)
            totals.append(jnp.sum(states[m] * weight, axis=0, keepdims=True))
        total = jnp.concatenate(totals, axis=0).astype(jnp.bfloat16)
        for slot in range(slots_ref.shape[0]):
            slots_ref[slot, :, cols] = total

    for n, group in enumerate(copies):
        for copy in group:
            copy.wait()
        pl.loop(n * (CHUNK // LANES), (n + 1) * (CHUNK // LANES))(tile)


def local_kernel(pre_ref, val_ref, rate_ref, weight_ref, skip_ref, out_ref, inner_buf, taps_buf, sums_buf):
    lag = lax.broadcasted_iota(jnp.int32, (STEPS, LANES), 0).astype(jnp.float32)
    first = lax.broadcasted_iota(jnp.int32, (STEPS, LANES), 0) == 0
    where = lax.broadcasted_iota(jnp.int32, (SUBS, LANES), 0)

    def at(step):
        return inner_buf[pl.ds(step, SUBS, stride=STEPS), :]

    def tile(index):
        cols = tile_of(index)
        inner_buf[...] = inner_of(pre_ref[:, cols], val_ref[:, cols])
        taps = jnp.where(first, skip_ref[:, cols], 0.0)
        for m in range(MODES):
            taps = taps + weight_ref[m : m + 1, cols] * jnp.exp(-rate_ref[m : m + 1, cols] * lag)
        for step in range(STEPS):
            taps_buf[pl.ds(step * SUBS, SUBS), :] = rows8(taps[step : step + 1])
        factors = [jnp.exp(-rows8(rate_ref[m : m + 1, cols])) for m in range(MODES)]
        states = [at(0)] * MODES
        for step in range(1, STEPS):
            value = at(step)
            states = [f * s + value for f, s in zip(factors, states)]
        entering = []
        for m in range(MODES):
            rate = rows8(rate_ref[m : m + 1, cols])
            state = states[m]
            span = 1
            while span < SUBS:
                moved = jnp.where(where >= span, pltpu.roll(state, span, 0), 0.0)
                state = state + jnp.exp(-rate * float(span * STEPS)) * moved
                span *= 2
            state = jnp.where(where >= 1, pltpu.roll(state, 1, 0), 0.0)
            entering.append(state * factors[m] * rows8(weight_ref[m : m + 1, cols]))
        for base in range(0, STEPS, SUBS):
            sums = []
            for _ in range(SUBS):
                sums.append(add_all(entering))
                entering = [f * e for f, e in zip(factors, entering)]
            for source in range(base + SUBS):
                value = at(source)
                for j in range(max(0, source - base), SUBS):
                    tap = taps_buf[pl.ds((base + j - source) * SUBS, SUBS), :]
                    sums[j] = sums[j] + tap * value
            for j in range(SUBS):
                sums_buf[pl.ds(base + j, SUBS, stride=STEPS), :] = sums[j]
        out_ref[:, cols] = sums_buf[...]

    pl.loop(0, out_ref.shape[1] // LANES)(tile)


def spread_kernel(place_ref, slots_ref, rate_ref, near_ref, sends_ref):
    y_hi, z, x = place_ref[0], place_ref[1], place_ref[2]
    shift_rows = (x * ROWS).astype(jnp.float32)
    wrap_rows = ((Z - 1 - z) * (ROWS * X)).astype(jnp.float32)

    def tile(index):
        cols = tile_of(index)
        rate = rate_ref[:, cols]
        decay = jnp.exp(-float(ROWS) * rate)
        slots = [slots_ref[i, :, cols].astype(jnp.float32) for i in range(Y_HI * X)]

        def through(state, rest):
            for slot in rest:
                state = state * decay + slot
            return state

        ends = [through(slots[X * y], slots[X * y + 1 : X * y + X]) for y in range(Y_HI)]
        near = jnp.zeros_like(rate)
        for i in range(X - 1):
            slot = jnp.where(y_hi == 0, slots[i], slots[X + i])
            near = jnp.where(i < x, near * decay + slot, near)
        near_ref[:, cols] = near
        shift = jnp.exp(-rate * shift_rows)
        here = jnp.where(y_hi == 0, ends[0], ends[1]) * shift
        state = jnp.where(y_hi == 1, jnp.exp(-rate * wrap_rows) * ends[0], 0.0) * shift
        decay = jnp.exp(-float(ROWS * X) * rate)
        for i in range(Z):
            sends_ref[i, :, cols] = state.astype(jnp.bfloat16)
            state = state * decay + jnp.where(z == i, here, 0.0)

    pl.loop(0, near_ref.shape[1] // LANES)(tile)


def mix_kernel(
    place_ref, far_ref, near_ref, rate_ref, weight_ref, left_ref, right_ref, post_ref, proj_ref, sent_ref, kept_ref, gated_buf
):
    width = near_ref.shape[1]
    ahead = (lax.broadcasted_iota(jnp.int32, (SUBS, LANES), 0) + 1).astype(jnp.float32)

    def tile(index, local_ref, offset):
        here = tile_of(index)
        cols = tile_of(index + offset)
        carry = near_ref[:, cols] + add_all(far_ref[i, :, cols].astype(jnp.float32) for i in range(Z))
        carry = carry * weight_ref[:, cols]
        terms = []
        factors = []
        for m in range(MODES):
            rate = rows8(rate_ref[m : m + 1, cols])
            terms.append(jnp.exp(-rate * ahead) * rows8(carry[m : m + 1]))
            factors.append(jnp.exp(-rate * float(SUBS)))
        for start in range(0, ROWS, 2 * SUBS):
            sums = []
            for _ in range(2):
                sums.append(add_all(terms))
                terms = [f * t for f, t in zip(factors, terms)]
            rows = pl.ds(start, 2 * SUBS)
            conv = local_ref[rows, here] + jnp.concatenate(sums, axis=0)
            gated_buf[rows, cols] = (post_ref[rows, cols].astype(jnp.float32) * conv).astype(jnp.bfloat16)

    half = left_ref.shape[1] // LANES
    pl.loop(0, half)(lambda i: tile(i, left_ref, 0))
    pl.loop(0, half)(lambda i: tile(i, right_ref, half))
    y_lo, core = place_ref[3], place_ref[4]
    for chip in range(Y_LO):
        for own, out_ref in enumerate((sent_ref, kept_ref)):
            to_chip = 1 - y_lo if chip == 0 else y_lo
            to_core = core if own else 1 - core
            first = (to_chip * CORE + to_core) * width

            def strip(n, first=first, chip=chip, out_ref=out_ref):
                cols = pl.ds(pl.multiple_of(first + n * CHUNK, CHUNK), CHUNK)
                sums = jnp.dot(gated_buf[...], proj_ref[:, cols], preferred_element_type=jnp.float32)
                out_ref[chip, :, pl.ds(pl.multiple_of(n * CHUNK, CHUNK), CHUNK)] = sums.astype(out_ref.dtype)

            pl.loop(0, width // CHUNK)(strip)


def body(pre_gate, post_gate, values, decay_rates, residues, skip_gain, out_weight):
    rows, width = pre_gate.shape
    half = width // 2
    places = [lax.axis_index(name) for name in ("y_hi", "z", "x", "y_lo", "core")]
    place = jnp.stack(places)
    rates = decay_rates.T
    parts = width // CHUNK
    slots = pl.pallas_call(
        states_kernel,
        in_specs=[ANY] * 3,
        out_specs=VMEM,
        out_shape=shape_of((Y_HI * X, MODES, width), jnp.bfloat16),
        scratch_shapes=[
            pltpu.VMEM((rows, width), jnp.bfloat16),
            pltpu.VMEM((rows, width), jnp.bfloat16),
            pltpu.VMEM((MODES, width), jnp.float32),
            pltpu.SemaphoreType.DMA((parts, 3)),
        ],
        name="states",
        compiler_params=PARAMS,
    )(in_hbm(pre_gate), in_hbm(values), in_hbm(rates))
    slots = lax.all_to_all(slots, ("y_hi", "x"), 0, 0, tiled=True)
    weights = (residues * jnp.sqrt(-jnp.expm1(-2.0 * decay_rates))).T

    def local(start, pre, val):
        cols = slice(start, start + half)
        column = pl.BlockSpec((rows, half), lambda i: (0, start // half))
        modes = pl.BlockSpec((MODES, half), lambda i: (0, start // half))
        one = pl.BlockSpec((1, half), lambda i: (0, start // half))
        return pl.pallas_call(
            local_kernel,
            grid=(1,),
            in_specs=[column, column, modes, modes, one],
            out_specs=pl.BlockSpec((rows, half), lambda i: (0, 0)),
            out_shape=shape_of((rows, half)),
            scratch_shapes=[pltpu.VMEM((rows, LANES), jnp.float32)] * 3,
            cost_estimate=pl.CostEstimate(flops=10**8, bytes_accessed=2**20, transcendentals=0),
            name="local",
            compiler_params=PARAMS,
        )(pre, val, rates, weights, skip_gain[None, :])

    left = local(0, pre_gate, values)
    near, sends = pl.pallas_call(
        spread_kernel,
        in_specs=[SMEM, VMEM, VMEM],
        out_specs=[VMEM, VMEM],
        out_shape=[shape_of((MODES, width)), shape_of((Z, MODES, width), jnp.bfloat16)],
        name="spread",
        compiler_params=PARAMS,
    )(place, slots, rates)
    later_pre, later_val, _ = lax.optimization_barrier((pre_gate, values, near))
    right = local(half, later_pre, later_val)
    far = lax.all_to_all(sends, "z", 0, 0, tiled=True)
    sent, kept = pl.pallas_call(
        mix_kernel,
        in_specs=[SMEM] + [VMEM] * 8,
        out_specs=[VMEM, VMEM],
        out_shape=[shape_of((2, rows, width), jnp.bfloat16), shape_of((2, rows, width))],
        scratch_shapes=[pltpu.VMEM((rows, width), jnp.bfloat16)],
        name="mix",
        compiler_params=PARAMS,
    )(place, far, near, rates, weights, in_vmem(left), in_vmem(right), in_vmem(post_gate), in_vmem(out_weight))

    def swap(array, axis):
        return lax.ppermute(array.astype(jnp.bfloat16), axis, [(0, 1), (1, 0)]).astype(jnp.float32)

    far_sum = swap(swap(sent[0], "core") + kept[0], "y_lo")
    near_sum = swap(sent[1], "core") + kept[1]
    return (near_sum + far_sum).astype(jnp.bfloat16)


def solution(mesh):
    axes = ("y_hi", "z", "x", "y_lo", "core")
    split = Mesh(mesh.devices.reshape(Y_HI, Z, X, Y_LO, CORE), axes)
    seq, chan = axes[:3], axes[3:]
    placed = (P(seq, chan), P(seq, chan), P(seq, chan), P(chan, None), P(chan, None), P(chan), P(chan, None))
    return jax.shard_map(body, mesh=split, in_specs=placed, out_specs=P(seq, chan), check_vma=False)
```

time: 87.7 us -> 69.4 us (0.79); the launches traced: 86.3 us -> 69 us
  other arithmetic: 16.3 us -> 1.27 us
  matrix products: 9.76 us -> 0 us
  waiting for transfers between devices: 18.1 us -> 25.5 us
  Pallas kernels: 22.8 us -> 17.9 us
  local copies, waits for them, and re-layouts: 0.73 us -> 4.4 us
  starting transfers between devices: 18.6 us -> 19.8 us
    unnamed x7 -> x0, other arithmetic: 10.5 us -> none
    dot_general x4 -> x0, matrix products: 9.76 us -> none  [product(): return jnp.dot(gated, block(yl, k), preferred_element_type=jnp.float32)]
    pallas_call x3 -> x5, Pallas kernels: 22.8 us -> 17.9 us  [the longest x1 7.1 us: body(): pl.pallas_call(mix_kernel, in_specs=[SMEM] + [VMEM] * 8, out_specs=[VMEM,...]
    unnamed x4 -> x16, local copies, waits for them, and re-layouts: 0.01 us -> 4.24 us
    ppermute x3, waiting for transfers between devices: 10.3 us -> 14.2 us  [swap(): lax.ppermute(array.astype(jnp.bfloat16), axis, [(0, 1), (1, 0)])]
    all_to_all x2, waiting for transfers between devices: 7.8 us -> 11.3 us  [the longest x1 7.71 us: body(): slots = lax.all_to_all(slots, ('y_hi', 'x'), 0, 0, tiled=True)]
    another operation x1 -> x0, other arithmetic: 1.53 us -> none  [carries(): jnp.stack(sends)]
    transpose x1, other arithmetic: 1.54 us -> 0.05 us  [body(): weights = (residues * jnp.sqrt(-jnp.expm1(-2.0 * decay_rates))).T]
  transfers between devices with their start and end apart: 5 -> 5, of which waited for: 2 -> 5; matrix products, arithmetic and copies ran while one was open for 10% -> 0% of each run, Pallas kernels for 13% -> 8%
where the time goes in v1:
time: 69.4 us; the launch traced here: 69 us
  waiting for transfers between devices  25.5 us (37%)
  starting transfers between devices  19.8 us (29%)
  Pallas kernels  17.9 us (26%)
  local copies, waits for them, and re-layouts  4.4 us (6%)
  other arithmetic  1.27 us (2%)
    ppermute x3, waiting for transfers between devices, swap(): lax.ppermute(array.astype(jnp.bfloat16), axis, [(0, 1), (1, 0)])  14.2 us
    all_to_all x1, starting transfers between devices, body(): far = lax.all_to_all(sends, 'z', 0, 0, tiled=True)  8.32 us
    all_to_all x1, waiting for transfers between devices, body(): slots = lax.all_to_all(slots, ('y_hi', 'x'), 0, 0, tiled=True)  7.71 us
    all_to_all x1, starting transfers between devices, body(): slots = lax.all_to_all(slots, ('y_hi', 'x'), 0, 0, tiled=True)  7.49 us
    pallas_call x1, Pallas kernels, body(): pl.pallas_call(mix_kernel, in_specs=[SMEM] + [VMEM] * 8, out_specs=[VMEM,...  7.1 us
    pallas_call x2, Pallas kernels, local(): pl.pallas_call(local_kernel, grid=(1,), in_specs=[column, column, modes,...  5.76 us
    unnamed x16, local copies, waits for them, and re-layouts  4.24 us
    ppermute x3, starting transfers between devices, swap(): lax.ppermute(array.astype(jnp.bfloat16), axis, [(0, 1), (1, 0)])  4.01 us
  transfers between devices with their start and end apart: 5, of which 5 were waited for; matrix products, arithmetic and copies ran while one was open for 0% of the time, Pallas kernels for 8%

profile of v1, /device:TPU:1, one launch (start us, length us, event | category | flops | bytes accessed | tf_op | source)
XLA Modules:
  0.0 69.0 jit_solution(9093824460929684865)
XLA Ops:
  0.0 0.0 copy-start.2
  0.0 0.0 copy-start.1
  0.0 0.0 copy-start.4
  0.0 0.0 copy-start.7
  0.0 0.0 copy-start.6
  0.0 3.5 %states.1 = bf16[8,16,1024]{2,1,0:T(8,128)(2,1)} custom-call(bf16[256,1024]{1,0:T(8,128)(2,1)} %pre_ref.2, bf16[256,1024]{1,0:T(8,128)(2,1)} %val_ref.2, f32[16,1024]{1,0:T(8,128)} %bitcast.23), custom_call_target="tpu_custom_call" | custom-call | tf_op jit(solution)/shard_map/states/pallas_call | solution.py:231
  3.5 7.5 %all-to-all-start = ((bf16[8,16,1024]{2,1,0:T(8,128)(2,1)}), bf16[8,16,1024]{2,1,0:T(8,128)(2,1)S(1)}, u32[]{:S(2)}, u32[]{:S(2)}) async-start(bf16[8,16,1024]{2,1,0:T(8,128)(2,1)} %states.1), calls=%async_computation | async-start | bytes 524288 | tf_op jit(solution)/shard_map/all_to_all | solution.py:245
  11.0 0.1 stack.23.place_ref
  11.1 7.7 %all-to-all-done.slots_ref = bf16[8,16,1024]{2,1,0:T(8,128)(2,1)S(1)} async-done(((bf16[8,16,1024]{2,1,0:T(8,128)(2,1)}), bf16[8,16,1024]{2,1,0:T(8,128)(2,1)S(1)}, u32[]{:S(2)}, u32[]{:S(2)}) %all-to-all-start) | async-done | bytes 262176 | tf_op jit(solution)/shard_map/all_to_all | solution.py:245
  18.8 0.0 copy-start.3
  18.8 0.8 %copy-done.3 = f32[1024,16]{0,1:T(8,128)S(1)} copy-done((f32[1024,16]{0,1:T(8,128)S(1)}, f32[1024,16]{0,1:T(8,128)}, u32[]{:S(2)}) %copy-start.3) | copy-done | bytes 65560
  19.6 1.5 %spread.1 = (f32[16,1024]{1,0:T(8,128)S(1)}, bf16[8,16,1024]{2,1,0:T(8,128)(2,1)}) custom-call(s32[5]{0:T(128)S(1)} %stack.23.place_ref, bf16[8,16,1024]{2,1,0:T(8,128)(2,1)S(1)} %all-to-all-done.slots_ref, f32[16,1024]{1,0:T(8,128)S(1)} %bitcast.24), custom_call_target="tpu_custom_call" | custom-call | tf_op jit(solution)/shard_map/spread/pallas_call | solution.py:266
  21.2 0.0 copy-start.5
  21.2 8.3 %all-to-all-start.1 = ((bf16[8,16,1024]{2,1,0:T(8,128)(2,1)}), bf16[8,16,1024]{2,1,0:T(8,128)(2,1)S(1)}, u32[]{:S(2)}, u32[]{:S(2)}) async-start(bf16[8,16,1024]{2,1,0:T(8,128)(2,1)} %get-tuple-element.11), calls=%async_computation.1 | async-start | bytes 524288 | tf_op jit(solution)/shard_map/all_to_all | solution.py:276
  29.5 0.0 copy-done.4
  29.5 0.0 copy-done.7
  29.6 0.0 copy-done.2
  29.6 0.0 copy-done.1
  29.6 0.0 copy-done.6
  29.6 2.9 %local.2.left_ref = f32[256,512]{1,0:T(8,128)S(1)} custom-call(bf16[256,1024]{1,0:T(8,128)(2,1)S(1)} %copy-done.1, bf16[256,1024]{1,0:T(8,128)(2,1)S(1)} %copy-done.2, f32[16,1024]{1,0:T(8,128)S(1)} %bitcast.25, f32[16,1024]{1,0:T(8,128)S(1)} %multiply_bitcast_fusion.weight_ref, f32[1,1024]{1,0:T(1,128)S(1)} %bitcast.28), custom_call_target="tpu_custom_call" | custom-call | flops 100000000 | bytes 1048576 | tf_op jit(solution)/shard_map/local/pallas_call | solution.py:253
  32.5 2.9 %local.3.right_ref = f32[256,512]{1,0:T(8,128)S(1)} custom-call(bf16[256,1024]{1,0:T(8,128)(2,1)S(1)} %copy-done.1, bf16[256,1024]{1,0:T(8,128)(2,1)S(1)} %copy-done.2, f32[16,1024]{1,0:T(8,128)S(1)} %bitcast.26, f32[16,1024]{1,0:T(8,128)S(1)} %multiply_bitcast_fusion.weight_ref, f32[1,1024]{1,0:T(1,128)S(1)} %bitcast.29), custom_call_target="tpu_custom_call" | custom-call | flops 100000000 | bytes 1048576 | tf_op jit(solution)/shard_map/local/pallas_call | solution.py:253
  35.4 3.6 %all-to-all-done.1.far_ref = bf16[8,16,1024]{2,1,0:T(8,128)(2,1)S(1)} async-done(((bf16[8,16,1024]{2,1,0:T(8,128)(2,1)}), bf16[8,16,1024]{2,1,0:T(8,128)(2,1)S(1)}, u32[]{:S(2)}, u32[]{:S(2)}) %all-to-all-start.1) | async-done | bytes 262176 | tf_op jit(solution)/shard_map/all_to_all | solution.py:276
  39.0 0.0 copy-done.5
  39.0 0.0 copy-start
  39.0 3.4 %copy-done = bf16[1024,4096]{1,0:T(8,128)(2,1)S(1)} copy-done((bf16[1024,4096]{1,0:T(8,128)(2,1)S(1)}, bf16[1024,4096]{1,0:T(8,128)(2,1)}, u32[]{:S(2)}) %copy-start) | copy-done | bytes 8388632
  42.4 7.1 %mix.1 = (bf16[2,256,1024]{2,1,0:T(8,128)(2,1)S(1)}, f32[2,256,1024]{2,1,0:T(8,128)S(1)}) custom-call(s32[5]{0:T(128)S(1)} %stack.23.place_ref, bf16[8,16,1024]{2,1,0:T(8,128)(2,1)S(1)} %all-to-all-done.1.far_ref, f32[16,1024]{1,0:T(8,128)S(1)} %get-tuple-element.12.near_ref, f32[16,1024]{1,0:T(8,128)S(1)} %bitcast.27, ...), custom_call_target="tpu_custom_call" | custom-call | tf_op jit(solution)/shard_map/mix/pallas_call | solution.py:277
  49.5 0.1 slice_bitcast_fusion.1
  49.6 3.4 %collective-permute-start.1 = (bf16[256,1024]{1,0:T(8,128)(2,1)S(1)}, bf16[256,1024]{1,0:T(8,128)(2,1)S(1)}, u32[]{:S(2)}, u32[]{:S(2)}) collective-permute-start(bf16[256,1024]{1,0:T(8,128)(2,1)S(1)} %get-tuple-element.18), channel_id=1, source_target_pairs={{0,1},{1,0},{2,3},{3,2},{4,5},{5,4},{6,7},{7,6},{8,9},{9,8},{10,11... | collective-permute-start | bytes 1572872 | tf_op jit(solution)/shard_map/ppermute | solution.py:288
  53.0 0.1 collective-permute-start
  53.1 1.4 %collective-permute-done.1 = bf16[256,1024]{1,0:T(8,128)(2,1)S(1)} collective-permute-done((bf16[256,1024]{1,0:T(8,128)(2,1)S(1)}, bf16[256,1024]{1,0:T(8,128)(2,1)S(1)}, u32[]{:S(2)}, u32[]{:S(2)}) %collective-permute-start.1) | collective-permute-done | bytes 524320 | tf_op jit(solution)/shard_map/ppermute | solution.py:288
  54.5 0.2 fusion
  54.7 0.5 collective-permute-start.2
  55.2 0.1 collective-permute-done
  55.3 12.6 %collective-permute-done.2 = bf16[256,1024]{1,0:T(8,128)(2,1)S(1)} collective-permute-done((bf16[256,1024]{1,0:T(8,128)(2,1)S(1)}, bf16[256,1024]{1,0:T(8,128)(2,1)S(1)}, u32[]{:S(2)}, u32[]{:S(2)}) %collective-permute-start.2) | collective-permute-done | bytes 524320 | tf_op jit(solution)/shard_map/ppermute | solution.py:288
  67.9 1.1 %fusion.2 = bf16[256,1024]{1,0:T(8,128)(2,1)} fusion(bf16[256,1024]{1,0:T(8,128)(2,1)S(1)} %collective-permute-done.2, f32[2,256,1024]{2,1,0:T(8,128)S(1)} %get-tuple-element.16, bf16[256,1024]{1,0:T(8,128)(2,1)S(1)} %collective-permute-done), kind=kLoop, calls=%fused_computation.4 | loop fusion | flops 1310720 | bytes 2621440 | tf_op jit(solution)/shard_map/convert_element_type | solution.py:292
  (1 shorter events, 0.0 us)
Async XLA Ops:
  0.0 29.6 %copy-start.2 = (bf16[256,1024]{1,0:T(8,128)(2,1)S(1)}, bf16[256,1024]{1,0:T(8,128)(2,1)}, u32[]{:S(2)}) copy-start(bf16[256,1024]{1,0:T(8,128)(2,1)} %val_ref.2) | copy-start | bytes 1572868
  0.0 29.6 %copy-start.1 = (bf16[256,1024]{1,0:T(8,128)(2,1)S(1)}, bf16[256,1024]{1,0:T(8,128)(2,1)}, u32[]{:S(2)}) copy-start(bf16[256,1024]{1,0:T(8,128)(2,1)} %pre_ref.2) | copy-start | bytes 1572868
  0.0 29.5 %copy-start.4 = (f32[1024,16]{0,1:T(8,128)S(1)}, f32[1024,16]{0,1:T(8,128)}, u32[]{:S(2)}) copy-start(f32[1024,16]{0,1:T(8,128)} %param.10) | copy-start | bytes 196612
  0.0 29.5 %copy-start.7 = (f32[1024,16]{0,1:T(8,128)S(1)}, f32[1024,16]{0,1:T(8,128)}, u32[]{:S(2)}) copy-start(f32[1024,16]{0,1:T(8,128)} %param.11) | copy-start | bytes 196612
  0.0 29.6 %copy-start.6 = (f32[1024]{0:T(1024)S(1)}, f32[1024]{0:T(1024)}, u32[]{:S(2)}) copy-start(f32[1024]{0:T(1024)} %param.12) | copy-start | bytes 12292
  3.5 15.3 %all-to-all-start = ((bf16[8,16,1024]{2,1,0:T(8,128)(2,1)}), bf16[8,16,1024]{2,1,0:T(8,128)(2,1)S(1)}, u32[]{:S(2)}, u32[]{:S(2)}) async-start(bf16[8,16,1024]{2,1,0:T(8,128)(2,1)} %states.1), calls=%async_computation | async-start | bytes 524288 | tf_op jit(solution)/shard_map/all_to_all | solution.py:245
  18.8 0.8 %copy-start.3 = (f32[1024,16]{0,1:T(8,128)S(1)}, f32[1024,16]{0,1:T(8,128)}, u32[]{:S(2)}) copy-start(f32[1024,16]{0,1:T(8,128)} %param.10) | copy-start | bytes 196612
  21.2 17.8 %copy-start.5 = (bf16[256,1024]{1,0:T(8,128)(2,1)S(1)}, bf16[256,1024]{1,0:T(8,128)(2,1)}, u32[]{:S(2)}) copy-start(bf16[256,1024]{1,0:T(8,128)(2,1)} %post_ref.1) | copy-start | bytes 1572868
  21.2 17.8 %all-to-all-start.1 = ((bf16[8,16,1024]{2,1,0:T(8,128)(2,1)}), bf16[8,16,1024]{2,1,0:T(8,128)(2,1)S(1)}, u32[]{:S(2)}, u32[]{:S(2)}) async-start(bf16[8,16,1024]{2,1,0:T(8,128)(2,1)} %get-tuple-element.11), calls=%async_computation.1 | async-start | bytes 524288 | tf_op jit(solution)/shard_map/all_to_all | solution.py:276
  39.0 3.4 %copy-start = (bf16[1024,4096]{1,0:T(8,128)(2,1)S(1)}, bf16[1024,4096]{1,0:T(8,128)(2,1)}, u32[]{:S(2)}) copy-start(bf16[1024,4096]{1,0:T(8,128)(2,1)} %proj_ref.1) | copy-start | bytes 25165828
  49.6 5.0 %collective-permute-start.1 = (bf16[256,1024]{1,0:T(8,128)(2,1)S(1)}, bf16[256,1024]{1,0:T(8,128)(2,1)S(1)}, u32[]{:S(2)}, u32[]{:S(2)}) collective-permute-start(bf16[256,1024]{1,0:T(8,128)(2,1)S(1)} %get-tuple-element.18), channel_id=1, source_target_pairs={{0,1},{1,0},{2,3},{3,2},{4,5},{5,4},{6,7},{7,6},{8,9},{9,8},{10,11... | collective-permute-start | bytes 1572872 | tf_op jit(solution)/shard_map/ppermute | solution.py:288
  53.0 2.3 %collective-permute-start = (bf16[256,1024]{1,0:T(8,128)(2,1)S(1)}, bf16[256,1024]{1,0:T(8,128)(2,1)S(1)}, u32[]{:S(2)}, u32[]{:S(2)}) collective-permute-start(bf16[256,1024]{1,0:T(8,128)(2,1)S(1)} %get-tuple-element.17), channel_id=1, source_target_pairs={{0,1},{1,0},{2,3},{3,2},{4,5},{5,4},{6,7},{7,6},{8,9},{9,8},{10,11... | collective-permute-start | bytes 1572872 | tf_op jit(solution)/shard_map/ppermute | solution.py:288
  54.7 13.2 %collective-permute-start.2 = (bf16[256,1024]{1,0:T(8,128)(2,1)S(1)}, bf16[256,1024]{1,0:T(8,128)(2,1)S(1)}, u32[]{:S(2)}, u32[]{:S(2)}) collective-permute-start(bf16[256,1024]{1,0:T(8,128)(2,1)S(1)} %fusion), channel_id=1, source_target_pairs={{0,2},{2,0},{1,3},{3,1},{4,6},{6,4},{5,7},{7,5},{8,10},{10,8},{9,1... | collective-permute-start | bytes 1572872 | tf_op jit(solution)/shard_map/ppermute | solution.py:288

commit v2 on v1

v2 whole, which is shorter than its diff:
```python
import functools

import jax
import jax.numpy as jnp
from jax import lax
from jax.experimental import pallas as pl
from jax.experimental.pallas import tpu as pltpu
from jax.sharding import Mesh
from jax.sharding import PartitionSpec as P

Y_HI, Z, X, Y_LO, CORE = 2, 8, 4, 2, 2
MODES = 16
ROWS = 256
SUBS = 8
STEPS = ROWS // SUBS
LANES = 128
PARTS = 4
CHUNK = 256
ANY = pl.BlockSpec(memory_space=pl.ANY)
VMEM = pl.BlockSpec(memory_space=pltpu.VMEM)
SMEM = pl.BlockSpec(memory_space=pltpu.SMEM)
COST = pl.CostEstimate(flops=2 * 10**9, bytes_accessed=4 * 2**20, transcendentals=0)
PARAMS = pltpu.CompilerParams(vmem_limit_bytes=16 * 2**20)


def in_hbm(array):
    return pltpu.with_memory_space_constraint(array, pltpu.HBM)


def in_vmem(array):
    return pltpu.with_memory_space_constraint(array, pltpu.VMEM)


def shape_of(shape, dtype=jnp.float32):
    return jax.ShapeDtypeStruct(shape, dtype)


def rows8(row):
    return jnp.broadcast_to(row, (SUBS, row.shape[-1]))


def add_all(terms):
    terms = list(terms)
    while len(terms) > 1:
        terms = [a + b for a, b in zip(terms[::2], terms[1::2])] + terms[len(terms) & ~1 :]
    return terms[0]


def tile_of(index):
    return pl.ds(pl.multiple_of(index * LANES, LANES), LANES)


def expm1(value):
    series = jnp.ones_like(value)
    for n in range(9, 1, -1):
        series = 1.0 + value * (1.0 / n) * series
    return jnp.where(jnp.abs(value) < 0.25, value * series, jnp.exp(value) - 1.0)


def states_kernel(
    pre_hbm, val_hbm, rate_hbm, residue_hbm, skip_hbm,
    slots_ref, inner_ref, rate_ref, weight_ref, skip_ref, pre_buf, val_buf, residue_buf, sems
):
    width = pre_hbm.shape[1]
    pairs = ((rate_hbm, rate_ref), (pre_hbm, pre_buf), (val_hbm, val_buf), (residue_hbm, residue_buf), (skip_hbm, skip_ref))
    copies = []
    for start in range(0, width, CHUNK):
        part = pl.ds(start, CHUNK)
        n = len(copies)
        copies.append(
            [pltpu.make_async_copy(hbm.at[:, part], buf.at[:, part], sems.at[n, j]) for j, (hbm, buf) in enumerate(pairs)]
        )
        for copy in copies[-1]:
            copy.start()
    left = (SUBS - 1 - lax.broadcasted_iota(jnp.int32, (SUBS, LANES), 0)).astype(jnp.float32)

    def tile(index):
        cols = tile_of(index)
        factors = [jnp.exp(-float(SUBS) * rows8(rate_ref[m : m + 1, cols])) for m in range(MODES)]
        states = None
        for start in range(0, ROWS, 2 * SUBS):
            rows = pl.ds(start, 2 * SUBS)
            product = pre_buf[rows, cols].astype(jnp.float32) * val_buf[rows, cols].astype(jnp.float32)
            product = product.astype(jnp.bfloat16)
            inner_ref[rows, cols] = product
            value = product.astype(jnp.float32)
            for half in (value[:SUBS], value[SUBS:]):
                if states is None:
                    states = [half] * MODES
                else:
                    states = [f * s + half for f, s in zip(factors, states)]
        totals = []
        for m in range(MODES):
            weight = jnp.exp(-rows8(rate_ref[m : m + 1, cols]) * left)
            totals.append(jnp.sum(states[m] * weight, axis=0, keepdims=True))
        total = jnp.concatenate(totals, axis=0).astype(jnp.bfloat16)
        for slot in range(slots_ref.shape[0]):
            slots_ref[slot, :, cols] = total
        weight_ref[:, cols] = residue_buf[:, cols] * jnp.sqrt(-expm1(-2.0 * rate_ref[:, cols]))

    for n, group in enumerate(copies):
        for copy in group:
            copy.wait()
        pl.loop(n * (CHUNK // LANES), (n + 1) * (CHUNK // LANES))(tile)


def local_kernel(inner_ref, rate_ref, weight_ref, skip_ref, out_ref, inner_buf, taps_buf, sums_buf, *, first_tile):
    lag = lax.broadcasted_iota(jnp.int32, (STEPS, LANES), 0).astype(jnp.float32)
    start = lax.broadcasted_iota(jnp.int32, (STEPS, LANES), 0) == 0
    where = lax.broadcasted_iota(jnp.int32, (SUBS, LANES), 0)

    def at(step):
        return inner_buf[pl.ds(step, SUBS, stride=STEPS), :]

    def tile(index):
        here = tile_of(index)
        cols = tile_of(index + first_tile)
        inner_buf[...] = inner_ref[:, cols].astype(jnp.float32)
        taps = jnp.where(start, skip_ref[:, cols], 0.0)
        for m in range(MODES):
            taps = taps + weight_ref[m : m + 1, cols] * jnp.exp(-rate_ref[m : m + 1, cols] * lag)
        for step in range(STEPS):
            taps_buf[pl.ds(step * SUBS, SUBS), :] = rows8(taps[step : step + 1])
        factors = [jnp.exp(-rows8(rate_ref[m : m + 1, cols])) for m in range(MODES)]
        states = [at(0)] * MODES
        for step in range(1, STEPS):
            value = at(step)
            states = [f * s + value for f, s in zip(factors, states)]
        entering = []
        for m in range(MODES):
            rate = rows8(rate_ref[m : m + 1, cols])
            state = states[m]
            span = 1
            while span < SUBS:
                moved = jnp.where(where >= span, pltpu.roll(state, span, 0), 0.0)
                state = state + jnp.exp(-rate * float(span * STEPS)) * moved
                span *= 2
            state = jnp.where(where >= 1, pltpu.roll(state, 1, 0), 0.0)
            entering.append(state * factors[m] * rows8(weight_ref[m : m + 1, cols]))
        for base in range(0, STEPS, SUBS):
            sums = []
            for _ in range(SUBS):
                sums.append(add_all(entering))
                entering = [f * e for f, e in zip(factors, entering)]
            for source in range(base + SUBS):
                value = at(source)
                for j in range(max(0, source - base), SUBS):
                    tap = taps_buf[pl.ds((base + j - source) * SUBS, SUBS), :]
                    sums[j] = sums[j] + tap * value
            for j in range(SUBS):
                sums_buf[pl.ds(base + j, SUBS, stride=STEPS), :] = sums[j]
        out_ref[:, here] = sums_buf[...]

    pl.loop(0, out_ref.shape[1] // LANES)(tile)


def second_local_kernel(inner_ref, rate_ref, weight_ref, skip_ref, hbm, out_ref, into_ref, *scratch, first_tile):
    *buffers, sem = scratch
    copy = pltpu.make_async_copy(hbm, into_ref, sem)
    copy.start()
    local_kernel(inner_ref, rate_ref, weight_ref, skip_ref, out_ref, *buffers, first_tile=first_tile)
    copy.wait()


def spread_kernel(place_ref, slots_ref, rate_ref, near_ref, sends_ref):
    y_hi, z, x = place_ref[0], place_ref[1], place_ref[2]
    shift_rows = (x * ROWS).astype(jnp.float32)
    wrap_rows = ((Z - 1 - z) * (ROWS * X)).astype(jnp.float32)

    def tile(index):
        cols = tile_of(index)
        rate = rate_ref[:, cols]
        decay = jnp.exp(-float(ROWS) * rate)
        slots = [slots_ref[i, :, cols].astype(jnp.float32) for i in range(Y_HI * X)]

        def through(state, rest):
            for slot in rest:
                state = state * decay + slot
            return state

        ends = [through(slots[X * y], slots[X * y + 1 : X * y + X]) for y in range(Y_HI)]
        near = jnp.zeros_like(rate)
        for i in range(X - 1):
            slot = jnp.where(y_hi == 0, slots[i], slots[X + i])
            near = jnp.where(i < x, near * decay + slot, near)
        near_ref[:, cols] = near
        shift = jnp.exp(-rate * shift_rows)
        here = jnp.where(y_hi == 0, ends[0], ends[1]) * shift
        state = jnp.where(y_hi == 1, jnp.exp(-rate * wrap_rows) * ends[0], 0.0) * shift
        decay = jnp.exp(-float(ROWS * X) * rate)
        for i in range(Z):
            sends_ref[i, :, cols] = state.astype(jnp.bfloat16)
            state = state * decay + jnp.where(z == i, here, 0.0)

    pl.loop(0, near_ref.shape[1] // LANES)(tile)


def fetch(place_ref, proj_hbm, proj_ref, sems, near):
    y_lo, core = place_ref[3], place_ref[4]
    chip = y_lo if near else 1 - y_lo
    width = proj_hbm.shape[0]
    copies = []
    for n, to_core in enumerate((1 - core, core)):
        cols = pl.ds(pl.multiple_of((chip * CORE + to_core) * width, width), width)
        copies.append([])
        for part in range(PARTS):
            rows = pl.ds(part * (width // PARTS), width // PARTS)
            into = proj_ref.at[rows, pl.ds(n * width, width)]
            copies[-1].append(pltpu.make_async_copy(proj_hbm.at[rows, cols], into, sems.at[n, part]))
            copies[-1][-1].start()
    return copies


def mix_kernel(
    place_ref, proj_hbm, far_ref, near_ref, rate_ref, weight_ref, left_ref, right_ref, post_ref, gated_ref, sent_ref, proj_ref, sems
):
    copies = fetch(place_ref, proj_hbm, proj_ref, sems, False)
    rows_count, width = gated_ref.shape
    ahead = (lax.broadcasted_iota(jnp.int32, (SUBS, LANES), 0) + 1).astype(jnp.float32)

    def tile(index, local_ref, offset):
        here = tile_of(index)
        cols = tile_of(index + offset)
        carry = near_ref[:, cols] + add_all(far_ref[i, :, cols].astype(jnp.float32) for i in range(Z))
        carry = carry * weight_ref[:, cols]
        terms = []
        factors = []
        for m in range(MODES):
            rate = rows8(rate_ref[m : m + 1, cols])
            terms.append(jnp.exp(-rate * ahead) * rows8(carry[m : m + 1]))
            factors.append(jnp.exp(-rate * float(SUBS)))
        for start in range(0, rows_count, 2 * SUBS):
            sums = []
            for _ in range(2):
                sums.append(add_all(terms))
                terms = [f * t for f, t in zip(factors, terms)]
            rows = pl.ds(start, 2 * SUBS)
            conv = local_ref[rows, here] + jnp.concatenate(sums, axis=0)
            gated_ref[rows, cols] = (post_ref[rows, cols].astype(jnp.float32) * conv).astype(jnp.bfloat16)

    half = left_ref.shape[1] // LANES
    pl.loop(0, half)(lambda i: tile(i, left_ref, 0))
    pl.loop(0, half)(lambda i: tile(i, right_ref, half))
    arrive(copies[0])
    sums = jnp.dot(gated_ref[...], proj_ref[:, :width], preferred_element_type=jnp.float32)
    sent_ref[...] = sums.astype(sent_ref.dtype)
    arrive(copies[1])


def arrive(copies):
    for copy in copies:
        copy.wait()


def own_kernel(gated_ref, proj_ref, kept_ref):
    width = gated_ref.shape[1]
    kept_ref[...] = jnp.dot(gated_ref[...], proj_ref[:, width:], preferred_element_type=jnp.float32)


def near_kernel(place_ref, proj_hbm, gated_ref, sent_ref, kept_ref, proj_ref, sems):
    copies = fetch(place_ref, proj_hbm, proj_ref, sems, True)
    width = gated_ref.shape[1]
    for n, out_ref in enumerate((sent_ref, kept_ref)):
        arrive(copies[n])
        sums = jnp.dot(gated_ref[...], proj_ref[:, n * width : (n + 1) * width], preferred_element_type=jnp.float32)
        out_ref[...] = sums.astype(out_ref.dtype)


def body(pre_gate, post_gate, values, decay_rates, residues, skip_gain, out_weight):
    rows, width = pre_gate.shape
    half = width // 2
    places = [lax.axis_index(name) for name in ("y_hi", "z", "x", "y_lo", "core")]
    place = jnp.stack(places)
    rates = decay_rates.T
    parts = width // CHUNK
    bf16 = jnp.bfloat16
    slots, inner, rates, weights, skips = pl.pallas_call(
        states_kernel,
        in_specs=[ANY] * 5,
        out_specs=[VMEM] * 5,
        out_shape=[
            shape_of((Y_HI * X, MODES, width), bf16),
            shape_of((rows, width), bf16),
            shape_of((MODES, width)),
            shape_of((MODES, width)),
            shape_of((1, width)),
        ],
        scratch_shapes=[
            pltpu.VMEM((rows, width), bf16),
            pltpu.VMEM((rows, width), bf16),
            pltpu.VMEM((MODES, width), jnp.float32),
            pltpu.SemaphoreType.DMA((parts, 5)),
        ],
        name="states",
        compiler_params=PARAMS,
    )(*(in_hbm(a) for a in (pre_gate, values, decay_rates.T, residues.T, skip_gain[None, :])))
    slots = lax.all_to_all(slots, ("y_hi", "x"), 0, 0, tiled=True)

    def local(start, inner, kernel, more=()):
        return pl.pallas_call(
            functools.partial(kernel, first_tile=start // LANES),
            in_specs=[VMEM] * 4 + [ANY] * len(more),
            out_specs=[VMEM] * (1 + len(more)),
            out_shape=[shape_of((rows, half))] + [shape_of(a.shape, a.dtype) for a in more],
            scratch_shapes=[pltpu.VMEM((rows, LANES), jnp.float32)] * 3 + [pltpu.SemaphoreType.DMA] * len(more),
            cost_estimate=pl.CostEstimate(flops=10**8, bytes_accessed=2**20, transcendentals=0),
            name="local",
            compiler_params=PARAMS,
        )(*(in_vmem(a) for a in (inner, rates, weights, skips)), *(in_hbm(a) for a in more))

    (left,) = local(0, inner, local_kernel)
    slots, left = lax.optimization_barrier((slots, left))
    near, sends = pl.pallas_call(
        spread_kernel,
        in_specs=[SMEM, VMEM, VMEM],
        out_specs=[VMEM, VMEM],
        out_shape=[shape_of((MODES, width)), shape_of((Z, MODES, width), bf16)],
        name="spread",
        compiler_params=PARAMS,
    )(place, in_vmem(slots), in_vmem(rates))
    later_inner, _ = lax.optimization_barrier((inner, near))
    right, post = local(half, later_inner, second_local_kernel, (post_gate,))
    far = lax.all_to_all(sends, "z", 0, 0, tiled=True)
    arrays = tuple(in_vmem(a) for a in (far, near, rates, weights, left, right, post))
    gated, sent, proj_far = pl.pallas_call(
        mix_kernel,
        in_specs=[SMEM, ANY] + [VMEM] * 7,
        out_specs=[VMEM] * 3,
        out_shape=[shape_of((rows, width), bf16), shape_of((rows, width), bf16), shape_of((width, CORE * width), bf16)],
        scratch_shapes=[pltpu.SemaphoreType.DMA((CORE, PARTS))],
        cost_estimate=COST,
        name="mix",
        compiler_params=PARAMS,
    )(place, in_hbm(out_weight), *arrays)
    kept = pl.pallas_call(
        own_kernel,
        in_specs=[VMEM] * 2,
        out_specs=VMEM,
        out_shape=shape_of((rows, width)),
        cost_estimate=COST,
        name="own",
        compiler_params=PARAMS,
    )(in_vmem(gated), in_vmem(proj_far))

    def swap(array, axis):
        return lax.ppermute(array.astype(jnp.bfloat16), axis, [(0, 1), (1, 0)]).astype(jnp.float32)

    to_far = (swap(sent, "core") + kept).astype(bf16)
    gated, to_far = lax.optimization_barrier((gated, to_far))
    far_sum = swap(to_far, "y_lo")
    sent, kept = pl.pallas_call(
        near_kernel,
        in_specs=[SMEM, ANY, VMEM],
        out_specs=[VMEM] * 2,
        out_shape=[shape_of((rows, width), bf16), shape_of((rows, width))],
        scratch_shapes=[pltpu.VMEM((width, CORE * width), bf16), pltpu.SemaphoreType.DMA((CORE, PARTS))],
        cost_estimate=COST,
        name="near",
        compiler_params=PARAMS,
    )(place, in_hbm(out_weight), in_vmem(gated))
    quarter = rows // 4
    received = [swap(sent[i : i + quarter], "core") for i in range(0, rows, quarter)]
    near_sum = jnp.concatenate(received, axis=0) + kept
    return (near_sum + far_sum).astype(bf16)


def solution(mesh):
    axes = ("y_hi", "z", "x", "y_lo", "core")
    split = Mesh(mesh.devices.reshape(Y_HI, Z, X, Y_LO, CORE), axes)
    seq, chan = axes[:3], axes[3:]
    placed = (P(seq, chan), P(seq, chan), P(seq, chan), P(chan, None), P(chan, None), P(chan), P(chan, None))
    return jax.shard_map(body, mesh=split, in_specs=placed, out_specs=P(seq, chan), check_vma=False)
```

time: 69.4 us -> 60.7 us (0.87)
  waiting for transfers between devices: 25.5 us -> 20.2 us
  local copies, waits for them, and re-layouts: 4.4 us -> 0.12 us
  starting transfers between devices: 19.8 us -> 20.9 us
    ppermute x3 -> x6, waiting for transfers between devices: 14.2 us -> 8.6 us  [swap(): lax.ppermute(array.astype(jnp.bfloat16), axis, [(0, 1), (1, 0)])]
    unnamed x16 -> x0, local copies, waits for them, and re-layouts: 4.24 us -> none
    all_to_all x1, waiting for transfers between devices: 3.62 us -> 6.66 us  [body(): far = lax.all_to_all(sends, 'z', 0, 0, tiled=True)]
    all_to_all x1, waiting for transfers between devices: 7.71 us -> 4.9 us  [body(): slots = lax.all_to_all(slots, ('y_hi', 'x'), 0, 0, tiled=True)]
    ppermute x3 -> x6, starting transfers between devices: 4.01 us -> 5.27 us  [swap(): lax.ppermute(array.astype(jnp.bfloat16), axis, [(0, 1), (1, 0)])]
    pallas_call x4 -> x6, Pallas kernels: 16.3 us -> 16.4 us  [the longest x2 5.62 us: local(): pl.pallas_call(functools.partial(kernel, first_tile=start // LANES), in_s...]
  transfers between devices with their start and end apart: 5 -> 8, of which waited for: 5 -> 8; matrix products, arithmetic and copies ran while one was open for 0% -> 0% of each run, Pallas kernels for 8% -> 16%
where the time goes in v2:
time: 60.7 us; the launch traced here: 60.4 us
  starting transfers between devices  20.9 us (34%)
  waiting for transfers between devices  20.2 us (33%)
  Pallas kernels  17.9 us (29%)
  other arithmetic  1.18 us (2%)
    ppermute x6, waiting for transfers between devices, swap(): lax.ppermute(array.astype(jnp.bfloat16), axis, [(0, 1), (1, 0)])  8.6 us
    all_to_all x1, starting transfers between devices, body(): far = lax.all_to_all(sends, 'z', 0, 0, tiled=True)  8.19 us
    all_to_all x1, starting transfers between devices, body(): slots = lax.all_to_all(slots, ('y_hi', 'x'), 0, 0, tiled=True)  7.49 us
    all_to_all x1, waiting for transfers between devices, body(): far = lax.all_to_all(sends, 'z', 0, 0, tiled=True)  6.66 us
    pallas_call x2, Pallas kernels, local(): pl.pallas_call(functools.partial(kernel, first_tile=start // LANES), in_s...  5.62 us
    ppermute x6, starting transfers between devices, swap(): lax.ppermute(array.astype(jnp.bfloat16), axis, [(0, 1), (1, 0)])  5.27 us
    all_to_all x1, waiting for transfers between devices, body(): slots = lax.all_to_all(slots, ('y_hi', 'x'), 0, 0, tiled=True)  4.9 us
    pallas_call x1, Pallas kernels, body(): pl.pallas_call(states_kernel, in_specs=[ANY] * 5, out_specs=[VMEM] * 5, o...  3.61 us
  transfers between devices with their start and end apart: 8, of which 8 were waited for; matrix products, arithmetic and copies ran while one was open for 0% of the time, Pallas kernels for 16%

profile of v2, /device:TPU:1, one launch (start us, length us, event | category | flops | bytes accessed | tf_op | source)
XLA Modules:
  0.0 60.4 jit_solution(2484274995424995924)
XLA Ops:
  0.0 3.6 %states.1 = (bf16[8,16,1024]{2,1,0:T(8,128)(2,1)}, bf16[256,1024]{1,0:T(8,128)(2,1)S(1)}, f32[16,1024]{1,0:T(8,128)S(1)}, f32[16,1024]{1,0:T(8,128)S(1)}, f32[1,1024]{1,0:T(1,128)S(1)}) custom-call(bf16[256,1024]{1,0:T(8,128)(2,1)} %pre_hbm.1, bf16[256,1024]{1,0:T(8,128)(2,1)} %val_hbm.1, f32[16,1024]{1,0:T(8,128)} %bitcast.8, f32[16,1024]{1,0:T(8,128)} %bitcast.9, ...), custom_call_target="tpu_custom_call" | custom-call | tf_op jit(solution)/shard_map/states/pallas_call | solution.py:277
  3.6 7.5 %all-to-all-start = ((bf16[8,16,1024]{2,1,0:T(8,128)(2,1)}), bf16[8,16,1024]{2,1,0:T(8,128)(2,1)S(1)}, u32[]{:S(2)}, u32[]{:S(2)}) async-start(bf16[8,16,1024]{2,1,0:T(8,128)(2,1)} %get-tuple-element.24), calls=%async_computation | async-start | bytes 524288 | tf_op jit(solution)/shard_map/all_to_all | solution.py:297
  11.1 0.1 stack.23.place_ref
  11.2 2.8 %local.2.left_ref = f32[256,512]{1,0:T(8,128)S(1)} custom-call(bf16[256,1024]{1,0:T(8,128)(2,1)S(1)} %get-tuple-element.33.inner_ref, f32[16,1024]{1,0:T(8,128)S(1)} %get-tuple-element.26.rate_ref, f32[16,1024]{1,0:T(8,128)S(1)} %get-tuple-element.27.weight_ref, f32[1,1024]{1,0:T(1,128)S(1)} %get-tuple-element.28.skip_ref), custom_call_target="tpu_custom_call" | custom-call | flops 100000000 | bytes 1048576 | tf_op jit(solution)/shard_map/local/pallas_call | solution.py:300
  14.0 4.9 %all-to-all-done.slots_ref = bf16[8,16,1024]{2,1,0:T(8,128)(2,1)S(1)} async-done(((bf16[8,16,1024]{2,1,0:T(8,128)(2,1)}), bf16[8,16,1024]{2,1,0:T(8,128)(2,1)S(1)}, u32[]{:S(2)}, u32[]{:S(2)}) %all-to-all-start) | async-done | bytes 262176 | tf_op jit(solution)/shard_map/all_to_all | solution.py:297
  18.9 1.5 %spread.1 = (f32[16,1024]{1,0:T(8,128)S(1)}, bf16[8,16,1024]{2,1,0:T(8,128)(2,1)}) custom-call(s32[5]{0:T(128)S(1)} %stack.23.place_ref, bf16[8,16,1024]{2,1,0:T(8,128)(2,1)S(1)} %all-to-all-done.slots_ref, f32[16,1024]{1,0:T(8,128)S(1)} %get-tuple-element.26.rate_ref), custom_call_target="tpu_custom_call" | custom-call | tf_op jit(solution)/shard_map/spread/pallas_call | solution.py:313
  20.5 8.2 %all-to-all-start.1 = ((bf16[8,16,1024]{2,1,0:T(8,128)(2,1)}), bf16[8,16,1024]{2,1,0:T(8,128)(2,1)S(1)}, u32[]{:S(2)}, u32[]{:S(2)}) async-start(bf16[8,16,1024]{2,1,0:T(8,128)(2,1)} %get-tuple-element.30), calls=%async_computation.1 | async-start | bytes 524288 | tf_op jit(solution)/shard_map/all_to_all | solution.py:323
  28.6 2.8 %local.3 = (f32[256,512]{1,0:T(8,128)S(1)}, bf16[256,1024]{1,0:T(8,128)(2,1)S(1)}) custom-call(bf16[256,1024]{1,0:T(8,128)(2,1)S(1)} %get-tuple-element.33.inner_ref, f32[16,1024]{1,0:T(8,128)S(1)} %get-tuple-element.26.rate_ref, f32[16,1024]{1,0:T(8,128)S(1)} %get-tuple-element.27.weight_ref, f32[1,1024]{1,0:T(1,128)S(1)} %get-tuple-element.28.skip_ref, ...), custom_call_target="tpu_custom_call" | custom-call | flops 100000000 | bytes 1048576 | tf_op jit(solution)/shard_map/local/pallas_call | solution.py:300
  31.5 6.7 %all-to-all-done.1.far_ref = bf16[8,16,1024]{2,1,0:T(8,128)(2,1)S(1)} async-done(((bf16[8,16,1024]{2,1,0:T(8,128)(2,1)}), bf16[8,16,1024]{2,1,0:T(8,128)(2,1)S(1)}, u32[]{:S(2)}, u32[]{:S(2)}) %all-to-all-start.1) | async-done | bytes 262176 | tf_op jit(solution)/shard_map/all_to_all | solution.py:323
  38.1 2.9 %mix.1 = (bf16[256,1024]{1,0:T(8,128)(2,1)S(1)}, bf16[256,1024]{1,0:T(8,128)(2,1)S(1)}, bf16[1024,2048]{1,0:T(8,128)(2,1)S(1)}) custom-call(s32[5]{0:T(128)S(1)} %stack.23.place_ref, bf16[1024,4096]{1,0:T(8,128)(2,1)} %proj_hbm.3, bf16[8,16,1024]{2,1,0:T(8,128)(2,1)S(1)} %all-to-all-done.1.far_ref, f32[16,1024]{1,0:T(8,128)S(1)} %get-tuple-element.31.near_ref, ...), custom_call_target="tpu_custom_call" | custom-call | flops 2000000000 | bytes 4194304 | tf_op jit(solution)/shard_map/mix/pallas_call | solution.py:325
  41.0 3.4 %collective-permute-start = (bf16[256,1024]{1,0:T(8,128)(2,1)S(1)}, bf16[256,1024]{1,0:T(8,128)(2,1)S(1)}, u32[]{:S(2)}, u32[]{:S(2)}) collective-permute-start(bf16[256,1024]{1,0:T(8,128)(2,1)S(1)} %get-tuple-element.37), channel_id=1, source_target_pairs={{0,1},{1,0},{2,3},{3,2},{4,5},{5,4},{6,7},{7,6},{8,9},{9,8},{10,11... | collective-permute-start | bytes 1572872 | tf_op jit(solution)/shard_map/ppermute | solution.py:346
  44.4 0.7 %own.1 = f32[256,1024]{1,0:T(8,128)S(1)} custom-call(bf16[256,1024]{1,0:T(8,128)(2,1)S(1)} %get-tuple-element.39.gated_ref, bf16[1024,2048]{1,0:T(8,128)(2,1)S(1)} %get-tuple-element.38.proj_ref), custom_call_target="tpu_custom_call" | custom-call | flops 2000000000 | bytes 4194304 | tf_op jit(solution)/shard_map/own/pallas_call | solution.py:335
  45.1 0.8 %collective-permute-done = bf16[256,1024]{1,0:T(8,128)(2,1)S(1)} collective-permute-done((bf16[256,1024]{1,0:T(8,128)(2,1)S(1)}, bf16[256,1024]{1,0:T(8,128)(2,1)S(1)}, u32[]{:S(2)}, u32[]{:S(2)}) %collective-permute-start) | collective-permute-done | bytes 524320 | tf_op jit(solution)/shard_map/ppermute | solution.py:346
  46.0 0.1 add_convert_fusion.1
  46.1 0.5 collective-permute-start.5
  46.6 3.6 %near.1 = (bf16[256,1024]{1,0:T(8,128)(2,1)S(1)}, f32[256,1024]{1,0:T(8,128)S(1)}) custom-call(s32[5]{0:T(128)S(1)} %stack.23.place_ref, bf16[1024,4096]{1,0:T(8,128)(2,1)} %proj_hbm.3, bf16[256,1024]{1,0:T(8,128)(2,1)S(1)} %get-tuple-element.39.gated_ref), custom_call_target="tpu_custom_call" | custom-call | flops 2000000000 | bytes 4194304 | tf_op jit(solution)/shard_map/near/pallas_call | solution.py:351
  50.2 0.7 %collective-permute-start.1 = (bf16[64,1024]{1,0:T(8,128)(2,1)S(1)}, bf16[64,1024]{1,0:T(8,128)(2,1)S(1)}, u32[]{:S(2)}, u32[]{:S(2)}) collective-permute-start(bf16[64,1024]{1,0:T(8,128)(2,1)S(1)} %get-tuple-element.43), channel_id=1, source_target_pairs={{0,1},{1,0},{2,3},{3,2},{4,5},{5,4},{6,7},{7,6},{8,9},{9,8},{10,11... | collective-permute-start | bytes 393224 | tf_op jit(solution)/shard_map/ppermute | solution.py:346
  51.0 0.1 collective-permute-start.4
  51.1 0.4 collective-permute-start.3
  51.5 0.1 collective-permute-start.2
  51.6 0.4 collective-permute-done.1
  51.9 0.4 collective-permute-done.4
  52.3 0.2 collective-permute-done.3
  52.5 0.3 collective-permute-done.2
  52.8 6.5 %collective-permute-done.5 = bf16[256,1024]{1,0:T(8,128)(2,1)S(1)} collective-permute-done((bf16[256,1024]{1,0:T(8,128)(2,1)S(1)}, bf16[256,1024]{1,0:T(8,128)(2,1)S(1)}, u32[]{:S(2)}, u32[]{:S(2)}) %collective-permute-start.5) | collective-permute-done | bytes 524320 | tf_op jit(solution)/shard_map/ppermute | solution.py:346
  59.3 1.0 %add_convert_fusion = bf16[256,1024]{1,0:T(8,128)(2,1)} fusion(bf16[256,1024]{1,0:T(8,128)(2,1)S(1)} %collective-permute-done.5, f32[256,1024]{1,0:T(8,128)S(1)} %get-tuple-element.41, bf16[64,1024]{1,0:T(8,128)(2,1)S(1)} %collective-permute-done.4, bf16[64,1024]{1,0:T(8,128)(2,1)S(1)} %collective-permute-done.3, ...), kind=kLoop, calls=%fused_computation | loop fusion | flops 3145728 | bytes 2621440 | tf_op jit(solution)/shard_map/convert_element_type | solution.py:364
  (1 shorter events, 0.0 us)
Async XLA Ops:
  3.6 15.3 %all-to-all-start = ((bf16[8,16,1024]{2,1,0:T(8,128)(2,1)}), bf16[8,16,1024]{2,1,0:T(8,128)(2,1)S(1)}, u32[]{:S(2)}, u32[]{:S(2)}) async-start(bf16[8,16,1024]{2,1,0:T(8,128)(2,1)} %get-tuple-element.24), calls=%async_computation | async-start | bytes 524288 | tf_op jit(solution)/shard_map/all_to_all | solution.py:297
  20.5 17.7 %all-to-all-start.1 = ((bf16[8,16,1024]{2,1,0:T(8,128)(2,1)}), bf16[8,16,1024]{2,1,0:T(8,128)(2,1)S(1)}, u32[]{:S(2)}, u32[]{:S(2)}) async-start(bf16[8,16,1024]{2,1,0:T(8,128)(2,1)} %get-tuple-element.30), calls=%async_computation.1 | async-start | bytes 524288 | tf_op jit(solution)/shard_map/all_to_all | solution.py:323
  41.0 5.0 %collective-permute-start = (bf16[256,1024]{1,0:T(8,128)(2,1)S(1)}, bf16[256,1024]{1,0:T(8,128)(2,1)S(1)}, u32[]{:S(2)}, u32[]{:S(2)}) collective-permute-start(bf16[256,1024]{1,0:T(8,128)(2,1)S(1)} %get-tuple-element.37), channel_id=1, source_target_pairs={{0,1},{1,0},{2,3},{3,2},{4,5},{5,4},{6,7},{7,6},{8,9},{9,8},{10,11... | collective-permute-start | bytes 1572872 | tf_op jit(solution)/shard_map/ppermute | solution.py:346
  46.1 13.2 %collective-permute-start.5 = (bf16[256,1024]{1,0:T(8,128)(2,1)S(1)}, bf16[256,1024]{1,0:T(8,128)(2,1)S(1)}, u32[]{:S(2)}, u32[]{:S(2)}) collective-permute-start(bf16[256,1024]{1,0:T(8,128)(2,1)S(1)} %add_convert_fusion.1), channel_id=1, source_target_pairs={{0,2},{2,0},{1,3},{3,1},{4,6},{6,4},{5,7},{7,5},{8,10},{10,8},{9,1... | collective-permute-start | bytes 1572872 | tf_op jit(solution)/shard_map/ppermute | solution.py:346
  50.2 1.7 %collective-permute-start.1 = (bf16[64,1024]{1,0:T(8,128)(2,1)S(1)}, bf16[64,1024]{1,0:T(8,128)(2,1)S(1)}, u32[]{:S(2)}, u32[]{:S(2)}) collective-permute-start(bf16[64,1024]{1,0:T(8,128)(2,1)S(1)} %get-tuple-element.43), channel_id=1, source_target_pairs={{0,1},{1,0},{2,3},{3,2},{4,5},{5,4},{6,7},{7,6},{8,9},{9,8},{10,11... | collective-permute-start | bytes 393224 | tf_op jit(solution)/shard_map/ppermute | solution.py:346
  51.0 1.3 %collective-permute-start.4 = (bf16[64,1024]{1,0:T(8,128)(2,1)S(1)}, bf16[64,1024]{1,0:T(8,128)(2,1)S(1)}, u32[]{:S(2)}, u32[]{:S(2)}) collective-permute-start(bf16[64,1024]{1,0:T(8,128)(2,1)S(1)} %get-tuple-element.44), channel_id=1, source_target_pairs={{0,1},{1,0},{2,3},{3,2},{4,5},{5,4},{6,7},{7,6},{8,9},{9,8},{10,11... | collective-permute-start | bytes 393224 | tf_op jit(solution)/shard_map/ppermute | solution.py:346
  51.1 1.4 %collective-permute-start.3 = (bf16[64,1024]{1,0:T(8,128)(2,1)S(1)}, bf16[64,1024]{1,0:T(8,128)(2,1)S(1)}, u32[]{:S(2)}, u32[]{:S(2)}) collective-permute-start(bf16[64,1024]{1,0:T(8,128)(2,1)S(1)} %get-tuple-element.45), channel_id=1, source_target_pairs={{0,1},{1,0},{2,3},{3,2},{4,5},{5,4},{6,7},{7,6},{8,9},{9,8},{10,11... | collective-permute-start | bytes 393224 | tf_op jit(solution)/shard_map/ppermute | solution.py:346
  51.5 1.3 %collective-permute-start.2 = (bf16[64,1024]{1,0:T(8,128)(2,1)S(1)}, bf16[64,1024]{1,0:T(8,128)(2,1)S(1)}, u32[]{:S(2)}, u32[]{:S(2)}) collective-permute-start(bf16[64,1024]{1,0:T(8,128)(2,1)S(1)} %get-tuple-element.46), channel_id=1, source_target_pairs={{0,1},{1,0},{2,3},{3,2},{4,5},{5,4},{6,7},{7,6},{8,9},{9,8},{10,11... | collective-permute-start | bytes 393224 | tf_op jit(solution)/shard_map/ppermute | solution.py:346

commit v3 on v2

v3 whole, which is shorter than its diff:
```python
import functools

import jax
import jax.numpy as jnp
from jax import lax
from jax.experimental import pallas as pl
from jax.experimental.pallas import tpu as pltpu
from jax.sharding import Mesh
from jax.sharding import PartitionSpec as P

Y_HI, Z, X, Y_LO, CORE = 2, 8, 4, 2, 2
MODES = 16
ROWS = 256
SUBS = 8
STEPS = ROWS // SUBS
LANES = 128
CHUNK = 256
ANY = pl.BlockSpec(memory_space=pl.ANY)
VMEM = pl.BlockSpec(memory_space=pltpu.VMEM)
SMEM = pl.BlockSpec(memory_space=pltpu.SMEM)
EXCHANGES = (("x", X, 1), ("x", X, 3), ("z", Z, 1), ("z", Z, 2), ("z", Z, 6), ("y_hi", Y_HI, 1))
LOCAL_COST = pl.CostEstimate(flops=10**8, bytes_accessed=2**20, transcendentals=0)
COST = pl.CostEstimate(flops=2 * 10**9, bytes_accessed=4 * 2**20, transcendentals=0)
PARAMS = pltpu.CompilerParams(vmem_limit_bytes=16 * 2**20)


def in_hbm(array):
    return pltpu.with_memory_space_constraint(array, pltpu.HBM)


def in_vmem(array):
    return pltpu.with_memory_space_constraint(array, pltpu.VMEM)


def shape_of(shape, dtype=jnp.float32):
    return jax.ShapeDtypeStruct(shape, dtype)


def rows8(row):
    return jnp.broadcast_to(row, (SUBS, row.shape[-1]))


def add_all(terms):
    terms = list(terms)
    while len(terms) > 1:
        terms = [a + b for a, b in zip(terms[::2], terms[1::2])] + terms[len(terms) & ~1 :]
    return terms[0]


def tile_of(index):
    return pl.ds(pl.multiple_of(index * LANES, LANES), LANES)


def expm1(value):
    series = jnp.ones_like(value)
    for n in range(9, 1, -1):
        series = 1.0 + value * (1.0 / n) * series
    return jnp.where(jnp.abs(value) < 0.25, value * series, jnp.exp(value) - 1.0)


def states_kernel(
    pre_hbm, val_hbm, rate_hbm, residue_hbm, skip_hbm,
    total_ref, inner_ref, rate_ref, weight_ref, skip_ref, pre_buf, val_buf, residue_buf, sems
):
    width = pre_hbm.shape[1]
    pairs = ((rate_hbm, rate_ref), (pre_hbm, pre_buf), (val_hbm, val_buf), (residue_hbm, residue_buf), (skip_hbm, skip_ref))
    copies = []
    for start in range(0, width, CHUNK):
        part = pl.ds(start, CHUNK)
        n = len(copies)
        copies.append(
            [pltpu.make_async_copy(hbm.at[:, part], buf.at[:, part], sems.at[n, j]) for j, (hbm, buf) in enumerate(pairs)]
        )
        for copy in copies[-1]:
            copy.start()
    left = (SUBS - 1 - lax.broadcasted_iota(jnp.int32, (SUBS, LANES), 0)).astype(jnp.float32)

    def tile(index):
        cols = tile_of(index)
        factors = [jnp.exp(-float(SUBS) * rows8(rate_ref[m : m + 1, cols])) for m in range(MODES)]
        states = None
        for start in range(0, ROWS, 2 * SUBS):
            rows = pl.ds(start, 2 * SUBS)
            product = pre_buf[rows, cols].astype(jnp.float32) * val_buf[rows, cols].astype(jnp.float32)
            product = product.astype(jnp.bfloat16)
            inner_ref[rows, cols] = product
            value = product.astype(jnp.float32)
            for half in (value[:SUBS], value[SUBS:]):
                if states is None:
                    states = [half] * MODES
                else:
                    states = [f * s + half for f, s in zip(factors, states)]
        totals = []
        for m in range(MODES):
            weight = jnp.exp(-rows8(rate_ref[m : m + 1, cols]) * left)
            totals.append(jnp.sum(states[m] * weight, axis=0, keepdims=True))
        total_ref[:, cols] = jnp.concatenate(totals, axis=0)
        weight_ref[:, cols] = residue_buf[:, cols] * jnp.sqrt(-expm1(-2.0 * rate_ref[:, cols]))

    for n, group in enumerate(copies):
        for copy in group:
            copy.wait()
        pl.loop(n * (CHUNK // LANES), (n + 1) * (CHUNK // LANES))(tile)


def local_kernel(inner_ref, rate_ref, weight_ref, skip_ref, out_ref, inner_buf, taps_buf, sums_buf, *, first_tile):
    lag = lax.broadcasted_iota(jnp.int32, (STEPS, LANES), 0).astype(jnp.float32)
    start = lax.broadcasted_iota(jnp.int32, (STEPS, LANES), 0) == 0
    where = lax.broadcasted_iota(jnp.int32, (SUBS, LANES), 0)

    def at(step):
        return inner_buf[pl.ds(step, SUBS, stride=STEPS), :]

    def tile(index):
        here = tile_of(index)
        cols = tile_of(index + first_tile)
        inner_buf[...] = inner_ref[:, cols].astype(jnp.float32)
        taps = jnp.where(start, skip_ref[:, cols], 0.0)
        for m in range(MODES):
            taps = taps + weight_ref[m : m + 1, cols] * jnp.exp(-rate_ref[m : m + 1, cols] * lag)
        for step in range(STEPS):
            taps_buf[pl.ds(step * SUBS, SUBS), :] = rows8(taps[step : step + 1])
        factors = [jnp.exp(-rows8(rate_ref[m : m + 1, cols])) for m in range(MODES)]
        states = [at(0)] * MODES
        for step in range(1, STEPS):
            value = at(step)
            states = [f * s + value for f, s in zip(factors, states)]
        entering = []
        for m in range(MODES):
            rate = rows8(rate_ref[m : m + 1, cols])
            state = states[m]
            span = 1
            while span < SUBS:
                moved = jnp.where(where >= span, pltpu.roll(state, span, 0), 0.0)
                state = state + jnp.exp(-rate * float(span * STEPS)) * moved
                span *= 2
            state = jnp.where(where >= 1, pltpu.roll(state, 1, 0), 0.0)
            entering.append(state * factors[m] * rows8(weight_ref[m : m + 1, cols]))
        for base in range(0, STEPS, SUBS):
            sums = []
            for _ in range(SUBS):
                sums.append(add_all(entering))
                entering = [f * e for f, e in zip(factors, entering)]
            for source in range(base + SUBS):
                value = at(source)
                for j in range(max(0, source - base), SUBS):
                    tap = taps_buf[pl.ds((base + j - source) * SUBS, SUBS), :]
                    sums[j] = sums[j] + tap * value
            for j in range(SUBS):
                sums_buf[pl.ds(base + j, SUBS, stride=STEPS), :] = sums[j]
        out_ref[:, here] = sums_buf[...]

    pl.loop(0, out_ref.shape[1] // LANES)(tile)


def first_column(place_ref, role, width):
    y_lo, core = place_ref[0], place_ref[1]
    chip = y_lo if role >= CORE else 1 - y_lo
    to_core = core if role % CORE else 1 - core
    return pl.multiple_of((chip * CORE + to_core) * width, width)


def fetching_kernel(place_ref, proj_hbm, post_hbm, inner_ref, rate_ref, weight_ref, skip_ref, out_ref, *refs, first_tile):
    *roles, post_ref, inner_buf, taps_buf, sums_buf, sems = refs
    width, part = roles[0].shape
    cols = pl.ds(first_tile * LANES, part)
    copies = [pltpu.make_async_copy(post_hbm.at[:, cols], post_ref, sems.at[len(roles)])]
    for role, role_ref in enumerate(roles):
        start = pl.multiple_of(first_column(place_ref, role, width) + first_tile * LANES, part)
        copies.append(pltpu.make_async_copy(proj_hbm.at[:, pl.ds(start, part)], role_ref, sems.at[role]))
    for copy in copies:
        copy.start()
    buffers = (inner_buf, taps_buf, sums_buf)
    local_kernel(inner_ref, rate_ref, weight_ref, skip_ref, out_ref, *buffers, first_tile=first_tile)
    for copy in copies:
        copy.wait()


def project(gated_ref, proj_refs, out_ref):
    start = 0
    for proj_ref in proj_refs:
        part = proj_ref.shape[1]
        sums = jnp.dot(gated_ref[...], proj_ref[...], preferred_element_type=jnp.float32)
        out_ref[:, start : start + part] = sums.astype(out_ref.dtype)
        start += part


def mix_kernel(carry_ref, rate_ref, weight_ref, *refs):
    *refs, gated_ref, sent_ref = refs
    parts = len(refs) // 3
    local_refs, post_refs, proj_refs = refs[:parts], refs[parts : 2 * parts], refs[2 * parts :]
    rows_count = gated_ref.shape[0]
    ahead = (lax.broadcasted_iota(jnp.int32, (SUBS, LANES), 0) + 1).astype(jnp.float32)

    def tile(index, local_ref, post_ref, offset):
        here = tile_of(index)
        cols = tile_of(index + offset)
        carry = carry_ref[:, cols] * weight_ref[:, cols]
        terms = []
        factors = []
        for m in range(MODES):
            rate = rows8(rate_ref[m : m + 1, cols])
            terms.append(jnp.exp(-rate * ahead) * rows8(carry[m : m + 1]))
            factors.append(jnp.exp(-rate * float(SUBS)))
        for start in range(0, rows_count, 2 * SUBS):
            sums = []
            for _ in range(2):
                sums.append(add_all(terms))
                terms = [f * t for f, t in zip(factors, terms)]
            rows = pl.ds(start, 2 * SUBS)
            conv = local_ref[rows, here] + jnp.concatenate(sums, axis=0)
            gated_ref[rows, cols] = (post_ref[rows, here].astype(jnp.float32) * conv).astype(jnp.bfloat16)

    each = local_refs[0].shape[1] // LANES
    for part in range(parts):
        sources = (local_refs[part], post_refs[part], part * each)
        pl.loop(0, each)(lambda i, sources=sources: tile(i, *sources))
    project(gated_ref, proj_refs, sent_ref)


def own_kernel(gated_ref, *refs):
    *proj_refs, kept_ref = refs
    project(gated_ref, proj_refs, kept_ref)


def near_kernel(gated_ref, *refs):
    *proj_refs, sent_ref, kept_ref = refs
    parts = len(proj_refs) // 2
    project(gated_ref, proj_refs[:parts], sent_ref)
    project(gated_ref, proj_refs[parts:], kept_ref)


def body(pre_gate, post_gate, values, decay_rates, residues, skip_gain, out_weight):
    rows, width = pre_gate.shape
    y_hi, z, x = (lax.axis_index(name) for name in ("y_hi", "z", "x"))
    place = jnp.stack([lax.axis_index("y_lo"), lax.axis_index("core")])
    block = (y_hi * Z + z) * X + x
    parts = width // CHUNK
    bf16 = jnp.bfloat16
    places = []
    for step in range(len(EXCHANGES)):
        later = (block >> step) & 1
        offset = (block & ((1 << step) - 1)) * ROWS
        places += [later.astype(jnp.float32), (1 - later).astype(jnp.float32), -offset.astype(jnp.float32)]
    pre_gate, place, *places = lax.optimization_barrier((pre_gate, place, *places))
    total, inner, rates, weights, skips = pl.pallas_call(
        states_kernel,
        in_specs=[ANY] * 5,
        out_specs=[VMEM] * 5,
        out_shape=[
            shape_of((MODES, width)),
            shape_of((rows, width), bf16),
            shape_of((MODES, width)),
            shape_of((MODES, width)),
            shape_of((1, width)),
        ],
        scratch_shapes=[
            pltpu.VMEM((rows, width), bf16),
            pltpu.VMEM((rows, width), bf16),
            pltpu.VMEM((MODES, width), jnp.float32),
            pltpu.SemaphoreType.DMA((parts, 5)),
        ],
        name="states",
        compiler_params=PARAMS,
    )(*(in_hbm(a) for a in (pre_gate, values, decay_rates.T, residues.T, skip_gain[None, :])))

    def local(part, inner):
        outs = [shape_of((rows, CHUNK))] + [shape_of((width, CHUNK), bf16)] * (2 * CORE) + [shape_of((rows, CHUNK), bf16)]
        return pl.pallas_call(
            functools.partial(fetching_kernel, first_tile=part * (CHUNK // LANES)),
            in_specs=[SMEM, ANY, ANY] + [VMEM] * 4,
            out_specs=[VMEM] * len(outs),
            out_shape=outs,
            scratch_shapes=[pltpu.VMEM((rows, LANES), jnp.float32)] * 3 + [pltpu.SemaphoreType.DMA((len(outs),))],
            cost_estimate=LOCAL_COST,
            name="local",
            compiler_params=PARAMS,
        )(place, in_hbm(out_weight), in_hbm(post_gate), *(in_vmem(a) for a in (inner, rates, weights, skips)))

    group = total
    carry = jnp.zeros_like(total)
    pieces = []
    for step, (axis, size, flip) in enumerate(EXCHANGES):
        pairs = [(i, i ^ flip) for i in range(size)]
        other = lax.ppermute(group.astype(bf16), axis, pairs).astype(jnp.float32)
        later, earlier, offset = places[3 * step : 3 * step + 3]
        decay = jnp.exp(-float(ROWS << step) * rates)
        carry = carry + later * jnp.exp(offset * rates) * other
        group = (later * other + earlier * group) * decay + (later * group + earlier * other)
        part = step - (len(EXCHANGES) - parts)
        if part >= 0:
            piece = local(part, inner)
            group, carry, *piece = lax.optimization_barrier((group, carry, *piece))
            pieces.append(piece)
        inner, group, carry = lax.optimization_barrier((inner, group, carry))
    locals_, *roles, posts = (list(part) for part in zip(*pieces))
    arrays = (carry, rates, weights, *locals_, *posts, *roles[0])
    gated, sent = pl.pallas_call(
        mix_kernel,
        in_specs=[VMEM] * len(arrays),
        out_specs=[VMEM] * 2,
        out_shape=[shape_of((rows, width), bf16), shape_of((rows, width), bf16)],
        cost_estimate=COST,
        name="mix",
        compiler_params=PARAMS,
    )(*(in_vmem(a) for a in arrays))
    kept = pl.pallas_call(
        own_kernel,
        in_specs=[VMEM] * (1 + parts),
        out_specs=VMEM,
        out_shape=shape_of((rows, width)),
        cost_estimate=COST,
        name="own",
        compiler_params=PARAMS,
    )(*(in_vmem(a) for a in (gated, *roles[1])))

    def swap(array, axis):
        return lax.ppermute(array.astype(jnp.bfloat16), axis, [(0, 1), (1, 0)]).astype(jnp.float32)

    to_far = (swap(sent, "core") + kept).astype(bf16)
    gated, to_far = lax.optimization_barrier((gated, to_far))
    far_sum = swap(to_far, "y_lo")
    sent, kept = pl.pallas_call(
        near_kernel,
        in_specs=[VMEM] * (1 + 2 * parts),
        out_specs=[VMEM] * 2,
        out_shape=[shape_of((rows, width), bf16), shape_of((rows, width))],
        cost_estimate=COST,
        name="near",
        compiler_params=PARAMS,
    )(*(in_vmem(a) for a in (gated, *roles[2], *roles[3])))
    quarter = rows // 4
    received = [swap(sent[i : i + quarter], "core") for i in range(0, rows, quarter)]
    near_sum = jnp.concatenate(received, axis=0) + kept
    return (near_sum + far_sum).astype(bf16)


def solution(mesh):
    axes = ("y_hi", "z", "x", "y_lo", "core")
    split = Mesh(mesh.devices.reshape(Y_HI, Z, X, Y_LO, CORE), axes)
    seq, chan = axes[:3], axes[3:]
    placed = (P(seq, chan), P(seq, chan), P(seq, chan), P(chan, None), P(chan, None), P(chan), P(chan, None))
    return jax.shard_map(body, mesh=split, in_specs=placed, out_specs=P(seq, chan), check_vma=False)
```

time: 60.7 us -> 55.7 us (0.918)
  waiting for transfers between devices: 20.2 us -> 12.6 us
  starting transfers between devices: 20.9 us -> 25.2 us
  Pallas kernels: 17.9 us -> 15.8 us
    ppermute x0 -> x6, starting transfers between devices: none -> 16.8 us  [body(): other = lax.ppermute(group.astype(bf16), axis, pairs).astype(jnp.float32)]
    all_to_all x2 -> x0, starting transfers between devices: 15.7 us -> none  [the longest x1 8.19 us: body(): far = lax.all_to_all(sends, 'z', 0, 0, tiled=True)]
    all_to_all x2 -> x0, waiting for transfers between devices: 11.6 us -> none  [the longest x1 6.66 us: body(): far = lax.all_to_all(sends, 'z', 0, 0, tiled=True)]
    ppermute x6, starting transfers between devices: 5.27 us -> 8.45 us  [swap(): lax.ppermute(array.astype(jnp.bfloat16), axis, [(0, 1), (1, 0)])]
    ppermute x0 -> x6, waiting for transfers between devices: none -> 2.62 us  [body(): other = lax.ppermute(group.astype(bf16), axis, pairs).astype(jnp.float32)]
    ppermute x6, waiting for transfers between devices: 8.6 us -> 10 us  [swap(): lax.ppermute(array.astype(jnp.bfloat16), axis, [(0, 1), (1, 0)])]
    pallas_call x6 -> x7, Pallas kernels: 14.3 us -> 12.9 us  [the longest x4 8.83 us: local(): pl.pallas_call(functools.partial(fetching_kernel, first_tile=part * (CHUN...]
    pallas_call x1, Pallas kernels: 3.61 us -> 2.95 us  [body(): pl.pallas_call(states_kernel, in_specs=[ANY] * 5, out_specs=[VMEM] * 5, o...]
  transfers between devices with their start and end apart: 8 -> 12, of which waited for: 8 -> 8; matrix products, arithmetic and copies ran while one was open for 0% -> 0% of each run, Pallas kernels for 16% -> 19%
where the time goes in v3:
time: 55.7 us; the launch traced here: 55.5 us
  starting transfers between devices  25.2 us (45%)
  Pallas kernels  15.8 us (28%)
  waiting for transfers between devices  12.6 us (23%)
  other arithmetic  1.57 us (3%)
    ppermute x6, starting transfers between devices, body(): other = lax.ppermute(group.astype(bf16), axis, pairs).astype(jnp.float32)  16.8 us
    ppermute x6, waiting for transfers between devices, swap(): lax.ppermute(array.astype(jnp.bfloat16), axis, [(0, 1), (1, 0)])  10 us
    pallas_call x4, Pallas kernels, local(): pl.pallas_call(functools.partial(fetching_kernel, first_tile=part * (CHUN...  8.83 us
    ppermute x6, starting transfers between devices, swap(): lax.ppermute(array.astype(jnp.bfloat16), axis, [(0, 1), (1, 0)])  8.45 us
    pallas_call x1, Pallas kernels, body(): pl.pallas_call(states_kernel, in_specs=[ANY] * 5, out_specs=[VMEM] * 5, o...  2.95 us
    ppermute x6, waiting for transfers between devices, body(): other = lax.ppermute(group.astype(bf16), axis, pairs).astype(jnp.float32)  2.62 us
    pallas_call x1, Pallas kernels, body(): pl.pallas_call(mix_kernel, in_specs=[VMEM] * len(arrays), out_specs=[VMEM...  2.1 us
    pallas_call x1, Pallas kernels, body(): pl.pallas_call(near_kernel, in_specs=[VMEM] * (1 + 2 * parts), out_specs=...  1.24 us
  transfers between devices with their start and end apart: 12, of which 8 were waited for; matrix products, arithmetic and copies ran while one was open for 0% of the time, Pallas kernels for 19%

profile of v3, /device:TPU:1, one launch (start us, length us, event | category | flops | bytes accessed | tf_op | source)
XLA Modules:
  0.0 55.5 jit_solution(5956702836333756141)
XLA Ops:
  0.0 0.1 pad_add_fusion.place_ref
  0.1 3.0 %states.1 = (f32[16,1024]{1,0:T(8,128)S(1)}, bf16[256,1024]{1,0:T(8,128)(2,1)S(1)}, f32[16,1024]{1,0:T(8,128)S(1)}, f32[16,1024]{1,0:T(8,128)S(1)}, f32[1,1024]{1,0:T(1,128)S(1)}) custom-call(bf16[256,1024]{1,0:T(8,128)(2,1)} %pre_hbm, bf16[256,1024]{1,0:T(8,128)(2,1)} %val_hbm.1, f32[16,1024]{1,0:T(8,128)} %bitcast.5, f32[16,1024]{1,0:T(8,128)} %bitcast.6, ...), custom_call_target="tpu_custom_call" | custom-call | tf_op jit(solution)/shard_map/states/pallas_call | solution.py:246
  3.0 2.1 %collective-permute-start = (bf16[16,1024]{1,0:T(8,128)(2,1)S(1)}, bf16[16,1024]{1,0:T(8,128)(2,1)S(1)}, u32[]{:S(2)}, u32[]{:S(2)}) collective-permute-start(bf16[16,1024]{1,0:T(8,128)(2,1)S(1)} %convert_element_type.117), channel_id=1, source_target_pairs={{0,4},{4,0},{8,12},{12,8},{1,5},{5,1},{9,13},{13,9},{2,6},{6,2},{1... | collective-permute-start | bytes 98312 | tf_op jit(solution)/shard_map/ppermute | solution.py:285
  5.2 1.3 %collective-permute-done = bf16[16,1024]{1,0:T(8,128)(2,1)S(1)} collective-permute-done((bf16[16,1024]{1,0:T(8,128)(2,1)S(1)}, bf16[16,1024]{1,0:T(8,128)(2,1)S(1)}, u32[]{:S(2)}, u32[]{:S(2)}) %collective-permute-start) | collective-permute-done | bytes 32800 | tf_op jit(solution)/shard_map/ppermute | solution.py:285
  6.5 2.8 %collective-permute-start.1 = (bf16[16,1024]{1,0:T(8,128)(2,1)S(1)}, bf16[16,1024]{1,0:T(8,128)(2,1)S(1)}, u32[]{:S(2)}, u32[]{:S(2)}) collective-permute-start(bf16[16,1024]{1,0:T(8,128)(2,1)S(1)} %convert_element_type.119), channel_id=1, source_target_pairs={{0,12},{4,8},{8,4},{12,0},{1,13},{5,9},{9,5},{13,1},{2,14},{6,10},... | collective-permute-start | bytes 98312 | tf_op jit(solution)/shard_map/ppermute | solution.py:285
  9.4 1.3 %collective-permute-done.1 = bf16[16,1024]{1,0:T(8,128)(2,1)S(1)} collective-permute-done((bf16[16,1024]{1,0:T(8,128)(2,1)S(1)}, bf16[16,1024]{1,0:T(8,128)(2,1)S(1)}, u32[]{:S(2)}, u32[]{:S(2)}) %collective-permute-start.1) | collective-permute-done | bytes 32800 | tf_op jit(solution)/shard_map/ppermute | solution.py:285
  10.7 1.9 %collective-permute-start.2 = (bf16[16,1024]{1,0:T(8,128)(2,1)S(1)}, bf16[16,1024]{1,0:T(8,128)(2,1)S(1)}, u32[]{:S(2)}, u32[]{:S(2)}) collective-permute-start(bf16[16,1024]{1,0:T(8,128)(2,1)S(1)} %convert_element_type.121), channel_id=1, source_target_pairs={{0,16},{16,0},{32,48},{48,32},{64,80},{80,64},{96,112},{112,96},{1... | collective-permute-start | bytes 98312 | tf_op jit(solution)/shard_map/ppermute | solution.py:285
  12.6 2.2 %local.4 = (f32[256,256]{1,0:T(8,128)S(1)}, bf16[1024,256]{1,0:T(8,128)(2,1)S(1)}, bf16[1024,256]{1,0:T(8,128)(2,1)S(1)}, bf16[1024,256]{1,0:T(8,128)(2,1)S(1)},...) custom-call(s32[2]{0:T(128)S(1)} %pad_add_fusion.place_ref, bf16[1024,4096]{1,0:T(8,128)(2,1)} %proj_hbm.7, ...), custom_call_target="tpu_custom_call" | custom-call | flops 100000000 | bytes 1048576 | tf_op jit(solution)/shard_map/local/pallas_call | solution.py:269
  14.9 0.0 collective-permute-done.2
  14.9 0.1 fusion.13
  14.9 3.1 %collective-permute-start.3 = (bf16[16,1024]{1,0:T(8,128)(2,1)S(1)}, bf16[16,1024]{1,0:T(8,128)(2,1)S(1)}, u32[]{:S(2)}, u32[]{:S(2)}) collective-permute-start(bf16[16,1024]{1,0:T(8,128)(2,1)S(1)} %convert_element_type.123), channel_id=1, source_target_pairs={{0,32},{16,48},{32,0},{48,16},{64,96},{80,112},{96,64},{112,80},{1... | collective-permute-start | bytes 98312 | tf_op jit(solution)/shard_map/ppermute | solution.py:285
  18.0 2.2 %local.5 = (f32[256,256]{1,0:T(8,128)S(1)}, bf16[1024,256]{1,0:T(8,128)(2,1)S(1)}, bf16[1024,256]{1,0:T(8,128)(2,1)S(1)}, bf16[1024,256]{1,0:T(8,128)(2,1)S(1)},...) custom-call(s32[2]{0:T(128)S(1)} %pad_add_fusion.place_ref, bf16[1024,4096]{1,0:T(8,128)(2,1)} %proj_hbm.7, ...), custom_call_target="tpu_custom_call" | custom-call | flops 100000000 | bytes 1048576 | tf_op jit(solution)/shard_map/local/pallas_call | solution.py:269
  20.2 0.0 collective-permute-done.3
  20.2 0.1 fusion.18
  20.3 3.9 %collective-permute-start.4 = (bf16[16,1024]{1,0:T(8,128)(2,1)S(1)}, bf16[16,1024]{1,0:T(8,128)(2,1)S(1)}, u32[]{:S(2)}, u32[]{:S(2)}) collective-permute-start(bf16[16,1024]{1,0:T(8,128)(2,1)S(1)} %convert_element_type.125), channel_id=1, source_target_pairs={{0,96},{16,112},{32,64},{48,80},{64,32},{80,48},{96,0},{112,16},{1... | collective-permute-start | bytes 98312 | tf_op jit(solution)/shard_map/ppermute | solution.py:285
  24.2 2.2 %local.6 = (f32[256,256]{1,0:T(8,128)S(1)}, bf16[1024,256]{1,0:T(8,128)(2,1)S(1)}, bf16[1024,256]{1,0:T(8,128)(2,1)S(1)}, bf16[1024,256]{1,0:T(8,128)(2,1)S(1)},...) custom-call(s32[2]{0:T(128)S(1)} %pad_add_fusion.place_ref, bf16[1024,4096]{1,0:T(8,128)(2,1)} %proj_hbm.7, ...), custom_call_target="tpu_custom_call" | custom-call | flops 100000000 | bytes 1048576 | tf_op jit(solution)/shard_map/local/pallas_call | solution.py:269
  26.4 0.0 collective-permute-done.4
  26.5 3.0 %collective-permute-start.5 = (bf16[16,1024]{1,0:T(8,128)(2,1)S(1)}, bf16[16,1024]{1,0:T(8,128)(2,1)S(1)}, u32[]{:S(2)}, u32[]{:S(2)}) collective-permute-start(bf16[16,1024]{1,0:T(8,128)(2,1)S(1)} %fusion.21), channel_id=1, source_target_pairs={{0,128},{128,0},{1,129},{129,1},{2,130},{130,2},{3,131},{131,3},{4... | collective-permute-start | bytes 98312 | tf_op jit(solution)/shard_map/ppermute | solution.py:285
  29.5 2.2 %local.7 = (f32[256,256]{1,0:T(8,128)S(1)}, bf16[1024,256]{1,0:T(8,128)(2,1)S(1)}, bf16[1024,256]{1,0:T(8,128)(2,1)S(1)}, bf16[1024,256]{1,0:T(8,128)(2,1)S(1)},...) custom-call(s32[2]{0:T(128)S(1)} %pad_add_fusion.place_ref, bf16[1024,4096]{1,0:T(8,128)(2,1)} %proj_hbm.7, ...), custom_call_target="tpu_custom_call" | custom-call | flops 100000000 | bytes 1048576 | tf_op jit(solution)/shard_map/local/pallas_call | solution.py:269
  31.7 0.0 collective-permute-done.5
  31.7 2.1 %mix.1 = (bf16[256,1024]{1,0:T(8,128)(2,1)S(1)}, bf16[256,1024]{1,0:T(8,128)(2,1)S(1)}) custom-call(f32[16,1024]{1,0:T(8,128)S(1)} %multiply_add_fusion.carry_ref, f32[16,1024]{1,0:T(8,128)S(1)} %get-tuple-element.111.rate_ref, f32[16,1024]{1,0:T(8,128)S(1)} %get-tuple-element.126.weight_ref, f32[256,256]{1,0:T(8,128)S(1)} %get-tuple-element.177.refs_0_, ...), custom_call_target="tpu_custom_call" | custom-call | flops 2000000000 | bytes 4194304 | tf_op jit(solution)/shard_map/mix/pallas_call | solution.py:298
  33.9 5.7 %collective-permute-start.6 = (bf16[256,1024]{1,0:T(8,128)(2,1)S(1)}, bf16[256,1024]{1,0:T(8,128)(2,1)S(1)}, u32[]{:S(2)}, u32[]{:S(2)}) collective-permute-start(bf16[256,1024]{1,0:T(8,128)(2,1)S(1)} %get-tuple-element.190), channel_id=1, source_target_pairs={{0,1},{1,0},{2,3},{3,2},{4,5},{5,4},{6,7},{7,6},{8,9},{9,8},{10,11... | collective-permute-start | bytes 1572872 | tf_op jit(solution)/shard_map/ppermute | solution.py:318
  39.6 0.7 %own.1 = f32[256,1024]{1,0:T(8,128)S(1)} custom-call(bf16[256,1024]{1,0:T(8,128)(2,1)S(1)} %get-tuple-element.195.gated_ref, bf16[1024,256]{1,0:T(8,128)(2,1)S(1)} %get-tuple-element.191.refs_0_, bf16[1024,256]{1,0:T(8,128)(2,1)S(1)} %get-tuple-element.192.refs_1_, bf16[1024,256]{1,0:T(8,128)(2,1)S(1)} %get-tuple-element.193.refs_2_, ...), custom_call_target="tpu_custom_call" | custom-call | flops 2000000000 | bytes 4194304 | tf_op jit(solution)/shard_map/own/pallas_call | solution.py:307
  40.3 0.8 %collective-permute-done.6 = bf16[256,1024]{1,0:T(8,128)(2,1)S(1)} collective-permute-done((bf16[256,1024]{1,0:T(8,128)(2,1)S(1)}, bf16[256,1024]{1,0:T(8,128)(2,1)S(1)}, u32[]{:S(2)}, u32[]{:S(2)}) %collective-permute-start.6) | collective-permute-done | bytes 524320 | tf_op jit(solution)/shard_map/ppermute | solution.py:318
  41.1 0.1 add_convert_fusion.1
  41.3 1.4 %collective-permute-start.11 = (bf16[256,1024]{1,0:T(8,128)(2,1)S(1)}, bf16[256,1024]{1,0:T(8,128)(2,1)S(1)}, u32[]{:S(2)}, u32[]{:S(2)}) collective-permute-start(bf16[256,1024]{1,0:T(8,128)(2,1)S(1)} %add_convert_fusion.1), channel_id=1, source_target_pairs={{0,2},{2,0},{1,3},{3,1},{4,6},{6,4},{5,7},{7,5},{8,10},{10,8},{9,1... | collective-permute-start | bytes 1572872 | tf_op jit(solution)/shard_map/ppermute | solution.py:318
  42.6 1.2 %near.1 = (bf16[256,1024]{1,0:T(8,128)(2,1)S(1)}, f32[256,1024]{1,0:T(8,128)S(1)}) custom-call(bf16[256,1024]{1,0:T(8,128)(2,1)S(1)} %get-tuple-element.195.gated_ref, bf16[1024,256]{1,0:T(8,128)(2,1)S(1)} %get-tuple-element.196.refs_0_, bf16[1024,256]{1,0:T(8,128)(2,1)S(1)} %get-tuple-element.197.refs_1_, bf16[1024,256]{1,0:T(8,128)(2,1)S(1)} %get-tuple-element.198.refs_2_, ...), custom_call_target="tpu_custom_call" | custom-call | flops 2000000000 | bytes 4194304 | tf_op jit(solution)/shard_map/near/pallas_call | solution.py:323
  43.9 0.7 %collective-permute-start.7 = (bf16[64,1024]{1,0:T(8,128)(2,1)S(1)}, bf16[64,1024]{1,0:T(8,128)(2,1)S(1)}, u32[]{:S(2)}, u32[]{:S(2)}) collective-permute-start(bf16[64,1024]{1,0:T(8,128)(2,1)S(1)} %get-tuple-element.207), channel_id=1, source_target_pairs={{0,1},{1,0},{2,3},{3,2},{4,5},{5,4},{6,7},{7,6},{8,9},{9,8},{10,11... | collective-permute-start | bytes 393224 | tf_op jit(solution)/shard_map/ppermute | solution.py:318
  44.7 0.1 collective-permute-start.10
  44.8 0.4 collective-permute-start.9
  45.2 0.1 collective-permute-start.8
  45.3 0.4 collective-permute-done.7
  45.7 0.4 collective-permute-done.10
  46.0 0.2 collective-permute-done.9
  46.2 0.3 collective-permute-done.8
  46.5 8.0 %collective-permute-done.11 = bf16[256,1024]{1,0:T(8,128)(2,1)S(1)} collective-permute-done((bf16[256,1024]{1,0:T(8,128)(2,1)S(1)}, bf16[256,1024]{1,0:T(8,128)(2,1)S(1)}, u32[]{:S(2)}, u32[]{:S(2)}) %collective-permute-start.11) | collective-permute-done | bytes 524320 | tf_op jit(solution)/shard_map/ppermute | solution.py:318
  54.5 1.0 %add_convert_fusion = bf16[256,1024]{1,0:T(8,128)(2,1)} fusion(bf16[256,1024]{1,0:T(8,128)(2,1)S(1)} %collective-permute-done.11, f32[256,1024]{1,0:T(8,128)S(1)} %get-tuple-element.205, bf16[64,1024]{1,0:T(8,128)(2,1)S(1)} %collective-permute-done.10, bf16[64,1024]{1,0:T(8,128)(2,1)S(1)} %collective-permute-done.9, ...), kind=kLoop, calls=%fused_computation | loop fusion | flops 3145728 | bytes 2621440 | tf_op jit(solution)/shard_map/convert_element_type | solution.py:335
  (11 shorter events, 0.3 us)
Async XLA Ops:
  3.0 3.4 %collective-permute-start = (bf16[16,1024]{1,0:T(8,128)(2,1)S(1)}, bf16[16,1024]{1,0:T(8,128)(2,1)S(1)}, u32[]{:S(2)}, u32[]{:S(2)}) collective-permute-start(bf16[16,1024]{1,0:T(8,128)(2,1)S(1)} %convert_element_type.117), channel_id=1, source_target_pairs={{0,4},{4,0},{8,12},{12,8},{1,5},{5,1},{9,13},{13,9},{2,6},{6,2},{1... | collective-permute-start | bytes 98312 | tf_op jit(solution)/shard_map/ppermute | solution.py:285
  6.5 4.1 %collective-permute-start.1 = (bf16[16,1024]{1,0:T(8,128)(2,1)S(1)}, bf16[16,1024]{1,0:T(8,128)(2,1)S(1)}, u32[]{:S(2)}, u32[]{:S(2)}) collective-permute-start(bf16[16,1024]{1,0:T(8,128)(2,1)S(1)} %convert_element_type.119), channel_id=1, source_target_pairs={{0,12},{4,8},{8,4},{12,0},{1,13},{5,9},{9,5},{13,1},{2,14},{6,10},... | collective-permute-start | bytes 98312 | tf_op jit(solution)/shard_map/ppermute | solution.py:285
  10.7 4.1 %collective-permute-start.2 = (bf16[16,1024]{1,0:T(8,128)(2,1)S(1)}, bf16[16,1024]{1,0:T(8,128)(2,1)S(1)}, u32[]{:S(2)}, u32[]{:S(2)}) collective-permute-start(bf16[16,1024]{1,0:T(8,128)(2,1)S(1)} %convert_element_type.121), channel_id=1, source_target_pairs={{0,16},{16,0},{32,48},{48,32},{64,80},{80,64},{96,112},{112,96},{1... | collective-permute-start | bytes 98312 | tf_op jit(solution)/shard_map/ppermute | solution.py:285
  14.9 5.3 %collective-permute-start.3 = (bf16[16,1024]{1,0:T(8,128)(2,1)S(1)}, bf16[16,1024]{1,0:T(8,128)(2,1)S(1)}, u32[]{:S(2)}, u32[]{:S(2)}) collective-permute-start(bf16[16,1024]{1,0:T(8,128)(2,1)S(1)} %convert_element_type.123), channel_id=1, source_target_pairs={{0,32},{16,48},{32,0},{48,16},{64,96},{80,112},{96,64},{112,80},{1... | collective-permute-start | bytes 98312 | tf_op jit(solution)/shard_map/ppermute | solution.py:285
  20.3 6.1 %collective-permute-start.4 = (bf16[16,1024]{1,0:T(8,128)(2,1)S(1)}, bf16[16,1024]{1,0:T(8,128)(2,1)S(1)}, u32[]{:S(2)}, u32[]{:S(2)}) collective-permute-start(bf16[16,1024]{1,0:T(8,128)(2,1)S(1)} %convert_element_type.125), channel_id=1, source_target_pairs={{0,96},{16,112},{32,64},{48,80},{64,32},{80,48},{96,0},{112,16},{1... | collective-permute-start | bytes 98312 | tf_op jit(solution)/shard_map/ppermute | solution.py:285
  26.5 5.2 %collective-permute-start.5 = (bf16[16,1024]{1,0:T(8,128)(2,1)S(1)}, bf16[16,1024]{1,0:T(8,128)(2,1)S(1)}, u32[]{:S(2)}, u32[]{:S(2)}) collective-permute-start(bf16[16,1024]{1,0:T(8,128)(2,1)S(1)} %fusion.21), channel_id=1, source_target_pairs={{0,128},{128,0},{1,129},{129,1},{2,130},{130,2},{3,131},{131,3},{4... | collective-permute-start | bytes 98312 | tf_op jit(solution)/shard_map/ppermute | solution.py:285
  33.9 7.3 %collective-permute-start.6 = (bf16[256,1024]{1,0:T(8,128)(2,1)S(1)}, bf16[256,1024]{1,0:T(8,128)(2,1)S(1)}, u32[]{:S(2)}, u32[]{:S(2)}) collective-permute-start(bf16[256,1024]{1,0:T(8,128)(2,1)S(1)} %get-tuple-element.190), channel_id=1, source_target_pairs={{0,1},{1,0},{2,3},{3,2},{4,5},{5,4},{6,7},{7,6},{8,9},{9,8},{10,11... | collective-permute-start | bytes 1572872 | tf_op jit(solution)/shard_map/ppermute | solution.py:318
  41.3 13.2 %collective-permute-start.11 = (bf16[256,1024]{1,0:T(8,128)(2,1)S(1)}, bf16[256,1024]{1,0:T(8,128)(2,1)S(1)}, u32[]{:S(2)}, u32[]{:S(2)}) collective-permute-start(bf16[256,1024]{1,0:T(8,128)(2,1)S(1)} %add_convert_fusion.1), channel_id=1, source_target_pairs={{0,2},{2,0},{1,3},{3,1},{4,6},{6,4},{5,7},{7,5},{8,10},{10,8},{9,1... | collective-permute-start | bytes 1572872 | tf_op jit(solution)/shard_map/ppermute | solution.py:318
  43.9 1.7 %collective-permute-start.7 = (bf16[64,1024]{1,0:T(8,128)(2,1)S(1)}, bf16[64,1024]{1,0:T(8,128)(2,1)S(1)}, u32[]{:S(2)}, u32[]{:S(2)}) collective-permute-start(bf16[64,1024]{1,0:T(8,128)(2,1)S(1)} %get-tuple-element.207), channel_id=1, source_target_pairs={{0,1},{1,0},{2,3},{3,2},{4,5},{5,4},{6,7},{7,6},{8,9},{9,8},{10,11... | collective-permute-start | bytes 393224 | tf_op jit(solution)/shard_map/ppermute | solution.py:318
  44.7 1.3 %collective-permute-start.10 = (bf16[64,1024]{1,0:T(8,128)(2,1)S(1)}, bf16[64,1024]{1,0:T(8,128)(2,1)S(1)}, u32[]{:S(2)}, u32[]{:S(2)}) collective-permute-start(bf16[64,1024]{1,0:T(8,128)(2,1)S(1)} %get-tuple-element.208), channel_id=1, source_target_pairs={{0,1},{1,0},{2,3},{3,2},{4,5},{5,4},{6,7},{7,6},{8,9},{9,8},{10,11... | collective-permute-start | bytes 393224 | tf_op jit(solution)/shard_map/ppermute | solution.py:318
  44.8 1.4 %collective-permute-start.9 = (bf16[64,1024]{1,0:T(8,128)(2,1)S(1)}, bf16[64,1024]{1,0:T(8,128)(2,1)S(1)}, u32[]{:S(2)}, u32[]{:S(2)}) collective-permute-start(bf16[64,1024]{1,0:T(8,128)(2,1)S(1)} %get-tuple-element.209), channel_id=1, source_target_pairs={{0,1},{1,0},{2,3},{3,2},{4,5},{5,4},{6,7},{7,6},{8,9},{9,8},{10,11... | collective-permute-start | bytes 393224 | tf_op jit(solution)/shard_map/ppermute | solution.py:318
  45.2 1.3 %collective-permute-start.8 = (bf16[64,1024]{1,0:T(8,128)(2,1)S(1)}, bf16[64,1024]{1,0:T(8,128)(2,1)S(1)}, u32[]{:S(2)}, u32[]{:S(2)}) collective-permute-start(bf16[64,1024]{1,0:T(8,128)(2,1)S(1)} %get-tuple-element.210), channel_id=1, source_target_pairs={{0,1},{1,0},{2,3},{3,2},{4,5},{5,4},{6,7},{7,6},{8,9},{9,8},{10,11... | collective-permute-start | bytes 393224 | tf_op jit(solution)/shard_map/ppermute | solution.py:318

commit v4 on v3

--- a/solution.py
+++ b/solution.py
@@ -18,7 +18,12 @@
 ANY = pl.BlockSpec(memory_space=pl.ANY)
 VMEM = pl.BlockSpec(memory_space=pltpu.VMEM)
 SMEM = pl.BlockSpec(memory_space=pltpu.SMEM)
-EXCHANGES = (("x", X, 1), ("x", X, 3), ("z", Z, 1), ("z", Z, 2), ("z", Z, 6), ("y_hi", Y_HI, 1))
+STAGES = (
+    ("x", X, ((1, 1), (3, 3), (2, 2))),
+    ("z", Z, ((1, 1), (2, 2), (3, 3))),
+    ("z", Z, ((6, 1),)),
+    ("y_hi", Y_HI, ((1, 1),)),
+)
 LOCAL_COST = pl.CostEstimate(flops=10**8, bytes_accessed=2**20, transcendentals=0)
 COST = pl.CostEstimate(flops=2 * 10**9, bytes_accessed=4 * 2**20, transcendentals=0)
 PARAMS = pltpu.CompilerParams(vmem_limit_bytes=16 * 2**20)
@@ -238,10 +243,16 @@
     parts = width // CHUNK
     bf16 = jnp.bfloat16
     places = []
-    for step in range(len(EXCHANGES)):
-        later = (block >> step) & 1
-        offset = (block & ((1 << step) - 1)) * ROWS
-        places += [later.astype(jnp.float32), (1 - later).astype(jnp.float32), -offset.astype(jnp.float32)]
+    blocks = 1
+    for _, _, partners in STAGES:
+        ways = len(partners) + 1
+        mine = block // blocks % ways
+        for other in (0,) + tuple(other for _, other in partners):
+            member = mine ^ other
+            after = (ways - 1 - member) * (blocks * ROWS)
+            before = (mine - 1 - member) * (blocks * ROWS) + block % blocks * ROWS
+            places += [-after.astype(jnp.float32), -jnp.maximum(before, 0).astype(jnp.float32), (member < mine).astype(jnp.float32)]
+        blocks *= ways
     pre_gate, place, *places = lax.optimization_barrier((pre_gate, place, *places))
     total, inner, rates, weights, skips = pl.pallas_call(
         states_kernel,
@@ -280,14 +291,19 @@
     group = total
     carry = jnp.zeros_like(total)
     pieces = []
-    for step, (axis, size, flip) in enumerate(EXCHANGES):
-        pairs = [(i, i ^ flip) for i in range(size)]
-        other = lax.ppermute(group.astype(bf16), axis, pairs).astype(jnp.float32)
-        later, earlier, offset = places[3 * step : 3 * step + 3]
-        decay = jnp.exp(-float(ROWS << step) * rates)
-        carry = carry + later * jnp.exp(offset * rates) * other
-        group = (later * other + earlier * group) * decay + (later * group + earlier * other)
-        part = step - (len(EXCHANGES) - parts)
+    for step, (axis, size, partners) in enumerate(STAGES):
+        others = [
+            lax.ppermute(group.astype(bf16), axis, [(i, i ^ flip) for i in range(size)]).astype(jnp.float32)
+            for flip, _ in partners
+        ]
+        after, _, _ = places[:3]
+        group = jnp.exp(after * rates) * group
+        for n, other in enumerate(others):
+            after, before, earlier = places[3 * n + 3 : 3 * n + 6]
+            group = group + jnp.exp(after * rates) * other
+            carry = carry + earlier * jnp.exp(before * rates) * other
+        places = places[3 * len(others) + 3 :]
+        part = step - (len(STAGES) - parts)
         if part >= 0:
             piece = local(part, inner)
             group, carry, *piece = lax.optimization_barrier((group, carry, *piece))

time: 55.7 us -> 53.2 us (0.955)
  starting transfers between devices: 25.2 us -> 22.8 us
    ppermute x6 -> x8, starting transfers between devices: 16.8 us -> 15.5 us  [body(): lax.ppermute(group.astype(bf16), axis, [(i, i ^ flip) for i in range(size)])]
    ppermute x6, starting transfers between devices: 8.45 us -> 7.32 us  [swap(): lax.ppermute(array.astype(jnp.bfloat16), axis, [(0, 1), (1, 0)])]
    ppermute x6 -> x8, waiting for transfers between devices: 2.62 us -> 2.53 us  [body(): lax.ppermute(group.astype(bf16), axis, [(i, i ^ flip) for i in range(size)])]
  transfers between devices with their start and end apart: 12 -> 14, of which waited for: 8 -> 8; matrix products, arithmetic and copies ran while one was open for 0% -> 0% of each run, Pallas kernels for 19% -> 20%
where the time goes in v4:
time: 53.2 us; the launch traced here: 52.9 us
  starting transfers between devices  22.8 us (43%)
  Pallas kernels  15.8 us (30%)
  waiting for transfers between devices  12.6 us (24%)
  other arithmetic  1.53 us (3%)
    ppermute x8, starting transfers between devices, body(): lax.ppermute(group.astype(bf16), axis, [(i, i ^ flip) for i in range(size)])  15.5 us
    ppermute x6, waiting for transfers between devices, swap(): lax.ppermute(array.astype(jnp.bfloat16), axis, [(0, 1), (1, 0)])  10 us
    pallas_call x4, Pallas kernels, local(): pl.pallas_call(functools.partial(fetching_kernel, first_tile=part * (CHUN...  8.83 us
    ppermute x6, starting transfers between devices, swap(): lax.ppermute(array.astype(jnp.bfloat16), axis, [(0, 1), (1, 0)])  7.32 us
    pallas_call x1, Pallas kernels, body(): pl.pallas_call(states_kernel, in_specs=[ANY] * 5, out_specs=[VMEM] * 5, o...  2.95 us
    ppermute x8, waiting for transfers between devices, body(): lax.ppermute(group.astype(bf16), axis, [(i, i ^ flip) for i in range(size)])  2.53 us
    pallas_call x1, Pallas kernels, body(): pl.pallas_call(mix_kernel, in_specs=[VMEM] * len(arrays), out_specs=[VMEM...  2.1 us
    pallas_call x1, Pallas kernels, body(): pl.pallas_call(near_kernel, in_specs=[VMEM] * (1 + 2 * parts), out_specs=...  1.24 us
  transfers between devices with their start and end apart: 14, of which 8 were waited for; matrix products, arithmetic and copies ran while one was open for 0% of the time, Pallas kernels for 20%

profile of v4, /device:TPU:1, one launch (start us, length us, event | category | flops | bytes accessed | tf_op | source)
XLA Modules:
  0.0 52.9 jit_solution(11319129531172850358)
XLA Ops:
  0.0 0.1 pad_add_fusion.place_ref
  0.1 3.0 %states.1 = (f32[16,1024]{1,0:T(8,128)S(1)}, bf16[256,1024]{1,0:T(8,128)(2,1)S(1)}, f32[16,1024]{1,0:T(8,128)S(1)}, f32[16,1024]{1,0:T(8,128)S(1)}, f32[1,1024]{1,0:T(1,128)S(1)}) custom-call(bf16[256,1024]{1,0:T(8,128)(2,1)} %pre_hbm, bf16[256,1024]{1,0:T(8,128)(2,1)} %val_hbm.1, f32[16,1024]{1,0:T(8,128)} %bitcast.5, f32[16,1024]{1,0:T(8,128)} %bitcast.6, ...), custom_call_target="tpu_custom_call" | custom-call | tf_op jit(solution)/shard_map/states/pallas_call | solution.py:257
  3.0 3.7 %collective-permute-start.2 = (bf16[16,1024]{1,0:T(8,128)(2,1)S(1)}, bf16[16,1024]{1,0:T(8,128)(2,1)S(1)}, u32[]{:S(2)}, u32[]{:S(2)}) collective-permute-start(bf16[16,1024]{1,0:T(8,128)(2,1)S(1)} %convert_element_type.166), channel_id=1, source_target_pairs={{0,8},{4,12},{8,0},{12,4},{1,9},{5,13},{9,1},{13,5},{2,10},{6,14},... | collective-permute-start | bytes 98312 | tf_op jit(solution)/shard_map/ppermute | solution.py:296
  6.7 0.9 %collective-permute-start.1 = (bf16[16,1024]{1,0:T(8,128)(2,1)S(1)}, bf16[16,1024]{1,0:T(8,128)(2,1)S(1)}, u32[]{:S(2)}, u32[]{:S(2)}) collective-permute-start(bf16[16,1024]{1,0:T(8,128)(2,1)S(1)} %convert_element_type.166), channel_id=1, source_target_pairs={{0,12},{4,8},{8,4},{12,0},{1,13},{5,9},{9,5},{13,1},{2,14},{6,10},... | collective-permute-start | bytes 98312 | tf_op jit(solution)/shard_map/ppermute | solution.py:296
  7.6 0.0 collective-permute-start
  7.6 2.2 %local.4 = (f32[256,256]{1,0:T(8,128)S(1)}, bf16[1024,256]{1,0:T(8,128)(2,1)S(1)}, bf16[1024,256]{1,0:T(8,128)(2,1)S(1)}, bf16[1024,256]{1,0:T(8,128)(2,1)S(1)},...) custom-call(s32[2]{0:T(128)S(1)} %pad_add_fusion.place_ref, bf16[1024,4096]{1,0:T(8,128)(2,1)} %proj_hbm.7, ...), custom_call_target="tpu_custom_call" | custom-call | flops 100000000 | bytes 1048576 | tf_op jit(solution)/shard_map/local/pallas_call | solution.py:280
  9.8 0.0 collective-permute-done.2
  9.8 1.2 %collective-permute-done.1 = bf16[16,1024]{1,0:T(8,128)(2,1)S(1)} collective-permute-done((bf16[16,1024]{1,0:T(8,128)(2,1)S(1)}, bf16[16,1024]{1,0:T(8,128)(2,1)S(1)}, u32[]{:S(2)}, u32[]{:S(2)}) %collective-permute-start.1) | collective-permute-done | bytes 32800 | tf_op jit(solution)/shard_map/ppermute | solution.py:296
  11.0 0.0 collective-permute-done
  11.0 0.1 fusion.4
  11.1 4.1 %collective-permute-start.5 = (bf16[16,1024]{1,0:T(8,128)(2,1)S(1)}, bf16[16,1024]{1,0:T(8,128)(2,1)S(1)}, u32[]{:S(2)}, u32[]{:S(2)}) collective-permute-start(bf16[16,1024]{1,0:T(8,128)(2,1)S(1)} %convert_element_type.170), channel_id=1, source_target_pairs={{0,48},{16,32},{32,16},{48,0},{64,112},{80,96},{96,80},{112,64},{1... | collective-permute-start | bytes 98312 | tf_op jit(solution)/shard_map/ppermute | solution.py:296
  15.2 0.0 collective-permute-start.4
  15.2 0.4 collective-permute-start.3
  15.6 2.2 %local.5 = (f32[256,256]{1,0:T(8,128)S(1)}, bf16[1024,256]{1,0:T(8,128)(2,1)S(1)}, bf16[1024,256]{1,0:T(8,128)(2,1)S(1)}, bf16[1024,256]{1,0:T(8,128)(2,1)S(1)},...) custom-call(s32[2]{0:T(128)S(1)} %pad_add_fusion.place_ref, bf16[1024,4096]{1,0:T(8,128)(2,1)} %proj_hbm.7, ...), custom_call_target="tpu_custom_call" | custom-call | flops 100000000 | bytes 1048576 | tf_op jit(solution)/shard_map/local/pallas_call | solution.py:280
  17.8 0.0 collective-permute-done.5
  17.8 1.3 %collective-permute-done.4 = bf16[16,1024]{1,0:T(8,128)(2,1)S(1)} collective-permute-done((bf16[16,1024]{1,0:T(8,128)(2,1)S(1)}, bf16[16,1024]{1,0:T(8,128)(2,1)S(1)}, u32[]{:S(2)}, u32[]{:S(2)}) %collective-permute-start.4) | collective-permute-done | bytes 32800 | tf_op jit(solution)/shard_map/ppermute | solution.py:296
  19.2 0.0 collective-permute-done.3
  19.2 0.1 fusion.10
  19.3 3.4 %collective-permute-start.6 = (bf16[16,1024]{1,0:T(8,128)(2,1)S(1)}, bf16[16,1024]{1,0:T(8,128)(2,1)S(1)}, u32[]{:S(2)}, u32[]{:S(2)}) collective-permute-start(bf16[16,1024]{1,0:T(8,128)(2,1)S(1)} %convert_element_type.174), channel_id=1, source_target_pairs={{0,96},{16,112},{32,64},{48,80},{64,32},{80,48},{96,0},{112,16},{1... | collective-permute-start | bytes 98312 | tf_op jit(solution)/shard_map/ppermute | solution.py:296
  22.7 2.2 %local.6 = (f32[256,256]{1,0:T(8,128)S(1)}, bf16[1024,256]{1,0:T(8,128)(2,1)S(1)}, bf16[1024,256]{1,0:T(8,128)(2,1)S(1)}, bf16[1024,256]{1,0:T(8,128)(2,1)S(1)},...) custom-call(s32[2]{0:T(128)S(1)} %pad_add_fusion.place_ref, bf16[1024,4096]{1,0:T(8,128)(2,1)} %proj_hbm.7, ...), custom_call_target="tpu_custom_call" | custom-call | flops 100000000 | bytes 1048576 | tf_op jit(solution)/shard_map/local/pallas_call | solution.py:280
  24.9 0.0 collective-permute-done.6
  25.0 3.0 %collective-permute-start.7 = (bf16[16,1024]{1,0:T(8,128)(2,1)S(1)}, bf16[16,1024]{1,0:T(8,128)(2,1)S(1)}, u32[]{:S(2)}, u32[]{:S(2)}) collective-permute-start(bf16[16,1024]{1,0:T(8,128)(2,1)S(1)} %fusion.11), channel_id=1, source_target_pairs={{0,128},{128,0},{1,129},{129,1},{2,130},{130,2},{3,131},{131,3},{4... | collective-permute-start | bytes 98312 | tf_op jit(solution)/shard_map/ppermute | solution.py:296
  28.0 2.2 %local.7 = (f32[256,256]{1,0:T(8,128)S(1)}, bf16[1024,256]{1,0:T(8,128)(2,1)S(1)}, bf16[1024,256]{1,0:T(8,128)(2,1)S(1)}, bf16[1024,256]{1,0:T(8,128)(2,1)S(1)},...) custom-call(s32[2]{0:T(128)S(1)} %pad_add_fusion.place_ref, bf16[1024,4096]{1,0:T(8,128)(2,1)} %proj_hbm.7, ...), custom_call_target="tpu_custom_call" | custom-call | flops 100000000 | bytes 1048576 | tf_op jit(solution)/shard_map/local/pallas_call | solution.py:280
  30.2 0.0 collective-permute-done.7
  30.3 2.1 %mix.1 = (bf16[256,1024]{1,0:T(8,128)(2,1)S(1)}, bf16[256,1024]{1,0:T(8,128)(2,1)S(1)}) custom-call(f32[16,1024]{1,0:T(8,128)S(1)} %multiply_add_fusion.carry_ref, f32[16,1024]{1,0:T(8,128)S(1)} %get-tuple-element.112.rate_ref, f32[16,1024]{1,0:T(8,128)S(1)} %get-tuple-element.124.weight_ref, f32[256,256]{1,0:T(8,128)S(1)} %get-tuple-element.183.refs_0_, ...), custom_call_target="tpu_custom_call" | custom-call | flops 2000000000 | bytes 4194304 | tf_op jit(solution)/shard_map/mix/pallas_call | solution.py:314
  32.4 4.4 %collective-permute-start.8 = (bf16[256,1024]{1,0:T(8,128)(2,1)S(1)}, bf16[256,1024]{1,0:T(8,128)(2,1)S(1)}, u32[]{:S(2)}, u32[]{:S(2)}) collective-permute-start(bf16[256,1024]{1,0:T(8,128)(2,1)S(1)} %get-tuple-element.196), channel_id=1, source_target_pairs={{0,1},{1,0},{2,3},{3,2},{4,5},{5,4},{6,7},{7,6},{8,9},{9,8},{10,11... | collective-permute-start | bytes 1572872 | tf_op jit(solution)/shard_map/ppermute | solution.py:334
  36.8 0.7 %own.1 = f32[256,1024]{1,0:T(8,128)S(1)} custom-call(bf16[256,1024]{1,0:T(8,128)(2,1)S(1)} %get-tuple-element.201.gated_ref, bf16[1024,256]{1,0:T(8,128)(2,1)S(1)} %get-tuple-element.197.refs_0_, bf16[1024,256]{1,0:T(8,128)(2,1)S(1)} %get-tuple-element.198.refs_1_, bf16[1024,256]{1,0:T(8,128)(2,1)S(1)} %get-tuple-element.199.refs_2_, ...), custom_call_target="tpu_custom_call" | custom-call | flops 2000000000 | bytes 4194304 | tf_op jit(solution)/shard_map/own/pallas_call | solution.py:323
  37.5 0.8 %collective-permute-done.8 = bf16[256,1024]{1,0:T(8,128)(2,1)S(1)} collective-permute-done((bf16[256,1024]{1,0:T(8,128)(2,1)S(1)}, bf16[256,1024]{1,0:T(8,128)(2,1)S(1)}, u32[]{:S(2)}, u32[]{:S(2)}) %collective-permute-start.8) | collective-permute-done | bytes 524320 | tf_op jit(solution)/shard_map/ppermute | solution.py:334
  38.4 0.1 add_convert_fusion.1
  38.5 1.6 %collective-permute-start.13 = (bf16[256,1024]{1,0:T(8,128)(2,1)S(1)}, bf16[256,1024]{1,0:T(8,128)(2,1)S(1)}, u32[]{:S(2)}, u32[]{:S(2)}) collective-permute-start(bf16[256,1024]{1,0:T(8,128)(2,1)S(1)} %add_convert_fusion.1), channel_id=1, source_target_pairs={{0,2},{2,0},{1,3},{3,1},{4,6},{6,4},{5,7},{7,5},{8,10},{10,8},{9,1... | collective-permute-start | bytes 1572872 | tf_op jit(solution)/shard_map/ppermute | solution.py:334
  40.1 1.2 %near.1 = (bf16[256,1024]{1,0:T(8,128)(2,1)S(1)}, f32[256,1024]{1,0:T(8,128)S(1)}) custom-call(bf16[256,1024]{1,0:T(8,128)(2,1)S(1)} %get-tuple-element.201.gated_ref, bf16[1024,256]{1,0:T(8,128)(2,1)S(1)} %get-tuple-element.202.refs_0_, bf16[1024,256]{1,0:T(8,128)(2,1)S(1)} %get-tuple-element.203.refs_1_, bf16[1024,256]{1,0:T(8,128)(2,1)S(1)} %get-tuple-element.204.refs_2_, ...), custom_call_target="tpu_custom_call" | custom-call | flops 2000000000 | bytes 4194304 | tf_op jit(solution)/shard_map/near/pallas_call | solution.py:339
  41.4 0.7 %collective-permute-start.9 = (bf16[64,1024]{1,0:T(8,128)(2,1)S(1)}, bf16[64,1024]{1,0:T(8,128)(2,1)S(1)}, u32[]{:S(2)}, u32[]{:S(2)}) collective-permute-start(bf16[64,1024]{1,0:T(8,128)(2,1)S(1)} %get-tuple-element.213), channel_id=1, source_target_pairs={{0,1},{1,0},{2,3},{3,2},{4,5},{5,4},{6,7},{7,6},{8,9},{9,8},{10,11... | collective-permute-start | bytes 393224 | tf_op jit(solution)/shard_map/ppermute | solution.py:334
  42.1 0.1 collective-permute-start.12
  42.2 0.4 collective-permute-start.11
  42.6 0.1 collective-permute-start.10
  42.7 0.4 collective-permute-done.9
  43.1 0.4 collective-permute-done.12
  43.4 0.2 collective-permute-done.11
  43.6 0.3 collective-permute-done.10
  44.0 8.0 %collective-permute-done.13 = bf16[256,1024]{1,0:T(8,128)(2,1)S(1)} collective-permute-done((bf16[256,1024]{1,0:T(8,128)(2,1)S(1)}, bf16[256,1024]{1,0:T(8,128)(2,1)S(1)}, u32[]{:S(2)}, u32[]{:S(2)}) %collective-permute-start.13) | collective-permute-done | bytes 524320 | tf_op jit(solution)/shard_map/ppermute | solution.py:334
  51.9 1.0 %add_convert_fusion = bf16[256,1024]{1,0:T(8,128)(2,1)} fusion(bf16[256,1024]{1,0:T(8,128)(2,1)S(1)} %collective-permute-done.13, f32[256,1024]{1,0:T(8,128)S(1)} %get-tuple-element.211, bf16[64,1024]{1,0:T(8,128)(2,1)S(1)} %collective-permute-done.12, bf16[64,1024]{1,0:T(8,128)(2,1)S(1)} %collective-permute-done.11, ...), kind=kLoop, calls=%fused_computation | loop fusion | flops 3145728 | bytes 2621440 | tf_op jit(solution)/shard_map/convert_element_type | solution.py:351
  (7 shorter events, 0.1 us)
Async XLA Ops:
  3.0 6.7 %collective-permute-start.2 = (bf16[16,1024]{1,0:T(8,128)(2,1)S(1)}, bf16[16,1024]{1,0:T(8,128)(2,1)S(1)}, u32[]{:S(2)}, u32[]{:S(2)}) collective-permute-start(bf16[16,1024]{1,0:T(8,128)(2,1)S(1)} %convert_element_type.166), channel_id=1, source_target_pairs={{0,8},{4,12},{8,0},{12,4},{1,9},{5,13},{9,1},{13,5},{2,10},{6,14},... | collective-permute-start | bytes 98312 | tf_op jit(solution)/shard_map/ppermute | solution.py:296
  6.7 4.3 %collective-permute-start.1 = (bf16[16,1024]{1,0:T(8,128)(2,1)S(1)}, bf16[16,1024]{1,0:T(8,128)(2,1)S(1)}, u32[]{:S(2)}, u32[]{:S(2)}) collective-permute-start(bf16[16,1024]{1,0:T(8,128)(2,1)S(1)} %convert_element_type.166), channel_id=1, source_target_pairs={{0,12},{4,8},{8,4},{12,0},{1,13},{5,9},{9,5},{13,1},{2,14},{6,10},... | collective-permute-start | bytes 98312 | tf_op jit(solution)/shard_map/ppermute | solution.py:296
  7.6 3.4 %collective-permute-start = (bf16[16,1024]{1,0:T(8,128)(2,1)S(1)}, bf16[16,1024]{1,0:T(8,128)(2,1)S(1)}, u32[]{:S(2)}, u32[]{:S(2)}) collective-permute-start(bf16[16,1024]{1,0:T(8,128)(2,1)S(1)} %convert_element_type.166), channel_id=1, source_target_pairs={{0,4},{4,0},{8,12},{12,8},{1,5},{5,1},{9,13},{13,9},{2,6},{6,2},{1... | collective-permute-start | bytes 98312 | tf_op jit(solution)/shard_map/ppermute | solution.py:296
  11.1 6.7 %collective-permute-start.5 = (bf16[16,1024]{1,0:T(8,128)(2,1)S(1)}, bf16[16,1024]{1,0:T(8,128)(2,1)S(1)}, u32[]{:S(2)}, u32[]{:S(2)}) collective-permute-start(bf16[16,1024]{1,0:T(8,128)(2,1)S(1)} %convert_element_type.170), channel_id=1, source_target_pairs={{0,48},{16,32},{32,16},{48,0},{64,112},{80,96},{96,80},{112,64},{1... | collective-permute-start | bytes 98312 | tf_op jit(solution)/shard_map/ppermute | solution.py:296
  15.2 3.9 %collective-permute-start.4 = (bf16[16,1024]{1,0:T(8,128)(2,1)S(1)}, bf16[16,1024]{1,0:T(8,128)(2,1)S(1)}, u32[]{:S(2)}, u32[]{:S(2)}) collective-permute-start(bf16[16,1024]{1,0:T(8,128)(2,1)S(1)} %convert_element_type.170), channel_id=1, source_target_pairs={{0,32},{16,48},{32,0},{48,16},{64,96},{80,112},{96,64},{112,80},{1... | collective-permute-start | bytes 98312 | tf_op jit(solution)/shard_map/ppermute | solution.py:296
  15.2 3.9 %collective-permute-start.3 = (bf16[16,1024]{1,0:T(8,128)(2,1)S(1)}, bf16[16,1024]{1,0:T(8,128)(2,1)S(1)}, u32[]{:S(2)}, u32[]{:S(2)}) collective-permute-start(bf16[16,1024]{1,0:T(8,128)(2,1)S(1)} %convert_element_type.170), channel_id=1, source_target_pairs={{0,16},{16,0},{32,48},{48,32},{64,80},{80,64},{96,112},{112,96},{1... | collective-permute-start | bytes 98312 | tf_op jit(solution)/shard_map/ppermute | solution.py:296
  19.3 5.7 %collective-permute-start.6 = (bf16[16,1024]{1,0:T(8,128)(2,1)S(1)}, bf16[16,1024]{1,0:T(8,128)(2,1)S(1)}, u32[]{:S(2)}, u32[]{:S(2)}) collective-permute-start(bf16[16,1024]{1,0:T(8,128)(2,1)S(1)} %convert_element_type.174), channel_id=1, source_target_pairs={{0,96},{16,112},{32,64},{48,80},{64,32},{80,48},{96,0},{112,16},{1... | collective-permute-start | bytes 98312 | tf_op jit(solution)/shard_map/ppermute | solution.py:296
  25.0 5.2 %collective-permute-start.7 = (bf16[16,1024]{1,0:T(8,128)(2,1)S(1)}, bf16[16,1024]{1,0:T(8,128)(2,1)S(1)}, u32[]{:S(2)}, u32[]{:S(2)}) collective-permute-start(bf16[16,1024]{1,0:T(8,128)(2,1)S(1)} %fusion.11), channel_id=1, source_target_pairs={{0,128},{128,0},{1,129},{129,1},{2,130},{130,2},{3,131},{131,3},{4... | collective-permute-start | bytes 98312 | tf_op jit(solution)/shard_map/ppermute | solution.py:296
  32.4 6.0 %collective-permute-start.8 = (bf16[256,1024]{1,0:T(8,128)(2,1)S(1)}, bf16[256,1024]{1,0:T(8,128)(2,1)S(1)}, u32[]{:S(2)}, u32[]{:S(2)}) collective-permute-start(bf16[256,1024]{1,0:T(8,128)(2,1)S(1)} %get-tuple-element.196), channel_id=1, source_target_pairs={{0,1},{1,0},{2,3},{3,2},{4,5},{5,4},{6,7},{7,6},{8,9},{9,8},{10,11... | collective-permute-start | bytes 1572872 | tf_op jit(solution)/shard_map/ppermute | solution.py:334
  38.5 13.4 %collective-permute-start.13 = (bf16[256,1024]{1,0:T(8,128)(2,1)S(1)}, bf16[256,1024]{1,0:T(8,128)(2,1)S(1)}, u32[]{:S(2)}, u32[]{:S(2)}) collective-permute-start(bf16[256,1024]{1,0:T(8,128)(2,1)S(1)} %add_convert_fusion.1), channel_id=1, source_target_pairs={{0,2},{2,0},{1,3},{3,1},{4,6},{6,4},{5,7},{7,5},{8,10},{10,8},{9,1... | collective-permute-start | bytes 1572872 | tf_op jit(solution)/shard_map/ppermute | solution.py:334
  41.4 1.7 %collective-permute-start.9 = (bf16[64,1024]{1,0:T(8,128)(2,1)S(1)}, bf16[64,1024]{1,0:T(8,128)(2,1)S(1)}, u32[]{:S(2)}, u32[]{:S(2)}) collective-permute-start(bf16[64,1024]{1,0:T(8,128)(2,1)S(1)} %get-tuple-element.213), channel_id=1, source_target_pairs={{0,1},{1,0},{2,3},{3,2},{4,5},{5,4},{6,7},{7,6},{8,9},{9,8},{10,11... | collective-permute-start | bytes 393224 | tf_op jit(solution)/shard_map/ppermute | solution.py:334
  42.1 1.3 %collective-permute-start.12 = (bf16[64,1024]{1,0:T(8,128)(2,1)S(1)}, bf16[64,1024]{1,0:T(8,128)(2,1)S(1)}, u32[]{:S(2)}, u32[]{:S(2)}) collective-permute-start(bf16[64,1024]{1,0:T(8,128)(2,1)S(1)} %get-tuple-element.214), channel_id=1, source_target_pairs={{0,1},{1,0},{2,3},{3,2},{4,5},{5,4},{6,7},{7,6},{8,9},{9,8},{10,11... | collective-permute-start | bytes 393224 | tf_op jit(solution)/shard_map/ppermute | solution.py:334
  42.2 1.4 %collective-permute-start.11 = (bf16[64,1024]{1,0:T(8,128)(2,1)S(1)}, bf16[64,1024]{1,0:T(8,128)(2,1)S(1)}, u32[]{:S(2)}, u32[]{:S(2)}) collective-permute-start(bf16[64,1024]{1,0:T(8,128)(2,1)S(1)} %get-tuple-element.215), channel_id=1, source_target_pairs={{0,1},{1,0},{2,3},{3,2},{4,5},{5,4},{6,7},{7,6},{8,9},{9,8},{10,11... | collective-permute-start | bytes 393224 | tf_op jit(solution)/shard_map/ppermute | solution.py:334
  42.6 1.3 %collective-permute-start.10 = (bf16[64,1024]{1,0:T(8,128)(2,1)S(1)}, bf16[64,1024]{1,0:T(8,128)(2,1)S(1)}, u32[]{:S(2)}, u32[]{:S(2)}) collective-permute-start(bf16[64,1024]{1,0:T(8,128)(2,1)S(1)} %get-tuple-element.216), channel_id=1, source_target_pairs={{0,1},{1,0},{2,3},{3,2},{4,5},{5,4},{6,7},{7,6},{8,9},{9,8},{10,11... | collective-permute-start | bytes 393224 | tf_op jit(solution)/shard_map/ppermute | solution.py:334

commit v5 on v4

--- a/solution.py
+++ b/solution.py
@@ -20,7 +20,7 @@
 SMEM = pl.BlockSpec(memory_space=pltpu.SMEM)
 STAGES = (
     ("x", X, ((1, 1), (3, 3), (2, 2))),
-    ("z", Z, ((1, 1), (2, 2), (3, 3))),
+    ("z", Z, ((1, 1), (3, 3), (2, 2))),
     ("z", Z, ((6, 1),)),
     ("y_hi", Y_HI, ((1, 1),)),
 )
@@ -53,6 +53,8 @@
 
 
 def tile_of(index):
+    if isinstance(index, int):
+        return pl.ds(index * LANES, LANES)
     return pl.ds(pl.multiple_of(index * LANES, LANES), LANES)
 
 
@@ -191,7 +193,7 @@
 
 
 def mix_kernel(carry_ref, rate_ref, weight_ref, *refs):
-    *refs, gated_ref, sent_ref = refs
+    *refs, gated_ref, sent_ref, sums_buf = refs
     parts = len(refs) // 3
     local_refs, post_refs, proj_refs = refs[:parts], refs[parts : 2 * parts], refs[2 * parts :]
     rows_count = gated_ref.shape[0]
@@ -217,10 +219,27 @@
             gated_ref[rows, cols] = (post_ref[rows, here].astype(jnp.float32) * conv).astype(jnp.bfloat16)
 
     each = local_refs[0].shape[1] // LANES
+    deep = each * LANES
+
+    def add_product(part):
+        cols = slice(part * deep, (part + 1) * deep)
+        gated = gated_ref[:, cols]
+        for n, proj_ref in enumerate(proj_refs):
+            into = slice(n * proj_ref.shape[1], (n + 1) * proj_ref.shape[1])
+            sums = jnp.dot(gated, proj_ref[cols, :], preferred_element_type=jnp.float32)
+            if part:
+                sums = sums + sums_buf[:, into]
+            if part < parts - 1:
+                sums_buf[:, into] = sums
+            else:
+                sent_ref[:, into] = sums.astype(sent_ref.dtype)
+
     for part in range(parts):
-        sources = (local_refs[part], post_refs[part], part * each)
-        pl.loop(0, each)(lambda i, sources=sources: tile(i, *sources))
-    project(gated_ref, proj_refs, sent_ref)
+        if part:
+            add_product(part - 1)
+        for i in range(each):
+            tile(i, local_refs[part], post_refs[part], part * each)
+    add_product(parts - 1)
 
 
 def own_kernel(gated_ref, *refs):
@@ -316,6 +335,7 @@
         in_specs=[VMEM] * len(arrays),
         out_specs=[VMEM] * 2,
         out_shape=[shape_of((rows, width), bf16), shape_of((rows, width), bf16)],
+        scratch_shapes=[pltpu.VMEM((rows, width), jnp.float32)],
         cost_estimate=COST,
         name="mix",
         compiler_params=PARAMS,
@@ -347,7 +367,7 @@
     )(*(in_vmem(a) for a in (gated, *roles[2], *roles[3])))
     quarter = rows // 4
     received = [swap(sent[i : i + quarter], "core") for i in range(0, rows, quarter)]
-    near_sum = jnp.concatenate(received, axis=0) + kept
+    near_sum = lax.optimization_barrier(jnp.concatenate(received, axis=0) + kept)
     return (near_sum + far_sum).astype(bf16)
 
 

time: 53.2 us -> 52.2 us (0.981)
  waiting for transfers between devices: 12.6 us -> 11.8 us
    ppermute x6, starting transfers between devices: 7.32 us -> 6.49 us  [swap(): lax.ppermute(array.astype(jnp.bfloat16), axis, [(0, 1), (1, 0)])]
    ppermute x8, starting transfers between devices: 15.5 us -> 16.3 us  [body(): lax.ppermute(group.astype(bf16), axis, [(i, i ^ flip) for i in range(size)])]
    ppermute x8, waiting for transfers between devices: 2.53 us -> 1.9 us  [body(): lax.ppermute(group.astype(bf16), axis, [(i, i ^ flip) for i in range(size)])]
  transfers between devices with their start and end apart: 14 -> 14, of which waited for: 8 -> 8; matrix products, arithmetic and copies ran while one was open for 0% -> 0% of each run, Pallas kernels for 20% -> 21%
where the time goes in v5:
time: 52.2 us; the launch traced here: 52 us
  starting transfers between devices  22.8 us (44%)
  Pallas kernels  15.6 us (30%)
  waiting for transfers between devices  11.8 us (23%)
  other arithmetic  1.59 us (3%)
    ppermute x8, starting transfers between devices, body(): lax.ppermute(group.astype(bf16), axis, [(i, i ^ flip) for i in range(size)])  16.3 us
    ppermute x6, waiting for transfers between devices, swap(): lax.ppermute(array.astype(jnp.bfloat16), axis, [(0, 1), (1, 0)])  9.89 us
    pallas_call x4, Pallas kernels, local(): pl.pallas_call(functools.partial(fetching_kernel, first_tile=part * (CHUN...  8.83 us
    ppermute x6, starting transfers between devices, swap(): lax.ppermute(array.astype(jnp.bfloat16), axis, [(0, 1), (1, 0)])  6.49 us
    pallas_call x1, Pallas kernels, body(): pl.pallas_call(states_kernel, in_specs=[ANY] * 5, out_specs=[VMEM] * 5, o...  2.95 us
    ppermute x8, waiting for transfers between devices, body(): lax.ppermute(group.astype(bf16), axis, [(i, i ^ flip) for i in range(size)])  1.9 us
    pallas_call x1, Pallas kernels, body(): pl.pallas_call(mix_kernel, in_specs=[VMEM] * len(arrays), out_specs=[VMEM...  1.89 us
    pallas_call x1, Pallas kernels, body(): pl.pallas_call(near_kernel, in_specs=[VMEM] * (1 + 2 * parts), out_specs=...  1.24 us
  transfers between devices with their start and end apart: 14, of which 8 were waited for; matrix products, arithmetic and copies ran while one was open for 0% of the time, Pallas kernels for 21%

profile of v5, /device:TPU:1, one launch (start us, length us, event | category | flops | bytes accessed | tf_op | source)
XLA Modules:
  0.0 52.0 jit_solution(15452451686693411812)
XLA Ops:
  0.0 0.1 pad_add_fusion.place_ref
  0.1 3.0 %states.1 = (f32[16,1024]{1,0:T(8,128)S(1)}, bf16[256,1024]{1,0:T(8,128)(2,1)S(1)}, f32[16,1024]{1,0:T(8,128)S(1)}, f32[16,1024]{1,0:T(8,128)S(1)}, f32[1,1024]{1,0:T(1,128)S(1)}) custom-call(bf16[256,1024]{1,0:T(8,128)(2,1)} %pre_hbm, bf16[256,1024]{1,0:T(8,128)(2,1)} %val_hbm.1, f32[16,1024]{1,0:T(8,128)} %bitcast.5, f32[16,1024]{1,0:T(8,128)} %bitcast.6, ...), custom_call_target="tpu_custom_call" | custom-call | tf_op jit(solution)/shard_map/states/pallas_call | solution.py:276
  3.0 3.7 %collective-permute-start.2 = (bf16[16,1024]{1,0:T(8,128)(2,1)S(1)}, bf16[16,1024]{1,0:T(8,128)(2,1)S(1)}, u32[]{:S(2)}, u32[]{:S(2)}) collective-permute-start(bf16[16,1024]{1,0:T(8,128)(2,1)S(1)} %convert_element_type.166), channel_id=1, source_target_pairs={{0,8},{4,12},{8,0},{12,4},{1,9},{5,13},{9,1},{13,5},{2,10},{6,14},... | collective-permute-start | bytes 98312 | tf_op jit(solution)/shard_map/ppermute | solution.py:315
  6.7 0.9 %collective-permute-start.1 = (bf16[16,1024]{1,0:T(8,128)(2,1)S(1)}, bf16[16,1024]{1,0:T(8,128)(2,1)S(1)}, u32[]{:S(2)}, u32[]{:S(2)}) collective-permute-start(bf16[16,1024]{1,0:T(8,128)(2,1)S(1)} %convert_element_type.166), channel_id=1, source_target_pairs={{0,12},{4,8},{8,4},{12,0},{1,13},{5,9},{9,5},{13,1},{2,14},{6,10},... | collective-permute-start | bytes 98312 | tf_op jit(solution)/shard_map/ppermute | solution.py:315
  7.6 0.0 collective-permute-start
  7.6 2.2 %local.4 = (f32[256,256]{1,0:T(8,128)S(1)}, bf16[1024,256]{1,0:T(8,128)(2,1)S(1)}, bf16[1024,256]{1,0:T(8,128)(2,1)S(1)}, bf16[1024,256]{1,0:T(8,128)(2,1)S(1)},...) custom-call(s32[2]{0:T(128)S(1)} %pad_add_fusion.place_ref, bf16[1024,4096]{1,0:T(8,128)(2,1)} %proj_hbm.7, ...), custom_call_target="tpu_custom_call" | custom-call | flops 100000000 | bytes 1048576 | tf_op jit(solution)/shard_map/local/pallas_call | solution.py:299
  9.8 0.0 collective-permute-done.2
  9.8 1.2 %collective-permute-done.1 = bf16[16,1024]{1,0:T(8,128)(2,1)S(1)} collective-permute-done((bf16[16,1024]{1,0:T(8,128)(2,1)S(1)}, bf16[16,1024]{1,0:T(8,128)(2,1)S(1)}, u32[]{:S(2)}, u32[]{:S(2)}) %collective-permute-start.1) | collective-permute-done | bytes 32800 | tf_op jit(solution)/shard_map/ppermute | solution.py:315
  11.0 0.0 collective-permute-done
  11.0 0.1 fusion.4
  11.1 2.8 %collective-permute-start.5 = (bf16[16,1024]{1,0:T(8,128)(2,1)S(1)}, bf16[16,1024]{1,0:T(8,128)(2,1)S(1)}, u32[]{:S(2)}, u32[]{:S(2)}) collective-permute-start(bf16[16,1024]{1,0:T(8,128)(2,1)S(1)} %convert_element_type.170), channel_id=1, source_target_pairs={{0,32},{16,48},{32,0},{48,16},{64,96},{80,112},{96,64},{112,80},{1... | collective-permute-start | bytes 98312 | tf_op jit(solution)/shard_map/ppermute | solution.py:315
  13.9 1.5 %collective-permute-start.4 = (bf16[16,1024]{1,0:T(8,128)(2,1)S(1)}, bf16[16,1024]{1,0:T(8,128)(2,1)S(1)}, u32[]{:S(2)}, u32[]{:S(2)}) collective-permute-start(bf16[16,1024]{1,0:T(8,128)(2,1)S(1)} %convert_element_type.170), channel_id=1, source_target_pairs={{0,48},{16,32},{32,16},{48,0},{64,112},{80,96},{96,80},{112,64},{1... | collective-permute-start | bytes 98312 | tf_op jit(solution)/shard_map/ppermute | solution.py:315
  15.3 0.2 collective-permute-start.3
  15.5 2.2 %local.5 = (f32[256,256]{1,0:T(8,128)S(1)}, bf16[1024,256]{1,0:T(8,128)(2,1)S(1)}, bf16[1024,256]{1,0:T(8,128)(2,1)S(1)}, bf16[1024,256]{1,0:T(8,128)(2,1)S(1)},...) custom-call(s32[2]{0:T(128)S(1)} %pad_add_fusion.place_ref, bf16[1024,4096]{1,0:T(8,128)(2,1)} %proj_hbm.7, ...), custom_call_target="tpu_custom_call" | custom-call | flops 100000000 | bytes 1048576 | tf_op jit(solution)/shard_map/local/pallas_call | solution.py:299
  17.7 0.0 collective-permute-done.5
  17.7 0.7 %collective-permute-done.4 = bf16[16,1024]{1,0:T(8,128)(2,1)S(1)} collective-permute-done((bf16[16,1024]{1,0:T(8,128)(2,1)S(1)}, bf16[16,1024]{1,0:T(8,128)(2,1)S(1)}, u32[]{:S(2)}, u32[]{:S(2)}) %collective-permute-start.4) | collective-permute-done | bytes 32800 | tf_op jit(solution)/shard_map/ppermute | solution.py:315
  18.4 0.0 collective-permute-done.3
  18.4 0.1 fusion.10
  18.6 4.3 %collective-permute-start.6 = (bf16[16,1024]{1,0:T(8,128)(2,1)S(1)}, bf16[16,1024]{1,0:T(8,128)(2,1)S(1)}, u32[]{:S(2)}, u32[]{:S(2)}) collective-permute-start(bf16[16,1024]{1,0:T(8,128)(2,1)S(1)} %convert_element_type.174), channel_id=1, source_target_pairs={{0,96},{16,112},{32,64},{48,80},{64,32},{80,48},{96,0},{112,16},{1... | collective-permute-start | bytes 98312 | tf_op jit(solution)/shard_map/ppermute | solution.py:315
  22.9 2.2 %local.6 = (f32[256,256]{1,0:T(8,128)S(1)}, bf16[1024,256]{1,0:T(8,128)(2,1)S(1)}, bf16[1024,256]{1,0:T(8,128)(2,1)S(1)}, bf16[1024,256]{1,0:T(8,128)(2,1)S(1)},...) custom-call(s32[2]{0:T(128)S(1)} %pad_add_fusion.place_ref, bf16[1024,4096]{1,0:T(8,128)(2,1)} %proj_hbm.7, ...), custom_call_target="tpu_custom_call" | custom-call | flops 100000000 | bytes 1048576 | tf_op jit(solution)/shard_map/local/pallas_call | solution.py:299
  25.1 0.0 collective-permute-done.6
  25.2 3.0 %collective-permute-start.7 = (bf16[16,1024]{1,0:T(8,128)(2,1)S(1)}, bf16[16,1024]{1,0:T(8,128)(2,1)S(1)}, u32[]{:S(2)}, u32[]{:S(2)}) collective-permute-start(bf16[16,1024]{1,0:T(8,128)(2,1)S(1)} %fusion.11), channel_id=1, source_target_pairs={{0,128},{128,0},{1,129},{129,1},{2,130},{130,2},{3,131},{131,3},{4... | collective-permute-start | bytes 98312 | tf_op jit(solution)/shard_map/ppermute | solution.py:315
  28.2 2.2 %local.7 = (f32[256,256]{1,0:T(8,128)S(1)}, bf16[1024,256]{1,0:T(8,128)(2,1)S(1)}, bf16[1024,256]{1,0:T(8,128)(2,1)S(1)}, bf16[1024,256]{1,0:T(8,128)(2,1)S(1)},...) custom-call(s32[2]{0:T(128)S(1)} %pad_add_fusion.place_ref, bf16[1024,4096]{1,0:T(8,128)(2,1)} %proj_hbm.7, ...), custom_call_target="tpu_custom_call" | custom-call | flops 100000000 | bytes 1048576 | tf_op jit(solution)/shard_map/local/pallas_call | solution.py:299
  30.4 0.0 collective-permute-done.7
  30.5 1.9 %mix.1 = (bf16[256,1024]{1,0:T(8,128)(2,1)S(1)}, bf16[256,1024]{1,0:T(8,128)(2,1)S(1)}) custom-call(f32[16,1024]{1,0:T(8,128)S(1)} %multiply_add_fusion.carry_ref, f32[16,1024]{1,0:T(8,128)S(1)} %get-tuple-element.112.rate_ref, f32[16,1024]{1,0:T(8,128)S(1)} %get-tuple-element.124.weight_ref, f32[256,256]{1,0:T(8,128)S(1)} %get-tuple-element.183.refs_0_, ...), custom_call_target="tpu_custom_call" | custom-call | flops 2000000000 | bytes 4194304 | tf_op jit(solution)/shard_map/mix/pallas_call | solution.py:333
  32.4 3.6 %collective-permute-start.8 = (bf16[256,1024]{1,0:T(8,128)(2,1)S(1)}, bf16[256,1024]{1,0:T(8,128)(2,1)S(1)}, u32[]{:S(2)}, u32[]{:S(2)}) collective-permute-start(bf16[256,1024]{1,0:T(8,128)(2,1)S(1)} %get-tuple-element.196), channel_id=1, source_target_pairs={{0,1},{1,0},{2,3},{3,2},{4,5},{5,4},{6,7},{7,6},{8,9},{9,8},{10,11... | collective-permute-start | bytes 1572872 | tf_op jit(solution)/shard_map/ppermute | solution.py:354
  36.0 0.7 %own.1 = f32[256,1024]{1,0:T(8,128)S(1)} custom-call(bf16[256,1024]{1,0:T(8,128)(2,1)S(1)} %get-tuple-element.201.gated_ref, bf16[1024,256]{1,0:T(8,128)(2,1)S(1)} %get-tuple-element.197.refs_0_, bf16[1024,256]{1,0:T(8,128)(2,1)S(1)} %get-tuple-element.198.refs_1_, bf16[1024,256]{1,0:T(8,128)(2,1)S(1)} %get-tuple-element.199.refs_2_, ...), custom_call_target="tpu_custom_call" | custom-call | flops 2000000000 | bytes 4194304 | tf_op jit(solution)/shard_map/own/pallas_call | solution.py:343
  36.7 0.8 %collective-permute-done.8 = bf16[256,1024]{1,0:T(8,128)(2,1)S(1)} collective-permute-done((bf16[256,1024]{1,0:T(8,128)(2,1)S(1)}, bf16[256,1024]{1,0:T(8,128)(2,1)S(1)}, u32[]{:S(2)}, u32[]{:S(2)}) %collective-permute-start.8) | collective-permute-done | bytes 524320 | tf_op jit(solution)/shard_map/ppermute | solution.py:354
  37.5 0.1 add_convert_fusion.1
  37.6 1.6 %collective-permute-start.13 = (bf16[256,1024]{1,0:T(8,128)(2,1)S(1)}, bf16[256,1024]{1,0:T(8,128)(2,1)S(1)}, u32[]{:S(2)}, u32[]{:S(2)}) collective-permute-start(bf16[256,1024]{1,0:T(8,128)(2,1)S(1)} %add_convert_fusion.1), channel_id=1, source_target_pairs={{0,2},{2,0},{1,3},{3,1},{4,6},{6,4},{5,7},{7,5},{8,10},{10,8},{9,1... | collective-permute-start | bytes 1572872 | tf_op jit(solution)/shard_map/ppermute | solution.py:354
  39.2 1.2 %near.1 = (bf16[256,1024]{1,0:T(8,128)(2,1)S(1)}, f32[256,1024]{1,0:T(8,128)S(1)}) custom-call(bf16[256,1024]{1,0:T(8,128)(2,1)S(1)} %get-tuple-element.201.gated_ref, bf16[1024,256]{1,0:T(8,128)(2,1)S(1)} %get-tuple-element.202.refs_0_, bf16[1024,256]{1,0:T(8,128)(2,1)S(1)} %get-tuple-element.203.refs_1_, bf16[1024,256]{1,0:T(8,128)(2,1)S(1)} %get-tuple-element.204.refs_2_, ...), custom_call_target="tpu_custom_call" | custom-call | flops 2000000000 | bytes 4194304 | tf_op jit(solution)/shard_map/near/pallas_call | solution.py:359
  40.5 0.7 %collective-permute-start.9 = (bf16[64,1024]{1,0:T(8,128)(2,1)S(1)}, bf16[64,1024]{1,0:T(8,128)(2,1)S(1)}, u32[]{:S(2)}, u32[]{:S(2)}) collective-permute-start(bf16[64,1024]{1,0:T(8,128)(2,1)S(1)} %get-tuple-element.213), channel_id=1, source_target_pairs={{0,1},{1,0},{2,3},{3,2},{4,5},{5,4},{6,7},{7,6},{8,9},{9,8},{10,11... | collective-permute-start | bytes 393224 | tf_op jit(solution)/shard_map/ppermute | solution.py:354
  41.2 0.1 collective-permute-start.12
  41.3 0.4 collective-permute-start.11
  41.7 0.1 collective-permute-start.10
  41.8 0.4 collective-permute-done.9
  42.2 0.4 collective-permute-done.12
  42.6 0.2 collective-permute-done.11
  42.8 0.3 collective-permute-done.10
  43.1 0.1 convert_add_fusion
  43.2 7.8 %collective-permute-done.13 = bf16[256,1024]{1,0:T(8,128)(2,1)S(1)} collective-permute-done((bf16[256,1024]{1,0:T(8,128)(2,1)S(1)}, bf16[256,1024]{1,0:T(8,128)(2,1)S(1)}, u32[]{:S(2)}, u32[]{:S(2)}) %collective-permute-start.13) | collective-permute-done | bytes 524320 | tf_op jit(solution)/shard_map/ppermute | solution.py:354
  51.0 1.0 %add_convert_fusion = bf16[256,1024]{1,0:T(8,128)(2,1)} fusion(f32[256,1024]{1,0:T(8,128)S(1)} %convert_add_fusion, bf16[256,1024]{1,0:T(8,128)(2,1)S(1)} %collective-permute-done.13), kind=kLoop, calls=%fused_computation | loop fusion | flops 786432 | bytes 2097152 | tf_op jit(solution)/shard_map/convert_element_type | solution.py:371
  (7 shorter events, 0.1 us)
Async XLA Ops:
  3.0 6.7 %collective-permute-start.2 = (bf16[16,1024]{1,0:T(8,128)(2,1)S(1)}, bf16[16,1024]{1,0:T(8,128)(2,1)S(1)}, u32[]{:S(2)}, u32[]{:S(2)}) collective-permute-start(bf16[16,1024]{1,0:T(8,128)(2,1)S(1)} %convert_element_type.166), channel_id=1, source_target_pairs={{0,8},{4,12},{8,0},{12,4},{1,9},{5,13},{9,1},{13,5},{2,10},{6,14},... | collective-permute-start | bytes 98312 | tf_op jit(solution)/shard_map/ppermute | solution.py:315
  6.7 4.3 %collective-permute-start.1 = (bf16[16,1024]{1,0:T(8,128)(2,1)S(1)}, bf16[16,1024]{1,0:T(8,128)(2,1)S(1)}, u32[]{:S(2)}, u32[]{:S(2)}) collective-permute-start(bf16[16,1024]{1,0:T(8,128)(2,1)S(1)} %convert_element_type.166), channel_id=1, source_target_pairs={{0,12},{4,8},{8,4},{12,0},{1,13},{5,9},{9,5},{13,1},{2,14},{6,10},... | collective-permute-start | bytes 98312 | tf_op jit(solution)/shard_map/ppermute | solution.py:315
  7.6 3.4 %collective-permute-start = (bf16[16,1024]{1,0:T(8,128)(2,1)S(1)}, bf16[16,1024]{1,0:T(8,128)(2,1)S(1)}, u32[]{:S(2)}, u32[]{:S(2)}) collective-permute-start(bf16[16,1024]{1,0:T(8,128)(2,1)S(1)} %convert_element_type.166), channel_id=1, source_target_pairs={{0,4},{4,0},{8,12},{12,8},{1,5},{5,1},{9,13},{13,9},{2,6},{6,2},{1... | collective-permute-start | bytes 98312 | tf_op jit(solution)/shard_map/ppermute | solution.py:315
  11.1 6.6 %collective-permute-start.5 = (bf16[16,1024]{1,0:T(8,128)(2,1)S(1)}, bf16[16,1024]{1,0:T(8,128)(2,1)S(1)}, u32[]{:S(2)}, u32[]{:S(2)}) collective-permute-start(bf16[16,1024]{1,0:T(8,128)(2,1)S(1)} %convert_element_type.170), channel_id=1, source_target_pairs={{0,32},{16,48},{32,0},{48,16},{64,96},{80,112},{96,64},{112,80},{1... | collective-permute-start | bytes 98312 | tf_op jit(solution)/shard_map/ppermute | solution.py:315
  13.9 4.6 %collective-permute-start.4 = (bf16[16,1024]{1,0:T(8,128)(2,1)S(1)}, bf16[16,1024]{1,0:T(8,128)(2,1)S(1)}, u32[]{:S(2)}, u32[]{:S(2)}) collective-permute-start(bf16[16,1024]{1,0:T(8,128)(2,1)S(1)} %convert_element_type.170), channel_id=1, source_target_pairs={{0,48},{16,32},{32,16},{48,0},{64,112},{80,96},{96,80},{112,64},{1... | collective-permute-start | bytes 98312 | tf_op jit(solution)/shard_map/ppermute | solution.py:315
  15.3 3.1 %collective-permute-start.3 = (bf16[16,1024]{1,0:T(8,128)(2,1)S(1)}, bf16[16,1024]{1,0:T(8,128)(2,1)S(1)}, u32[]{:S(2)}, u32[]{:S(2)}) collective-permute-start(bf16[16,1024]{1,0:T(8,128)(2,1)S(1)} %convert_element_type.170), channel_id=1, source_target_pairs={{0,16},{16,0},{32,48},{48,32},{64,80},{80,64},{96,112},{112,96},{1... | collective-permute-start | bytes 98312 | tf_op jit(solution)/shard_map/ppermute | solution.py:315
  18.6 6.6 %collective-permute-start.6 = (bf16[16,1024]{1,0:T(8,128)(2,1)S(1)}, bf16[16,1024]{1,0:T(8,128)(2,1)S(1)}, u32[]{:S(2)}, u32[]{:S(2)}) collective-permute-start(bf16[16,1024]{1,0:T(8,128)(2,1)S(1)} %convert_element_type.174), channel_id=1, source_target_pairs={{0,96},{16,112},{32,64},{48,80},{64,32},{80,48},{96,0},{112,16},{1... | collective-permute-start | bytes 98312 | tf_op jit(solution)/shard_map/ppermute | solution.py:315
  25.2 5.2 %collective-permute-start.7 = (bf16[16,1024]{1,0:T(8,128)(2,1)S(1)}, bf16[16,1024]{1,0:T(8,128)(2,1)S(1)}, u32[]{:S(2)}, u32[]{:S(2)}) collective-permute-start(bf16[16,1024]{1,0:T(8,128)(2,1)S(1)} %fusion.11), channel_id=1, source_target_pairs={{0,128},{128,0},{1,129},{129,1},{2,130},{130,2},{3,131},{131,3},{4... | collective-permute-start | bytes 98312 | tf_op jit(solution)/shard_map/ppermute | solution.py:315
  32.4 5.1 %collective-permute-start.8 = (bf16[256,1024]{1,0:T(8,128)(2,1)S(1)}, bf16[256,1024]{1,0:T(8,128)(2,1)S(1)}, u32[]{:S(2)}, u32[]{:S(2)}) collective-permute-start(bf16[256,1024]{1,0:T(8,128)(2,1)S(1)} %get-tuple-element.196), channel_id=1, source_target_pairs={{0,1},{1,0},{2,3},{3,2},{4,5},{5,4},{6,7},{7,6},{8,9},{9,8},{10,11... | collective-permute-start | bytes 1572872 | tf_op jit(solution)/shard_map/ppermute | solution.py:354
  37.6 13.4 %collective-permute-start.13 = (bf16[256,1024]{1,0:T(8,128)(2,1)S(1)}, bf16[256,1024]{1,0:T(8,128)(2,1)S(1)}, u32[]{:S(2)}, u32[]{:S(2)}) collective-permute-start(bf16[256,1024]{1,0:T(8,128)(2,1)S(1)} %add_convert_fusion.1), channel_id=1, source_target_pairs={{0,2},{2,0},{1,3},{3,1},{4,6},{6,4},{5,7},{7,5},{8,10},{10,8},{9,1... | collective-permute-start | bytes 1572872 | tf_op jit(solution)/shard_map/ppermute | solution.py:354
  40.5 1.7 %collective-permute-start.9 = (bf16[64,1024]{1,0:T(8,128)(2,1)S(1)}, bf16[64,1024]{1,0:T(8,128)(2,1)S(1)}, u32[]{:S(2)}, u32[]{:S(2)}) collective-permute-start(bf16[64,1024]{1,0:T(8,128)(2,1)S(1)} %get-tuple-element.213), channel_id=1, source_target_pairs={{0,1},{1,0},{2,3},{3,2},{4,5},{5,4},{6,7},{7,6},{8,9},{9,8},{10,11... | collective-permute-start | bytes 393224 | tf_op jit(solution)/shard_map/ppermute | solution.py:354
  41.2 1.3 %collective-permute-start.12 = (bf16[64,1024]{1,0:T(8,128)(2,1)S(1)}, bf16[64,1024]{1,0:T(8,128)(2,1)S(1)}, u32[]{:S(2)}, u32[]{:S(2)}) collective-permute-start(bf16[64,1024]{1,0:T(8,128)(2,1)S(1)} %get-tuple-element.214), channel_id=1, source_target_pairs={{0,1},{1,0},{2,3},{3,2},{4,5},{5,4},{6,7},{7,6},{8,9},{9,8},{10,11... | collective-permute-start | bytes 393224 | tf_op jit(solution)/shard_map/ppermute | solution.py:354
  41.3 1.4 %collective-permute-start.11 = (bf16[64,1024]{1,0:T(8,128)(2,1)S(1)}, bf16[64,1024]{1,0:T(8,128)(2,1)S(1)}, u32[]{:S(2)}, u32[]{:S(2)}) collective-permute-start(bf16[64,1024]{1,0:T(8,128)(2,1)S(1)} %get-tuple-element.215), channel_id=1, source_target_pairs={{0,1},{1,0},{2,3},{3,2},{4,5},{5,4},{6,7},{7,6},{8,9},{9,8},{10,11... | collective-permute-start | bytes 393224 | tf_op jit(solution)/shard_map/ppermute | solution.py:354
  41.7 1.3 %collective-permute-start.10 = (bf16[64,1024]{1,0:T(8,128)(2,1)S(1)}, bf16[64,1024]{1,0:T(8,128)(2,1)S(1)}, u32[]{:S(2)}, u32[]{:S(2)}) collective-permute-start(bf16[64,1024]{1,0:T(8,128)(2,1)S(1)} %get-tuple-element.216), channel_id=1, source_target_pairs={{0,1},{1,0},{2,3},{3,2},{4,5},{5,4},{6,7},{7,6},{8,9},{9,8},{10,11... | collective-permute-start | bytes 393224 | tf_op jit(solution)/shard_map/ppermute | solution.py:354

commit v6 on v5

--- a/solution.py
+++ b/solution.py
@@ -84,7 +84,8 @@
 
     def tile(index):
         cols = tile_of(index)
-        factors = [jnp.exp(-float(SUBS) * rows8(rate_ref[m : m + 1, cols])) for m in range(MODES)]
+        decay = jnp.exp(-float(SUBS) * rate_ref[:, cols])
+        factors = [rows8(decay[m : m + 1]) for m in range(MODES)]
         states = None
         for start in range(0, ROWS, 2 * SUBS):
             rows = pl.ds(start, 2 * SUBS)
@@ -127,7 +128,8 @@
             taps = taps + weight_ref[m : m + 1, cols] * jnp.exp(-rate_ref[m : m + 1, cols] * lag)
         for step in range(STEPS):
             taps_buf[pl.ds(step * SUBS, SUBS), :] = rows8(taps[step : step + 1])
-        factors = [jnp.exp(-rows8(rate_ref[m : m + 1, cols])) for m in range(MODES)]
+        decay = jnp.exp(-rate_ref[:, cols])
+        factors = [rows8(decay[m : m + 1]) for m in range(MODES)]
         states = [at(0)] * MODES
         for step in range(1, STEPS):
             value = at(step)
@@ -203,12 +205,13 @@
         here = tile_of(index)
         cols = tile_of(index + offset)
         carry = carry_ref[:, cols] * weight_ref[:, cols]
+        decay = jnp.exp(-float(SUBS) * rate_ref[:, cols])
         terms = []
         factors = []
         for m in range(MODES):
             rate = rows8(rate_ref[m : m + 1, cols])
             terms.append(jnp.exp(-rate * ahead) * rows8(carry[m : m + 1]))
-            factors.append(jnp.exp(-rate * float(SUBS)))
+            factors.append(rows8(decay[m : m + 1]))
         for start in range(0, rows_count, 2 * SUBS):
             sums = []
             for _ in range(2):

time: 52.2 us -> 52.2 us (level)
  no operation moved by 1% of the time
where the time goes in v6:
time: 52.2 us; the launch traced here: 52 us
  starting transfers between devices  22.8 us (44%)
  Pallas kernels  15.6 us (30%)
  waiting for transfers between devices  11.8 us (23%)
  other arithmetic  1.59 us (3%)
    ppermute x8, starting transfers between devices, body(): lax.ppermute(group.astype(bf16), axis, [(i, i ^ flip) for i in range(size)])  16.3 us
    ppermute x6, waiting for transfers between devices, swap(): lax.ppermute(array.astype(jnp.bfloat16), axis, [(0, 1), (1, 0)])  9.89 us
    pallas_call x4, Pallas kernels, local(): pl.pallas_call(functools.partial(fetching_kernel, first_tile=part * (CHUN...  8.83 us
    ppermute x6, starting transfers between devices, swap(): lax.ppermute(array.astype(jnp.bfloat16), axis, [(0, 1), (1, 0)])  6.5 us
    pallas_call x1, Pallas kernels, body(): pl.pallas_call(states_kernel, in_specs=[ANY] * 5, out_specs=[VMEM] * 5, o...  2.98 us
    ppermute x8, waiting for transfers between devices, body(): lax.ppermute(group.astype(bf16), axis, [(i, i ^ flip) for i in range(size)])  1.9 us
    pallas_call x1, Pallas kernels, body(): pl.pallas_call(mix_kernel, in_specs=[VMEM] * len(arrays), out_specs=[VMEM...  1.88 us
    pallas_call x1, Pallas kernels, body(): pl.pallas_call(near_kernel, in_specs=[VMEM] * (1 + 2 * parts), out_specs=...  1.24 us
  transfers between devices with their start and end apart: 14, of which 8 were waited for; matrix products, arithmetic and copies ran while one was open for 0% of the time, Pallas kernels for 21%

profile of v6, /device:TPU:1, one launch (start us, length us, event | category | flops | bytes accessed | tf_op | source)
XLA Modules:
  0.0 52.0 jit_solution(15459906381218832790)
XLA Ops:
  0.0 0.1 pad_add_fusion.place_ref
  0.1 3.0 %states.1 = (f32[16,1024]{1,0:T(8,128)S(1)}, bf16[256,1024]{1,0:T(8,128)(2,1)S(1)}, f32[16,1024]{1,0:T(8,128)S(1)}, f32[16,1024]{1,0:T(8,128)S(1)}, f32[1,1024]{1,0:T(1,128)S(1)}) custom-call(bf16[256,1024]{1,0:T(8,128)(2,1)} %pre_hbm, bf16[256,1024]{1,0:T(8,128)(2,1)} %val_hbm.1, f32[16,1024]{1,0:T(8,128)} %bitcast.5, f32[16,1024]{1,0:T(8,128)} %bitcast.6, ...), custom_call_target="tpu_custom_call" | custom-call | tf_op jit(solution)/shard_map/states/pallas_call | solution.py:279
  3.1 3.7 %collective-permute-start.2 = (bf16[16,1024]{1,0:T(8,128)(2,1)S(1)}, bf16[16,1024]{1,0:T(8,128)(2,1)S(1)}, u32[]{:S(2)}, u32[]{:S(2)}) collective-permute-start(bf16[16,1024]{1,0:T(8,128)(2,1)S(1)} %convert_element_type.166), channel_id=1, source_target_pairs={{0,8},{4,12},{8,0},{12,4},{1,9},{5,13},{9,1},{13,5},{2,10},{6,14},... | collective-permute-start | bytes 98312 | tf_op jit(solution)/shard_map/ppermute | solution.py:318
  6.7 0.9 %collective-permute-start.1 = (bf16[16,1024]{1,0:T(8,128)(2,1)S(1)}, bf16[16,1024]{1,0:T(8,128)(2,1)S(1)}, u32[]{:S(2)}, u32[]{:S(2)}) collective-permute-start(bf16[16,1024]{1,0:T(8,128)(2,1)S(1)} %convert_element_type.166), channel_id=1, source_target_pairs={{0,12},{4,8},{8,4},{12,0},{1,13},{5,9},{9,5},{13,1},{2,14},{6,10},... | collective-permute-start | bytes 98312 | tf_op jit(solution)/shard_map/ppermute | solution.py:318
  7.6 0.0 collective-permute-start
  7.6 2.2 %local.4 = (f32[256,256]{1,0:T(8,128)S(1)}, bf16[1024,256]{1,0:T(8,128)(2,1)S(1)}, bf16[1024,256]{1,0:T(8,128)(2,1)S(1)}, bf16[1024,256]{1,0:T(8,128)(2,1)S(1)},...) custom-call(s32[2]{0:T(128)S(1)} %pad_add_fusion.place_ref, bf16[1024,4096]{1,0:T(8,128)(2,1)} %proj_hbm.7, ...), custom_call_target="tpu_custom_call" | custom-call | flops 100000000 | bytes 1048576 | tf_op jit(solution)/shard_map/local/pallas_call | solution.py:302
  9.8 0.0 collective-permute-done.2
  9.8 1.2 %collective-permute-done.1 = bf16[16,1024]{1,0:T(8,128)(2,1)S(1)} collective-permute-done((bf16[16,1024]{1,0:T(8,128)(2,1)S(1)}, bf16[16,1024]{1,0:T(8,128)(2,1)S(1)}, u32[]{:S(2)}, u32[]{:S(2)}) %collective-permute-start.1) | collective-permute-done | bytes 32800 | tf_op jit(solution)/shard_map/ppermute | solution.py:318
  11.0 0.0 collective-permute-done
  11.0 0.1 fusion.4
  11.1 2.8 %collective-permute-start.5 = (bf16[16,1024]{1,0:T(8,128)(2,1)S(1)}, bf16[16,1024]{1,0:T(8,128)(2,1)S(1)}, u32[]{:S(2)}, u32[]{:S(2)}) collective-permute-start(bf16[16,1024]{1,0:T(8,128)(2,1)S(1)} %convert_element_type.170), channel_id=1, source_target_pairs={{0,32},{16,48},{32,0},{48,16},{64,96},{80,112},{96,64},{112,80},{1... | collective-permute-start | bytes 98312 | tf_op jit(solution)/shard_map/ppermute | solution.py:318
  13.9 1.5 %collective-permute-start.4 = (bf16[16,1024]{1,0:T(8,128)(2,1)S(1)}, bf16[16,1024]{1,0:T(8,128)(2,1)S(1)}, u32[]{:S(2)}, u32[]{:S(2)}) collective-permute-start(bf16[16,1024]{1,0:T(8,128)(2,1)S(1)} %convert_element_type.170), channel_id=1, source_target_pairs={{0,48},{16,32},{32,16},{48,0},{64,112},{80,96},{96,80},{112,64},{1... | collective-permute-start | bytes 98312 | tf_op jit(solution)/shard_map/ppermute | solution.py:318
  15.4 0.2 collective-permute-start.3
  15.5 2.2 %local.5 = (f32[256,256]{1,0:T(8,128)S(1)}, bf16[1024,256]{1,0:T(8,128)(2,1)S(1)}, bf16[1024,256]{1,0:T(8,128)(2,1)S(1)}, bf16[1024,256]{1,0:T(8,128)(2,1)S(1)},...) custom-call(s32[2]{0:T(128)S(1)} %pad_add_fusion.place_ref, bf16[1024,4096]{1,0:T(8,128)(2,1)} %proj_hbm.7, ...), custom_call_target="tpu_custom_call" | custom-call | flops 100000000 | bytes 1048576 | tf_op jit(solution)/shard_map/local/pallas_call | solution.py:302
  17.8 0.0 collective-permute-done.5
  17.8 0.7 %collective-permute-done.4 = bf16[16,1024]{1,0:T(8,128)(2,1)S(1)} collective-permute-done((bf16[16,1024]{1,0:T(8,128)(2,1)S(1)}, bf16[16,1024]{1,0:T(8,128)(2,1)S(1)}, u32[]{:S(2)}, u32[]{:S(2)}) %collective-permute-start.4) | collective-permute-done | bytes 32800 | tf_op jit(solution)/shard_map/ppermute | solution.py:318
  18.5 0.0 collective-permute-done.3
  18.5 0.1 fusion.10
  18.6 4.3 %collective-permute-start.6 = (bf16[16,1024]{1,0:T(8,128)(2,1)S(1)}, bf16[16,1024]{1,0:T(8,128)(2,1)S(1)}, u32[]{:S(2)}, u32[]{:S(2)}) collective-permute-start(bf16[16,1024]{1,0:T(8,128)(2,1)S(1)} %convert_element_type.174), channel_id=1, source_target_pairs={{0,96},{16,112},{32,64},{48,80},{64,32},{80,48},{96,0},{112,16},{1... | collective-permute-start | bytes 98312 | tf_op jit(solution)/shard_map/ppermute | solution.py:318
  22.9 2.2 %local.6 = (f32[256,256]{1,0:T(8,128)S(1)}, bf16[1024,256]{1,0:T(8,128)(2,1)S(1)}, bf16[1024,256]{1,0:T(8,128)(2,1)S(1)}, bf16[1024,256]{1,0:T(8,128)(2,1)S(1)},...) custom-call(s32[2]{0:T(128)S(1)} %pad_add_fusion.place_ref, bf16[1024,4096]{1,0:T(8,128)(2,1)} %proj_hbm.7, ...), custom_call_target="tpu_custom_call" | custom-call | flops 100000000 | bytes 1048576 | tf_op jit(solution)/shard_map/local/pallas_call | solution.py:302
  25.1 0.0 collective-permute-done.6
  25.2 3.0 %collective-permute-start.7 = (bf16[16,1024]{1,0:T(8,128)(2,1)S(1)}, bf16[16,1024]{1,0:T(8,128)(2,1)S(1)}, u32[]{:S(2)}, u32[]{:S(2)}) collective-permute-start(bf16[16,1024]{1,0:T(8,128)(2,1)S(1)} %fusion.11), channel_id=1, source_target_pairs={{0,128},{128,0},{1,129},{129,1},{2,130},{130,2},{3,131},{131,3},{4... | collective-permute-start | bytes 98312 | tf_op jit(solution)/shard_map/ppermute | solution.py:318
  28.2 2.2 %local.7 = (f32[256,256]{1,0:T(8,128)S(1)}, bf16[1024,256]{1,0:T(8,128)(2,1)S(1)}, bf16[1024,256]{1,0:T(8,128)(2,1)S(1)}, bf16[1024,256]{1,0:T(8,128)(2,1)S(1)},...) custom-call(s32[2]{0:T(128)S(1)} %pad_add_fusion.place_ref, bf16[1024,4096]{1,0:T(8,128)(2,1)} %proj_hbm.7, ...), custom_call_target="tpu_custom_call" | custom-call | flops 100000000 | bytes 1048576 | tf_op jit(solution)/shard_map/local/pallas_call | solution.py:302
  30.4 0.0 collective-permute-done.7
  30.5 1.9 %mix.1 = (bf16[256,1024]{1,0:T(8,128)(2,1)S(1)}, bf16[256,1024]{1,0:T(8,128)(2,1)S(1)}) custom-call(f32[16,1024]{1,0:T(8,128)S(1)} %multiply_add_fusion.carry_ref, f32[16,1024]{1,0:T(8,128)S(1)} %get-tuple-element.112.rate_ref, f32[16,1024]{1,0:T(8,128)S(1)} %get-tuple-element.124.weight_ref, f32[256,256]{1,0:T(8,128)S(1)} %get-tuple-element.183.refs_0_, ...), custom_call_target="tpu_custom_call" | custom-call | flops 2000000000 | bytes 4194304 | tf_op jit(solution)/shard_map/mix/pallas_call | solution.py:336
  32.4 3.6 %collective-permute-start.8 = (bf16[256,1024]{1,0:T(8,128)(2,1)S(1)}, bf16[256,1024]{1,0:T(8,128)(2,1)S(1)}, u32[]{:S(2)}, u32[]{:S(2)}) collective-permute-start(bf16[256,1024]{1,0:T(8,128)(2,1)S(1)} %get-tuple-element.196), channel_id=1, source_target_pairs={{0,1},{1,0},{2,3},{3,2},{4,5},{5,4},{6,7},{7,6},{8,9},{9,8},{10,11... | collective-permute-start | bytes 1572872 | tf_op jit(solution)/shard_map/ppermute | solution.py:357
  36.0 0.7 %own.1 = f32[256,1024]{1,0:T(8,128)S(1)} custom-call(bf16[256,1024]{1,0:T(8,128)(2,1)S(1)} %get-tuple-element.201.gated_ref, bf16[1024,256]{1,0:T(8,128)(2,1)S(1)} %get-tuple-element.197.refs_0_, bf16[1024,256]{1,0:T(8,128)(2,1)S(1)} %get-tuple-element.198.refs_1_, bf16[1024,256]{1,0:T(8,128)(2,1)S(1)} %get-tuple-element.199.refs_2_, ...), custom_call_target="tpu_custom_call" | custom-call | flops 2000000000 | bytes 4194304 | tf_op jit(solution)/shard_map/own/pallas_call | solution.py:346
  36.7 0.8 %collective-permute-done.8 = bf16[256,1024]{1,0:T(8,128)(2,1)S(1)} collective-permute-done((bf16[256,1024]{1,0:T(8,128)(2,1)S(1)}, bf16[256,1024]{1,0:T(8,128)(2,1)S(1)}, u32[]{:S(2)}, u32[]{:S(2)}) %collective-permute-start.8) | collective-permute-done | bytes 524320 | tf_op jit(solution)/shard_map/ppermute | solution.py:357
  37.5 0.1 add_convert_fusion.1
  37.7 1.5 %collective-permute-start.13 = (bf16[256,1024]{1,0:T(8,128)(2,1)S(1)}, bf16[256,1024]{1,0:T(8,128)(2,1)S(1)}, u32[]{:S(2)}, u32[]{:S(2)}) collective-permute-start(bf16[256,1024]{1,0:T(8,128)(2,1)S(1)} %add_convert_fusion.1), channel_id=1, source_target_pairs={{0,2},{2,0},{1,3},{3,1},{4,6},{6,4},{5,7},{7,5},{8,10},{10,8},{9,1... | collective-permute-start | bytes 1572872 | tf_op jit(solution)/shard_map/ppermute | solution.py:357
  39.2 1.2 %near.1 = (bf16[256,1024]{1,0:T(8,128)(2,1)S(1)}, f32[256,1024]{1,0:T(8,128)S(1)}) custom-call(bf16[256,1024]{1,0:T(8,128)(2,1)S(1)} %get-tuple-element.201.gated_ref, bf16[1024,256]{1,0:T(8,128)(2,1)S(1)} %get-tuple-element.202.refs_0_, bf16[1024,256]{1,0:T(8,128)(2,1)S(1)} %get-tuple-element.203.refs_1_, bf16[1024,256]{1,0:T(8,128)(2,1)S(1)} %get-tuple-element.204.refs_2_, ...), custom_call_target="tpu_custom_call" | custom-call | flops 2000000000 | bytes 4194304 | tf_op jit(solution)/shard_map/near/pallas_call | solution.py:362
  40.5 0.7 %collective-permute-start.9 = (bf16[64,1024]{1,0:T(8,128)(2,1)S(1)}, bf16[64,1024]{1,0:T(8,128)(2,1)S(1)}, u32[]{:S(2)}, u32[]{:S(2)}) collective-permute-start(bf16[64,1024]{1,0:T(8,128)(2,1)S(1)} %get-tuple-element.213), channel_id=1, source_target_pairs={{0,1},{1,0},{2,3},{3,2},{4,5},{5,4},{6,7},{7,6},{8,9},{9,8},{10,11... | collective-permute-start | bytes 393224 | tf_op jit(solution)/shard_map/ppermute | solution.py:357
  41.2 0.1 collective-permute-start.12
  41.3 0.4 collective-permute-start.11
  41.8 0.1 collective-permute-start.10
  41.9 0.4 collective-permute-done.9
  42.2 0.4 collective-permute-done.12
  42.6 0.2 collective-permute-done.11
  42.8 0.3 collective-permute-done.10
  43.1 0.1 convert_add_fusion
  43.3 7.8 %collective-permute-done.13 = bf16[256,1024]{1,0:T(8,128)(2,1)S(1)} collective-permute-done((bf16[256,1024]{1,0:T(8,128)(2,1)S(1)}, bf16[256,1024]{1,0:T(8,128)(2,1)S(1)}, u32[]{:S(2)}, u32[]{:S(2)}) %collective-permute-start.13) | collective-permute-done | bytes 524320 | tf_op jit(solution)/shard_map/ppermute | solution.py:357
  51.1 1.0 %add_convert_fusion = bf16[256,1024]{1,0:T(8,128)(2,1)} fusion(f32[256,1024]{1,0:T(8,128)S(1)} %convert_add_fusion, bf16[256,1024]{1,0:T(8,128)(2,1)S(1)} %collective-permute-done.13), kind=kLoop, calls=%fused_computation | loop fusion | flops 786432 | bytes 2097152 | tf_op jit(solution)/shard_map/convert_element_type | solution.py:374
  (7 shorter events, 0.1 us)
Async XLA Ops:
  3.1 6.7 %collective-permute-start.2 = (bf16[16,1024]{1,0:T(8,128)(2,1)S(1)}, bf16[16,1024]{1,0:T(8,128)(2,1)S(1)}, u32[]{:S(2)}, u32[]{:S(2)}) collective-permute-start(bf16[16,1024]{1,0:T(8,128)(2,1)S(1)} %convert_element_type.166), channel_id=1, source_target_pairs={{0,8},{4,12},{8,0},{12,4},{1,9},{5,13},{9,1},{13,5},{2,10},{6,14},... | collective-permute-start | bytes 98312 | tf_op jit(solution)/shard_map/ppermute | solution.py:318
  6.7 4.3 %collective-permute-start.1 = (bf16[16,1024]{1,0:T(8,128)(2,1)S(1)}, bf16[16,1024]{1,0:T(8,128)(2,1)S(1)}, u32[]{:S(2)}, u32[]{:S(2)}) collective-permute-start(bf16[16,1024]{1,0:T(8,128)(2,1)S(1)} %convert_element_type.166), channel_id=1, source_target_pairs={{0,12},{4,8},{8,4},{12,0},{1,13},{5,9},{9,5},{13,1},{2,14},{6,10},... | collective-permute-start | bytes 98312 | tf_op jit(solution)/shard_map/ppermute | solution.py:318
  7.6 3.4 %collective-permute-start = (bf16[16,1024]{1,0:T(8,128)(2,1)S(1)}, bf16[16,1024]{1,0:T(8,128)(2,1)S(1)}, u32[]{:S(2)}, u32[]{:S(2)}) collective-permute-start(bf16[16,1024]{1,0:T(8,128)(2,1)S(1)} %convert_element_type.166), channel_id=1, source_target_pairs={{0,4},{4,0},{8,12},{12,8},{1,5},{5,1},{9,13},{13,9},{2,6},{6,2},{1... | collective-permute-start | bytes 98312 | tf_op jit(solution)/shard_map/ppermute | solution.py:318
  11.1 6.6 %collective-permute-start.5 = (bf16[16,1024]{1,0:T(8,128)(2,1)S(1)}, bf16[16,1024]{1,0:T(8,128)(2,1)S(1)}, u32[]{:S(2)}, u32[]{:S(2)}) collective-permute-start(bf16[16,1024]{1,0:T(8,128)(2,1)S(1)} %convert_element_type.170), channel_id=1, source_target_pairs={{0,32},{16,48},{32,0},{48,16},{64,96},{80,112},{96,64},{112,80},{1... | collective-permute-start | bytes 98312 | tf_op jit(solution)/shard_map/ppermute | solution.py:318
  13.9 4.6 %collective-permute-start.4 = (bf16[16,1024]{1,0:T(8,128)(2,1)S(1)}, bf16[16,1024]{1,0:T(8,128)(2,1)S(1)}, u32[]{:S(2)}, u32[]{:S(2)}) collective-permute-start(bf16[16,1024]{1,0:T(8,128)(2,1)S(1)} %convert_element_type.170), channel_id=1, source_target_pairs={{0,48},{16,32},{32,16},{48,0},{64,112},{80,96},{96,80},{112,64},{1... | collective-permute-start | bytes 98312 | tf_op jit(solution)/shard_map/ppermute | solution.py:318
  15.4 3.1 %collective-permute-start.3 = (bf16[16,1024]{1,0:T(8,128)(2,1)S(1)}, bf16[16,1024]{1,0:T(8,128)(2,1)S(1)}, u32[]{:S(2)}, u32[]{:S(2)}) collective-permute-start(bf16[16,1024]{1,0:T(8,128)(2,1)S(1)} %convert_element_type.170), channel_id=1, source_target_pairs={{0,16},{16,0},{32,48},{48,32},{64,80},{80,64},{96,112},{112,96},{1... | collective-permute-start | bytes 98312 | tf_op jit(solution)/shard_map/ppermute | solution.py:318
  18.6 6.6 %collective-permute-start.6 = (bf16[16,1024]{1,0:T(8,128)(2,1)S(1)}, bf16[16,1024]{1,0:T(8,128)(2,1)S(1)}, u32[]{:S(2)}, u32[]{:S(2)}) collective-permute-start(bf16[16,1024]{1,0:T(8,128)(2,1)S(1)} %convert_element_type.174), channel_id=1, source_target_pairs={{0,96},{16,112},{32,64},{48,80},{64,32},{80,48},{96,0},{112,16},{1... | collective-permute-start | bytes 98312 | tf_op jit(solution)/shard_map/ppermute | solution.py:318
  25.2 5.2 %collective-permute-start.7 = (bf16[16,1024]{1,0:T(8,128)(2,1)S(1)}, bf16[16,1024]{1,0:T(8,128)(2,1)S(1)}, u32[]{:S(2)}, u32[]{:S(2)}) collective-permute-start(bf16[16,1024]{1,0:T(8,128)(2,1)S(1)} %fusion.11), channel_id=1, source_target_pairs={{0,128},{128,0},{1,129},{129,1},{2,130},{130,2},{3,131},{131,3},{4... | collective-permute-start | bytes 98312 | tf_op jit(solution)/shard_map/ppermute | solution.py:318
  32.4 5.1 %collective-permute-start.8 = (bf16[256,1024]{1,0:T(8,128)(2,1)S(1)}, bf16[256,1024]{1,0:T(8,128)(2,1)S(1)}, u32[]{:S(2)}, u32[]{:S(2)}) collective-permute-start(bf16[256,1024]{1,0:T(8,128)(2,1)S(1)} %get-tuple-element.196), channel_id=1, source_target_pairs={{0,1},{1,0},{2,3},{3,2},{4,5},{5,4},{6,7},{7,6},{8,9},{9,8},{10,11... | collective-permute-start | bytes 1572872 | tf_op jit(solution)/shard_map/ppermute | solution.py:357
  37.7 13.4 %collective-permute-start.13 = (bf16[256,1024]{1,0:T(8,128)(2,1)S(1)}, bf16[256,1024]{1,0:T(8,128)(2,1)S(1)}, u32[]{:S(2)}, u32[]{:S(2)}) collective-permute-start(bf16[256,1024]{1,0:T(8,128)(2,1)S(1)} %add_convert_fusion.1), channel_id=1, source_target_pairs={{0,2},{2,0},{1,3},{3,1},{4,6},{6,4},{5,7},{7,5},{8,10},{10,8},{9,1... | collective-permute-start | bytes 1572872 | tf_op jit(solution)/shard_map/ppermute | solution.py:357
  40.5 1.7 %collective-permute-start.9 = (bf16[64,1024]{1,0:T(8,128)(2,1)S(1)}, bf16[64,1024]{1,0:T(8,128)(2,1)S(1)}, u32[]{:S(2)}, u32[]{:S(2)}) collective-permute-start(bf16[64,1024]{1,0:T(8,128)(2,1)S(1)} %get-tuple-element.213), channel_id=1, source_target_pairs={{0,1},{1,0},{2,3},{3,2},{4,5},{5,4},{6,7},{7,6},{8,9},{9,8},{10,11... | collective-permute-start | bytes 393224 | tf_op jit(solution)/shard_map/ppermute | solution.py:357
  41.2 1.3 %collective-permute-start.12 = (bf16[64,1024]{1,0:T(8,128)(2,1)S(1)}, bf16[64,1024]{1,0:T(8,128)(2,1)S(1)}, u32[]{:S(2)}, u32[]{:S(2)}) collective-permute-start(bf16[64,1024]{1,0:T(8,128)(2,1)S(1)} %get-tuple-element.214), channel_id=1, source_target_pairs={{0,1},{1,0},{2,3},{3,2},{4,5},{5,4},{6,7},{7,6},{8,9},{9,8},{10,11... | collective-permute-start | bytes 393224 | tf_op jit(solution)/shard_map/ppermute | solution.py:357
  41.3 1.4 %collective-permute-start.11 = (bf16[64,1024]{1,0:T(8,128)(2,1)S(1)}, bf16[64,1024]{1,0:T(8,128)(2,1)S(1)}, u32[]{:S(2)}, u32[]{:S(2)}) collective-permute-start(bf16[64,1024]{1,0:T(8,128)(2,1)S(1)} %get-tuple-element.215), channel_id=1, source_target_pairs={{0,1},{1,0},{2,3},{3,2},{4,5},{5,4},{6,7},{7,6},{8,9},{9,8},{10,11... | collective-permute-start | bytes 393224 | tf_op jit(solution)/shard_map/ppermute | solution.py:357
  41.8 1.3 %collective-permute-start.10 = (bf16[64,1024]{1,0:T(8,128)(2,1)S(1)}, bf16[64,1024]{1,0:T(8,128)(2,1)S(1)}, u32[]{:S(2)}, u32[]{:S(2)}) collective-permute-start(bf16[64,1024]{1,0:T(8,128)(2,1)S(1)} %get-tuple-element.216), channel_id=1, source_target_pairs={{0,1},{1,0},{2,3},{3,2},{4,5},{5,4},{6,7},{7,6},{8,9},{9,8},{10,11... | collective-permute-start | bytes 393224 | tf_op jit(solution)/shard_map/ppermute | solution.py:357
